TPU v7x, 32 devices: a whole 2x2x4 slice. The times are simulated.
32 devices in a mesh: branch: 4 (over y, x), rows: 2 (over core), batch: 4 (over z).
Axes of the slice: x: 2, y: 2, z: 4, core: 2. Of those that a mesh axis runs over, the one named last changes fastest.
Arguments:
- trunk_input: bfloat16 [4, 24, 128, 2048], P('batch', 'rows', None, 'branch'), may hold values from -6.4 to 6.4, as said below
- conv_reduce: bfloat16 [2048, 512], P(None, 'branch'), may hold values from -0.125 to 0.125
- conv_dilated: bfloat16 [3, 3, 512, 512], P(None, None, None, 'branch'), may hold values from -0.09375 to 0.09375
- conv_expand: bfloat16 [512, 2048], P(None, 'branch'), may hold values from -0.25 to 0.25
- reduction_norm_params: float32 [2, 512], P(None, 'branch'), may hold values from -1.6 to 1.6, as said below
- dilated_norm_params: float32 [2, 512], P(None, 'branch'), may hold values from -1.6 to 1.6, as said below
- expansion_norm_params: float32 [2, 2048], P(None, 'branch'), may hold values from -1.6 to 1.6, as said below
- aspp_point: bfloat16 [256, 2048], P('branch'), may hold values from -0.125 to 0.125
- aspp_rates: bfloat16 [3, 3, 3, 256, 2048], P(None, None, None, 'branch'), may hold values from -0.046875 to 0.046875
- aspp_pool: bfloat16 [256, 2048], P('branch'), may hold values from -0.125 to 0.125
- branch_norms: float32 [2, 4, 256], P(None, None, 'branch'), may hold values from -1.6 to 1.6, as said below
- pooling_norm_params: float32 [2, 256], P(None, 'branch'), may hold values from -1.6 to 1.6, as said below
- aspp_project: bfloat16 [256, 5, 256], P('branch'), may hold values from -0.15625 to 0.15625
- projection_norm_params: float32 [2, 256], P(None, 'branch'), may hold values from -1.6 to 1.6, as said below
- head_weight: bfloat16 [256, 22], replicated, may hold values from -0.375 to 0.375
- head_bias: float32 [22], replicated, may hold values from -1.5 to 1.5
- log_vars: float32 [3], replicated, may hold values from -0.7 to 0.7
- crop_boxes: int32 [4, 4], replicated, may hold values from 0 to 128, as said below
- seg_labels: int32 [4, 24, 128], P('batch', 'rows'), may hold values from 0 to 18
- depth_target: float32 [4, 24, 128], P('batch', 'rows'), may hold values from -4 to 4
- normal_target: float32 [4, 2, 24, 128], P('batch', None, 'rows'), may hold values from -3 to 3
Outputs:
- aspp_features: bfloat16 [4, 24, 128, 256], P('batch', 'rows', None, 'branch')
- total_loss: float32 [], replicated
- grad_input: float32 [4, 24, 128, 2048], P('batch', 'rows', None, 'branch')
- grad_reduce: float32 [2048, 512], P(('rows', 'batch'), 'branch')
- grad_dilated: float32 [3, 3, 512, 512], P(None, None, ('rows', 'batch'), 'branch')
- grad_expand: float32 [512, 2048], P(('rows', 'batch'), 'branch')
- grad_norm_reduce: float32 [2, 512], P(None, 'branch')
- gradient_dilated_norm: float32 [2, 512], P(None, 'branch')
- grad_norm_expand: float32 [2, 2048], P(None, 'branch')
- grad_point: float32 [256, 2048], P('branch', ('rows', 'batch'))
- grad_rates: float32 [3, 3, 3, 256, 2048], P(None, None, None, 'branch', ('rows', 'batch'))
- grad_pool: float32 [256, 2048], P('branch', ('rows', 'batch'))
- grad_branch_norms: float32 [2, 4, 256], P(None, None, 'branch')
- grad_pool_norm: float32 [2, 256], P(None, 'branch')
- grad_project: float32 [256, 5, 256], P('branch', None, ('rows', 'batch'))
- grad_project_norm: float32 [2, 256], P(None, 'branch')
- grad_head_weight: float32 [256, 22], replicated
- grad_head_bias: float32 [22], replicated
- grad_log_vars: float32 [3], replicated
Inputs may be any that keep to these rules, and one draw needn't show every extreme that they name: `trunk_input`: the values of one image and channel scatter around a mean of their own. `reduction_norm_params`: row 0 holds gains, row 1 biases. `dilated_norm_params`: row 0 holds gains, row 1 biases. `expansion_norm_params`: row 0 holds gains, row 1 biases. `branch_norms`: row 0 holds gains, row 1 biases. `pooling_norm_params`: row 0 holds gains, row 1 biases. `projection_norm_params`: row 0 holds gains, row 1 biases. `crop_boxes`: each region lies inside the canvas and is either 24 rows by 96 columns or 16 rows by 128 columns; both kinds occur in every draw.
All inputs are finite; a program needn't handle non-finite values.
Results may differ from a plain program's by a relative error of at most 0.025.
The roundings to bfloat16 on the way count: a program that leaves them out, or rounds other values in their place, can miss the bound.
Values may be sent and summed in bfloat16 or wider, within the bound.
A program may use at most 384 MiB of HBM per device.

v0:
```python
import jax
import jax.numpy as jnp
from jax import lax
from jax.sharding import PartitionSpec as P

EPS = 1e-05
HIGH = lax.Precision.HIGHEST
RATES = (12, 24, 36)


def padded(cells, sides, width):
    for axis, dim in sides:
        count = lax.axis_size(axis)
        ends = count - 1
        head = lax.slice_in_dim(cells, 0, width, axis=dim)
        tail = lax.slice_in_dim(cells, cells.shape[dim] - width, cells.shape[dim], axis=dim)
        cells = jnp.concatenate(
            [
                lax.ppermute(tail, axis, [(i, (i + 1) % count) for i in range(ends)]),
                cells,
                lax.ppermute(head, axis, [((i + 1) % count, i) for i in range(ends)]),
            ],
            axis=dim,
        )
    return cells


def shifted_2(block, axis, distance):
    devices = range(lax.axis_size(axis))
    route = [(i - distance, i) for i in devices if i - distance in devices]
    return lax.ppermute(block, axis, route)


def move(tensor, offset, axis_id):
    length = tensor.shape[axis_id]
    if offset == 0:
        return tensor
    widths = [(0, 0)] * tensor.ndim
    if offset > 0:
        widths[axis_id] = (offset, 0)
        return lax.slice_in_dim(jnp.pad(tensor, widths), 0, length, axis=axis_id)
    widths[axis_id] = (0, -offset)
    return lax.slice_in_dim(jnp.pad(tensor, widths), -offset, length - offset, axis=axis_id)


def forward_dot(lhs_arr, rhs_arr):
    return jnp.dot(lhs_arr, rhs_arr, preferred_element_type=jnp.float32)


def backward_dot(grad_arr, kernel):
    return lax.dot_general(
        grad_arr,
        kernel,
        (((grad_arr.ndim - 1,), (1,)), ((), ())),
        preferred_element_type=jnp.float32,
    )


def pixel_dot(source, grad_arr):
    return lax.dot_general(
        source, grad_arr, (((0, 1, 2), (0, 1, 2)), ((), ())), preferred_element_type=jnp.float32
    )


def silu_slope(pre_act):
    sigmoid_v = jax.nn.sigmoid(pre_act)
    return sigmoid_v * (1.0 + pre_act * (1.0 - sigmoid_v))


def widen(tensor):
    return lax.all_gather(tensor, "branch", axis=3, tiled=True)


def narrow(tensor):
    return lax.psum_scatter(
        tensor.astype(jnp.bfloat16), "branch", scatter_dimension=3, tiled=True
    ).astype(jnp.float32)


def pad_rows(tensor):
    return padded(tensor, (("rows", 1),), 4)


def send_down(tensor, hops):
    if hops >= lax.axis_size("rows"):
        return jnp.zeros_like(tensor)
    return shifted_2(tensor, "rows", hops)


def send_up(tensor, hops):
    if hops >= lax.axis_size("rows"):
        return jnp.zeros_like(tensor)
    return shifted_2(tensor, "rows", -hops)


def over_rows(tensor):
    return lax.psum(tensor, "rows")


def norm_ahead_pass(tensor, weight, counted, affine):
    summed = lax.psum(jnp.sum(tensor * weight, axis=0), ("rows", "batch"))
    mean_val = summed / counted
    centered = tensor - mean_val
    spread = lax.psum(jnp.sum(weight * centered * centered, axis=0), ("rows", "batch"))
    variance = spread / counted
    inverse = lax.rsqrt(variance + EPS)
    normed = centered * inverse
    return (affine[0] * normed + affine[1], normed, inverse)


def norm_reverse_pass(grad_out, normed, inverse, weight_all, weight_stat, counted, affine):
    grad_bias, grad_gain = lax.psum(
        (jnp.sum(grad_out * weight_all, axis=0), jnp.sum(grad_out * normed * weight_all, axis=0)),
        ("rows", "batch"),
    )
    gain_row = affine[0]
    grad_in = inverse * (
        gain_row * grad_out - weight_stat / counted * gain_row * (grad_bias + normed * grad_gain)
    )
    return (grad_in, jnp.stack([grad_gain, grad_bias]))


def stacked_taps(kernels, col_tap):
    return jnp.concatenate([kernels[0, col_tap], kernels[1, col_tap], kernels[2, col_tap]], axis=0)


def local(
    trunk_input,
    conv_reduce,
    conv_dilated,
    conv_expand,
    reduction_norm_params,
    dilated_norm_params,
    expansion_norm_params,
    aspp_point,
    aspp_rates,
    aspp_pool,
    branch_norms,
    pooling_norm_params,
    aspp_project,
    projection_norm_params,
    head_weight,
    head_bias,
    log_vars,
    crop_boxes,
    seg_labels,
    depth_target,
    normal_target,
):
    image_inputs, tile_row_count, frame_columns, quarter = trunk_input.shape
    pixels = image_inputs * tile_row_count * frame_columns
    branch_part = aspp_point.shape[0]
    branch_total = lax.axis_size("branch")
    row_portion = 1.0 / lax.axis_size("rows")
    image_overall_count = float(crop_boxes.shape[0])
    first_image = lax.axis_index("batch") * image_inputs
    first_row = lax.axis_index("rows") * tile_row_count
    my_boxes = lax.dynamic_slice_in_dim(crop_boxes, first_image, image_inputs, 0)
    row_ids = first_row + jnp.arange(tile_row_count, dtype=jnp.int32)
    col_ids = jnp.arange(frame_columns, dtype=jnp.int32)
    inside_rows = (row_ids[None, :] >= my_boxes[:, 0:1]) & (
        row_ids[None, :] < my_boxes[:, 0:1] + my_boxes[:, 2:3]
    )
    inside_cols = (col_ids[None, :] >= my_boxes[:, 1:2]) & (
        col_ids[None, :] < my_boxes[:, 1:2] + my_boxes[:, 3:4]
    )
    valid_mask = (inside_rows[:, :, None] & inside_cols[:, None, :]).astype(jnp.float32)
    mask_column_vector = valid_mask.reshape(pixels, 1)
    mask_flat = valid_mask.reshape(pixels)
    pixel_number_count = jnp.sum((crop_boxes[:, 2] * crop_boxes[:, 3]).astype(jnp.float32))
    image_areas = (my_boxes[:, 2] * my_boxes[:, 3]).astype(jnp.float32)
    input_full = widen(trunk_input)
    reduced_output = forward_dot(input_full, conv_reduce).reshape(pixels, -1)
    normalized_first, standardized_first, inverse_deviation_first = norm_ahead_pass(
        reduced_output, mask_column_vector, pixel_number_count, reduction_norm_params
    )
    hidden_one = (
        jax.nn.silu(normalized_first)
        .astype(jnp.bfloat16)
        .reshape(image_inputs, tile_row_count, frame_columns, -1)
    )
    hidden_full = widen(pad_rows(hidden_one))
    dilated_out = 0.0
    for row_tap in range(3):
        band = hidden_full[:, 4 * row_tap : 4 * row_tap + tile_row_count]
        for col_tap in range(3):
            dilated_out = dilated_out + forward_dot(
                move(band, -(col_tap - 1) * 4, 2), conv_dilated[row_tap, col_tap]
            )
    normalized_second, standardized_second, inverse_deviation_second = norm_ahead_pass(
        dilated_out.reshape(pixels, -1), mask_column_vector, pixel_number_count, dilated_norm_params
    )
    hidden_two = (
        jax.nn.silu(normalized_second)
        .astype(jnp.bfloat16)
        .reshape(image_inputs, tile_row_count, frame_columns, -1)
    )
    hidden_two_full = widen(hidden_two)
    expanded_output = forward_dot(hidden_two_full, conv_expand).reshape(pixels, -1)
    normalized_third, standardized_third, inverse_deviation_third = norm_ahead_pass(
        expanded_output, mask_column_vector, pixel_number_count, expansion_norm_params
    )
    residual_sum = normalized_third + trunk_input.reshape(pixels, -1).astype(jnp.float32)
    trunk_out = (
        jax.nn.silu(residual_sum)
        .astype(jnp.bfloat16)
        .reshape(image_inputs, tile_row_count, frame_columns, quarter)
    )
    trunk_full = widen(trunk_out)
    branch_outs = [backward_dot(trunk_full, aspp_point)]
    for branch_id in range(3):
        dilation = RATES[branch_id]
        hops = dilation // tile_row_count
        partials = [0.0, 0.0, 0.0]
        for col_tap in range(3):
            shifted = move(trunk_full, -(col_tap - 1) * dilation, 2)
            products = backward_dot(shifted, stacked_taps(aspp_rates[branch_id], col_tap))
            for row_tap in range(3):
                partials[row_tap] = (
                    partials[row_tap]
                    + products[..., row_tap * branch_part : (row_tap + 1) * branch_part]
                )
        upper = send_down(partials[0].astype(jnp.bfloat16), hops).astype(jnp.float32)
        lower_part = send_up(partials[2].astype(jnp.bfloat16), hops).astype(jnp.float32)
        branch_outs.append(partials[1] + upper + lower_part)
    spatial_flattened = jnp.stack(branch_outs, axis=3).reshape(pixels, -1)
    branch_gain_bias = branch_norms.reshape(2, -1)
    normalized_spatial, standardized_spatial, inverse_deviation_spatial = norm_ahead_pass(
        spatial_flattened, mask_column_vector, pixel_number_count, branch_gain_bias
    )
    spatial_act = (
        jax.nn.silu(normalized_spatial)
        .astype(jnp.bfloat16)
        .reshape(image_inputs, tile_row_count, frame_columns, 4, branch_part)
    )
    pooled_local = lax.dot_general(
        valid_mask.astype(jnp.bfloat16),
        trunk_full,
        (((1, 2), (1, 2)), ((0,), (0,))),
        preferred_element_type=jnp.float32,
    )
    pooled = (over_rows(pooled_local) / image_areas[:, None]).astype(jnp.bfloat16)
    pooling_convolution = backward_dot(pooled, aspp_pool)
    normalized_poolbranch, standardized_poolbranch, inverse_deviation_poolbranch = norm_ahead_pass(
        pooling_convolution, row_portion, image_overall_count, pooling_norm_params
    )
    pool_act = jax.nn.silu(normalized_poolbranch).astype(jnp.bfloat16)
    pool_wide = jnp.broadcast_to(
        pool_act[:, None, None, None, :],
        (image_inputs, tile_row_count, frame_columns, 1, branch_part),
    )
    concat = jnp.concatenate([spatial_act, pool_wide], axis=3)
    concat_flat = widen(concat).reshape(pixels, -1)
    proj_kernel = (
        aspp_project.reshape(branch_part, 5, branch_total, branch_part)
        .transpose(0, 2, 1, 3)
        .reshape(branch_part, 5 * branch_total * branch_part)
    )
    projected_output = backward_dot(concat_flat, proj_kernel)
    normalized_projector, standardized_projector, inverse_deviation_projector = norm_ahead_pass(
        projected_output, mask_column_vector, pixel_number_count, projection_norm_params
    )
    features = (
        jax.nn.silu(normalized_projector)
        .astype(jnp.bfloat16)
        .reshape(image_inputs, tile_row_count, frame_columns, -1)
    )
    features_wide = widen(features).reshape(pixels, -1).astype(jnp.float32)
    head_wide = head_weight.astype(jnp.float32)
    logits = jnp.dot(features_wide, head_wide, precision=HIGH) + head_bias
    classes = head_bias.shape[0] - 3
    seg_logits = logits[:, :classes]
    labels_flat = seg_labels.reshape(pixels)
    classes_hot = (labels_flat[:, None] == jnp.arange(classes, dtype=jnp.int32)[None, :]).astype(
        jnp.float32
    )
    cross = jax.nn.logsumexp(seg_logits, axis=1) - jnp.sum(seg_logits * classes_hot, axis=1)
    depth_gap = logits[:, classes] - depth_target.reshape(pixels)
    smooth_abs = jnp.sqrt(depth_gap * depth_gap + 1.0)
    normal_gap = logits[:, classes + 1 :] - jnp.moveaxis(normal_target, 1, 3).reshape(pixels, 2)
    local_losses = jnp.stack(
        [
            jnp.sum(mask_flat * cross),
            jnp.sum(mask_flat * (smooth_abs - 1.0)),
            jnp.sum(mask_flat * jnp.sum(normal_gap * normal_gap, axis=1)),
        ]
    )
    task_weights = jnp.exp(-log_vars)
    grad_seg = (jax.nn.softmax(seg_logits, axis=1) - classes_hot) * (
        task_weights[0] / pixel_number_count * mask_flat
    )[:, None]
    grad_depth = depth_gap / smooth_abs * (task_weights[1] / pixel_number_count * mask_flat)
    grad_normal = 2.0 * normal_gap * (task_weights[2] / pixel_number_count * mask_flat)[:, None]
    grad_logits = jnp.concatenate([grad_seg, grad_depth[:, None], grad_normal], axis=1)
    head_local = lax.dot_general(
        features_wide, grad_logits, (((0,), (0,)), ((), ())), precision=HIGH
    )
    loss_parts, grad_head_weight, grad_head_bias = lax.psum(
        (local_losses, head_local, jnp.sum(grad_logits, axis=0)), ("rows", "batch")
    )
    task_losses = loss_parts / pixel_number_count
    total_loss = jnp.sum(task_weights * task_losses + log_vars)
    grad_log_vars = 1.0 - task_weights * task_losses
    grad_features = jnp.dot(grad_logits, head_wide.T, precision=HIGH)
    my_features_grad = lax.dynamic_slice_in_dim(
        grad_features, lax.axis_index("branch") * branch_part, branch_part, 1
    )
    gradient_before_projector = my_features_grad * silu_slope(normalized_projector)
    grad_proj_in, grad_project_norm = norm_reverse_pass(
        gradient_before_projector,
        standardized_projector,
        inverse_deviation_projector,
        1.0,
        mask_column_vector,
        pixel_number_count,
        projection_norm_params,
    )
    grad_proj_low = grad_proj_in.astype(jnp.bfloat16)
    proj_kernel_grad = lax.dot_general(
        grad_proj_low, concat_flat, (((0,), (0,)), ((), ())), preferred_element_type=jnp.float32
    )
    grad_project_local = (
        proj_kernel_grad.reshape(branch_part, branch_total, 5, branch_part)
        .transpose(0, 2, 1, 3)
        .reshape(branch_part, 5, branch_total * branch_part)
    )
    concat_grad = forward_dot(grad_proj_low, proj_kernel).reshape(
        image_inputs, tile_row_count, frame_columns, -1
    )
    concat_grad = narrow(concat_grad).reshape(pixels, 5, branch_part)
    pool_grad_img = over_rows(
        jnp.sum(concat_grad[:, 4, :].reshape(image_inputs, -1, branch_part), axis=1)
    )
    gradient_before_poolbranch = pool_grad_img * silu_slope(normalized_poolbranch)
    grad_pool_conv, grad_pool_norm = norm_reverse_pass(
        gradient_before_poolbranch,
        standardized_poolbranch,
        inverse_deviation_poolbranch,
        row_portion,
        1.0,
        image_overall_count,
        pooling_norm_params,
    )
    pool_conv_low = grad_pool_conv.astype(jnp.bfloat16)
    grad_pool_local = (
        lax.dot_general(
            pool_conv_low, pooled, (((0,), (0,)), ((), ())), preferred_element_type=jnp.float32
        )
        * row_portion
    )
    pooled_grad = forward_dot(pool_conv_low, aspp_pool)
    gradient_before_spatialbranch = concat_grad[:, :4, :].reshape(pixels, -1) * silu_slope(
        normalized_spatial
    )
    grad_spatial, branch_norm_grad = norm_reverse_pass(
        gradient_before_spatialbranch,
        standardized_spatial,
        inverse_deviation_spatial,
        1.0,
        mask_column_vector,
        pixel_number_count,
        branch_gain_bias,
    )
    grad_branch_norms = branch_norm_grad.reshape(2, 4, branch_part)
    spatial_low = grad_spatial.astype(jnp.bfloat16).reshape(
        image_inputs, tile_row_count, frame_columns, 4, branch_part
    )
    point_grad = spatial_low[:, :, :, 0]
    grad_point_local = pixel_dot(point_grad, trunk_full)
    trunk_grad = forward_dot(point_grad, aspp_point)
    trunk_grad = (
        trunk_grad + valid_mask[..., None] * (pooled_grad / image_areas[:, None])[:, None, None, :]
    )
    rate_grads = []
    for branch_id in range(3):
        dilation = RATES[branch_id]
        hops = dilation // tile_row_count
        centre = spatial_low[:, :, :, branch_id + 1]
        grad_taps = jnp.concatenate(
            [send_up(centre, hops), centre, send_down(centre, hops)], axis=3
        )
        per_col = []
        for col_tap in range(3):
            shifted = move(trunk_full, -(col_tap - 1) * dilation, 2)
            per_col.append(pixel_dot(grad_taps, shifted))
            tap_grad = forward_dot(grad_taps, stacked_taps(aspp_rates[branch_id], col_tap))
            trunk_grad = trunk_grad + move(tap_grad, (col_tap - 1) * dilation, 2)
        col_stack = jnp.stack(per_col, axis=0).reshape(3, 3, branch_part, -1)
        rate_grads.append(col_stack.transpose(1, 0, 2, 3))
    grad_rates_local = jnp.stack(rate_grads, axis=0)
    trunk_own = narrow(trunk_grad).reshape(pixels, -1)
    gradient_shortcut = trunk_own * silu_slope(residual_sum)
    grad_expanded, grad_norm_expand = norm_reverse_pass(
        gradient_shortcut,
        standardized_third,
        inverse_deviation_third,
        1.0,
        mask_column_vector,
        pixel_number_count,
        expansion_norm_params,
    )
    expanded_low = grad_expanded.astype(jnp.bfloat16).reshape(
        image_inputs, tile_row_count, frame_columns, -1
    )
    grad_expand_local = pixel_dot(hidden_two_full, expanded_low)
    hidden_two_grad = narrow(backward_dot(expanded_low, conv_expand)).reshape(pixels, -1)
    gradient_before_second = hidden_two_grad * silu_slope(normalized_second)
    gradient_dilated_input, gradient_dilated_norm = norm_reverse_pass(
        gradient_before_second,
        standardized_second,
        inverse_deviation_second,
        1.0,
        mask_column_vector,
        pixel_number_count,
        dilated_norm_params,
    )
    dilated_lowprec = gradient_dilated_input.astype(jnp.bfloat16).reshape(
        image_inputs, tile_row_count, frame_columns, -1
    )
    dilated_padded = pad_rows(dilated_lowprec)
    hidden_one_grad = 0.0
    kernel_grads = []
    for row_tap in range(3):
        band = hidden_full[:, 4 * row_tap : 4 * row_tap + tile_row_count]
        grad_band = dilated_padded[:, 8 - 4 * row_tap : 8 - 4 * row_tap + tile_row_count]
        for col_tap in range(3):
            kernel_grads.append(pixel_dot(move(band, -(col_tap - 1) * 4, 2), dilated_lowprec))
            hidden_one_grad = hidden_one_grad + backward_dot(
                move(grad_band, (col_tap - 1) * 4, 2), conv_dilated[row_tap, col_tap]
            )
    grad_dilated_local = jnp.stack(kernel_grads, axis=0).reshape(3, 3, hidden_full.shape[3], -1)
    hidden_one_own = narrow(hidden_one_grad).reshape(pixels, -1)
    gradient_before_first = hidden_one_own * silu_slope(normalized_first)
    grad_reduced, grad_norm_reduce = norm_reverse_pass(
        gradient_before_first,
        standardized_first,
        inverse_deviation_first,
        1.0,
        mask_column_vector,
        pixel_number_count,
        reduction_norm_params,
    )
    reduced_low = grad_reduced.astype(jnp.bfloat16).reshape(
        image_inputs, tile_row_count, frame_columns, -1
    )
    grad_reduce_local = pixel_dot(input_full, reduced_low)
    input_grad = narrow(backward_dot(reduced_low, conv_reduce))
    grad_input = input_grad + gradient_shortcut.reshape(
        image_inputs, tile_row_count, frame_columns, quarter
    )
    grad_reduce, grad_dilated, grad_expand, grad_point, grad_rates, grad_pool, grad_project = (
        lax.psum_scatter(grad_reduce_local, ("rows", "batch"), scatter_dimension=0, tiled=True),
        lax.psum_scatter(grad_dilated_local, ("rows", "batch"), scatter_dimension=2, tiled=True),
        lax.psum_scatter(grad_expand_local, ("rows", "batch"), scatter_dimension=0, tiled=True),
        lax.psum_scatter(grad_point_local, ("rows", "batch"), scatter_dimension=1, tiled=True),
        lax.psum_scatter(grad_rates_local, ("rows", "batch"), scatter_dimension=4, tiled=True),
        lax.psum_scatter(grad_pool_local, ("rows", "batch"), scatter_dimension=1, tiled=True),
        lax.psum_scatter(grad_project_local, ("rows", "batch"), scatter_dimension=2, tiled=True),
    )
    return (
        features,
        total_loss,
        grad_input,
        grad_reduce,
        grad_dilated,
        grad_expand,
        grad_norm_reduce,
        gradient_dilated_norm,
        grad_norm_expand,
        grad_point,
        grad_rates,
        grad_pool,
        grad_branch_norms,
        grad_pool_norm,
        grad_project,
        grad_project_norm,
        grad_head_weight,
        grad_head_bias,
        grad_log_vars,
    )


def solution(mesh):
    in_specs = (
        P("batch", "rows", None, "branch"),
        P(None, "branch"),
        P(None, None, None, "branch"),
        P(None, "branch"),
        P(None, "branch"),
        P(None, "branch"),
        P(None, "branch"),
        P("branch", None),
        P(None, None, None, "branch", None),
        P("branch", None),
        P(None, None, "branch"),
        P(None, "branch"),
        P("branch", None, None),
        P(None, "branch"),
        P(),
        P(),
        P(),
        P(),
        P("batch", "rows", None),
        P("batch", "rows", None),
        P("batch", None, "rows", None),
    )
    out_specs = (
        P("batch", "rows", None, "branch"),
        P(),
        P("batch", "rows", None, "branch"),
        P(("rows", "batch"), "branch"),
        P(None, None, ("rows", "batch"), "branch"),
        P(("rows", "batch"), "branch"),
        P(None, "branch"),
        P(None, "branch"),
        P(None, "branch"),
        P("branch", ("rows", "batch")),
        P(None, None, None, "branch", ("rows", "batch")),
        P("branch", ("rows", "batch")),
        P(None, None, "branch"),
        P(None, "branch"),
        P("branch", None, ("rows", "batch")),
        P(None, "branch"),
        P(),
        P(),
        P(),
    )
    return jax.shard_map(local, mesh=mesh, in_specs=in_specs, out_specs=out_specs, check_vma=False)
```

profile of v0, /device:TPU:0, one launch (start us, length us, event | category | flops | bytes accessed | tf_op | source)
XLA Modules:
  0.0 1552.9 jit_solution(7915229871930934254)
XLA Ops:
  13.4 69.2 %all-gather.7.cloned.1.call-done = bf16[1,12,128,2048]{3,2,1,0:T(8,128)(2,1)} async-done(((bf16[1,12,128,512]{3,2,1,0:T(8,128)(2,1)}), bf16[1,12,128,2048]{3,2,1,0:T(8,128)(2,1)}) %all-gather.7.cloned.1.call-update) | async-done | bytes 6291472 | tf_op jit(solution)/shard_map/all_gather | solution.py:71
  87.2 16.8 %psum.203 = f32[128]{0:T(128)S(1)} all-reduce(f32[128]{0:T(128)S(1)} %get-tuple-element.234), channel_id=1, replica_groups=mesh['branch'=4,'rows'=2,'batch'=4] {'rows','batch'}, use_global_device_ids=true, to_apply=%region_1.0 | all-reduce | flops 128 | bytes 1024 | tf_op jit(solution)/shard_map/psum | solution.py:101
  105.0 13.7 psum.204
  126.9 37.5 %all-gather.9.cloned.1.call-done = bf16[1,20,128,512]{3,2,1,0:T(8,128)(2,1)} async-done(((bf16[1,20,128,128]{3,2,1,0:T(8,128)(2,1)}), bf16[1,20,128,512]{3,2,1,0:T(8,128)(2,1)}) %all-gather.9.cloned.1.call-update) | async-done | bytes 2621456 | tf_op jit(solution)/shard_map/all_gather | solution.py:71
  173.0 16.9 %psum.205 = f32[128]{0:T(128)S(1)} all-reduce(f32[128]{0:T(128)S(1)} %get-tuple-element.236), channel_id=1, replica_groups=mesh['branch'=4,'rows'=2,'batch'=4] {'rows','batch'}, use_global_device_ids=true, to_apply=%region_6.7 | all-reduce | flops 128 | bytes 1024 | tf_op jit(solution)/shard_map/psum | solution.py:101
  190.9 13.7 psum.206
  206.4 30.5 %all-gather.15.cloned.1.call-done = bf16[12,128,512]{2,1,0:T(8,128)(2,1)} async-done(((bf16[12,128,128]{2,1,0:T(8,128)(2,1)}), bf16[12,128,512]{2,1,0:T(8,128)(2,1)}) %all-gather.15.cloned.1.call-update) | async-done | bytes 1572880 | tf_op jit(solution)/shard_map/all_gather | solution.py:71
  240.9 16.8 %psum.207 = f32[512]{0:T(512)S(1)} all-reduce(f32[512]{0:T(512)S(1)} %get-tuple-element.238), channel_id=1, replica_groups=mesh['branch'=4,'rows'=2,'batch'=4] {'rows','batch'}, use_global_device_ids=true, to_apply=%region_10.11 | all-reduce | flops 512 | bytes 4096 | tf_op jit(solution)/shard_map/psum | solution.py:101
  260.9 13.9 psum.208
  288.6 60.9 %all-gather.11.cloned.1.call-done = bf16[1,12,128,2048]{3,2,1,0:T(8,128)(2,1)} async-done(((bf16[1,12,128,512]{3,2,1,0:T(8,128)(2,1)}), bf16[1,12,128,2048]{3,2,1,0:T(8,128)(2,1)}) %all-gather.11.cloned.1.call-update) | async-done | bytes 6291472 | tf_op jit(solution)/shard_map/all_gather | solution.py:71
  386.7 17.8 %all-reduce.30 = (f32[64]{0:T(128)S(1)}, f32[256]{0:T(256)S(1)}) all-reduce(f32[64]{0:T(128)S(1)} %get-tuple-element.240, f32[256]{0:T(256)S(1)} %reduce_sum.319), channel_id=1, replica_groups=mesh['branch'=4,'rows'=2,'batch'=4] {'rows','batch'}, use_global_device_ids=true, to_apply=%region_18.19 | all-reduce | flops 320 | bytes 2560 | tf_op jit(solution)/shard_map/psum | solution.py:101
  406.7 14.1 all-reduce.29
  430.1 43.6 %all-gather.13.cloned.1.call-done = bf16[1,12,128,20,64]{2,4,1,0,3:T(8,128)(2,1)} async-done(((bf16[1,12,128,5,64]{2,4,1,0,3:T(8,128)(2,1)}), bf16[1,12,128,20,64]{2,4,1,0,3:T(8,128)(2,1)}) %all-gather.13.cloned.1.call-update) | async-done | bytes 3932176 | tf_op jit(solution)/shard_map/all_gather | solution.py:71
  483.2 16.8 %psum.214 = f32[64]{0:T(128)S(1)} all-reduce(f32[64]{0:T(128)S(1)} %get-tuple-element.242), channel_id=1, replica_groups=mesh['branch'=4,'rows'=2,'batch'=4] {'rows','batch'}, use_global_device_ids=true, to_apply=%region_21.22 | all-reduce | flops 64 | bytes 512 | tf_op jit(solution)/shard_map/psum | solution.py:101
  500.8 13.7 psum.215
  516.4 13.2 all_gather.23
  535.5 14.6 all-reduce.28
  576.9 42.7 %reduce-scatter.37.cloned.1.call-done = bf16[320,1536]{1,0:T(8,128)(2,1)} async-done(((bf16[1280,1536]{1,0:T(8,128)(2,1)}), bf16[320,1536]{1,0:T(8,128)(2,1)}) %reduce-scatter.37.cloned.1.call-update) | async-done | bytes 983056
  636.0 16.7 %all-reduce.27 = (f32[256]{0:T(256)S(1)}, f32[256]{0:T(256)S(1)}, f32[64]{0:T(128)S(1)}, f32[64]{0:T(128)S(1)}) all-reduce(f32[256]{0:T(256)S(1)} %reduce_sum.338, f32[256]{0:T(256)S(1)} %reduce_sum.336, f32[64]{0:T(128)S(1)} %multiply_bitcast_fusion, ...), channel_id=1, replica_groups=mesh['branch'=4,'rows'=2,'batch'=4] {'rows','batch'}, use_global_device_ids=true, to_apply=%region_42.43 | all-reduce | flops 640 | bytes 5120 | tf_op jit(solution)/shard_map/psum | solution.py:112
  722.2 34.4 %fusion.9 = bf16[1,12,128,2048]{3,2,1,0:T(8,128)(2,1)} fusion(f32[1,12,128,2048]{3,2,1,0:T(8,128)} %convolution_bitcast_fusion.5, f32[1,12,128,2048]{3,2,1,0:T(8,128)} %convolution_bitcast_fusion.4, f32[1,12,128,2048]{3,2,1,0:T(8,128)} %convolution_bitcast_fusion.3, f32[1,12,128,2048]{3,2,1,0:T(8,128)} %convolution_bitcast_fusion.2, ...), kind=kOutput, calls=%fused_computation.16 | convolution fusion | flops 1249837056 | bytes 120928256 | tf_op jit(solution)/shard_map/dot_general | solution.py:47
  756.7 68.3 %reduce-scatter.19.cloned.1.call-done = bf16[1,12,128,512]{3,2,1,0:T(8,128)(2,1)} async-done(((bf16[1,12,128,2048]{3,2,1,0:T(8,128)(2,1)}), bf16[1,12,128,512]{3,2,1,0:T(8,128)(2,1)}) %reduce-scatter.19.cloned.1.call-update) | async-done | bytes 1572880 | tf_op jit(solution)/shard_map/reduce_scatter | solution.py:75
  829.7 16.8 %all-reduce.26 = (f32[512]{0:T(512)S(1)}, f32[512]{0:T(512)S(1)}) all-reduce(f32[512]{0:T(512)S(1)} %get-tuple-element.115, f32[512]{0:T(512)S(1)} %get-tuple-element.114), channel_id=1, replica_groups=mesh['branch'=4,'rows'=2,'batch'=4] {'rows','batch'}, use_global_device_ids=true, to_apply=%region_51.52 | all-reduce | flops 1024 | bytes 8192 | tf_op jit(solution)/shard_map/psum | solution.py:112
  858.8 28.3 %reduce-scatter.39.cloned.1.call-done = bf16[128,1536]{1,0:T(8,128)(2,1)} async-done(((bf16[512,1536]{1,0:T(8,128)(2,1)}), bf16[128,1536]{1,0:T(8,128)(2,1)}) %reduce-scatter.39.cloned.1.call-update) | async-done | bytes 393232
  889.3 16.8 %all-reduce.25 = (f32[128]{0:T(128)S(1)}, f32[128]{0:T(128)S(1)}) all-reduce(f32[128]{0:T(128)S(1)} %get-tuple-element.121, f32[128]{0:T(128)S(1)} %get-tuple-element.120), channel_id=1, replica_groups=mesh['branch'=4,'rows'=2,'batch'=4] {'rows','batch'}, use_global_device_ids=true, to_apply=%region_56.57 | all-reduce | flops 256 | bytes 2048 | tf_op jit(solution)/shard_map/psum | solution.py:112
  964.0 28.1 %all-reduce.24 = (f32[3]{0:T(128)}, f32[128]{0:T(128)S(1)}, f32[128]{0:T(128)S(1)}, f32[256,22]{0,1:T(8,128)}, f32[22]{0:T(128)}) all-reduce(f32[3]{0:T(128)S(1)} %pad_maximum_fusion.19, f32[128]{0:T(128)S(1)} %get-tuple-element.119, f32[128]{0:T(128)S(1)} %get-tuple-element.118, ...), channel_id=1, replica_groups=mesh['branch'=4,'rows'=2,'batch'=4] {'rows','batch'}, use_global_device_ids=true, to_apply=%region_31.32 | all-reduce | flops 5913 | bytes 47304 | tf_op jit(solution)/shard_map/psum | solution.py:298
  1009.8 12.8 pad_maximum_fusion
  1058.5 250.5 %reduce-scatter.31.cloned.1.call-done = f32[3,3,3,64,256]{4,3,1,2,0:T(8,128)} async-done(((f32[3,3,3,64,2048]{4,3,1,2,0:T(8,128)}), f32[3,3,3,64,256]{4,3,1,2,0:T(8,128)}) %reduce-scatter.31.cloned.1.call-update) | async-done | bytes 1769488 | tf_op jit(solution)/shard_map/reduce_scatter | solution.py:456
  1311.8 71.6 %reduce-scatter.21.cloned.1.call-done = bf16[1,12,128,512]{3,2,1,0:T(8,128)(2,1)} async-done(((bf16[1,12,128,2048]{3,2,1,0:T(8,128)(2,1)}), bf16[1,12,128,512]{3,2,1,0:T(8,128)(2,1)}) %reduce-scatter.21.cloned.1.call-update) | async-done | bytes 1572880 | tf_op jit(solution)/shard_map/reduce_scatter | solution.py:75
  1388.0 30.6 %reduce-scatter.33.cloned.1.call-done = f32[64,256]{1,0:T(8,128)} async-done(((f32[64,2048]{1,0:T(8,128)}), f32[64,256]{1,0:T(8,128)}) %reduce-scatter.33.cloned.1.call-update) | async-done | bytes 65552 | tf_op jit(solution)/shard_map/reduce_scatter | solution.py:457
  1418.6 34.2 %reduce-scatter.29.cloned.1.call-done = f32[64,256]{1,0:T(8,128)} async-done(((f32[64,2048]{1,0:T(8,128)}), f32[64,256]{1,0:T(8,128)}) %reduce-scatter.29.cloned.1.call-update) | async-done | bytes 65552 | tf_op jit(solution)/shard_map/reduce_scatter | solution.py:455
  1452.8 37.0 %reduce-scatter.27.cloned.1.call-done = f32[64,512]{1,0:T(8,128)} async-done(((f32[512,512]{1,0:T(8,128)}), f32[64,512]{1,0:T(8,128)}) %reduce-scatter.27.cloned.1.call-update) | async-done | bytes 131088 | tf_op jit(solution)/shard_map/reduce_scatter | solution.py:454
  1489.8 56.0 %reduce-scatter.25.cloned.1.call-done = f32[3,3,64,128]{3,2,1,0:T(8,128)} async-done(((f32[3,3,512,128]{3,2,1,0:T(8,128)}), f32[3,3,64,128]{3,2,1,0:T(8,128)}) %reduce-scatter.25.cloned.1.call-update) | async-done | bytes 294928 | tf_op jit(solution)/shard_map/reduce_scatter | solution.py:453
  (642 shorter events, 358.7 us)
Async XLA Ops:
  7.2 75.4 %all-gather.7.cloned.1.call-start = ((), (), s32[]{:S(2)}) async-start(), calls=%async_computation.12 | async-start | bytes 7864320 | tf_op jit(solution)/shard_map/all_gather | solution.py:71
  8.0 156.4 %all-gather.9.cloned.1.call-start = ((), (), s32[]{:S(2)}) async-start(), calls=%async_computation.13 | async-start | bytes 3276800 | tf_op jit(solution)/shard_map/all_gather | solution.py:71
  11.9 558.9 %copy-start.113 = (pred[128]{0:T(512)(128)(4,1)}, pred[128]{0:T(512)(128)(4,1)S(1)}, u32[]{:S(2)}) copy-start(pred[128]{0:T(512)(128)(4,1)S(1)} %compare_and_fusion) | copy-start | bytes 388
  12.6 558.3 %copy-start.105 = (pred[12]{0:T(512)(128)(4,1)}, pred[12]{0:T(512)(128)(4,1)S(1)}, u32[]{:S(2)}) copy-start(pred[12]{0:T(512)(128)(4,1)S(1)} %compare_and_fusion.1) | copy-start | bytes 40
  13.3 106.0 %copy-start.126 = (f32[128]{0:T(128)}, f32[128]{0:T(128)S(1)}, u32[]{:S(2)}) copy-start(f32[128]{0:T(128)S(1)} %get-tuple-element.223) | copy-start | bytes 1540
  13.3 106.0 %copy-start.128 = (f32[128]{0:T(128)}, f32[128]{0:T(128)S(1)}, u32[]{:S(2)}) copy-start(f32[128]{0:T(128)S(1)} %get-tuple-element.224) | copy-start | bytes 1540
  119.7 3.6 collective-permute-start
  122.0 3.2 collective-permute-start.1
  126.2 110.7 %all-gather.15.cloned.1.call-start = ((), (), s32[]{:S(2)}) async-start(), calls=%async_computation.25 | async-start | bytes 1966080 | tf_op jit(solution)/shard_map/all_gather | solution.py:71
  126.3 79.0 %copy-start.117 = (f32[128]{0:T(128)}, f32[128]{0:T(128)S(1)}, u32[]{:S(2)}) copy-start(f32[128]{0:T(128)S(1)} %get-tuple-element.221) | copy-start | bytes 1540
  126.3 79.0 %copy-start.130 = (f32[128]{0:T(128)}, f32[128]{0:T(128)S(1)}, u32[]{:S(2)}) copy-start(f32[128]{0:T(128)S(1)} %get-tuple-element.222) | copy-start | bytes 1540
  206.3 143.1 %all-gather.11.cloned.1.call-start = ((), (), s32[]{:S(2)}) async-start(), calls=%async_computation.14 | async-start | bytes 7864320 | tf_op jit(solution)/shard_map/all_gather | solution.py:71
  279.7 194.0 %all-gather.13.cloned.1.call-start = ((), (), s32[]{:S(2)}) async-start(), calls=%async_computation.15 | async-start | bytes 4915200 | tf_op jit(solution)/shard_map/all_gather | solution.py:71
  365.2 21.0 %collective-permute-start.2 = (bf16[1,12,128,64]{2,3,1,0:T(8,128)(2,1)S(1)}, bf16[1,12,128,64]{2,3,1,0:T(8,128)(2,1)S(1)}, u32[]{:S(2)}, u32[]{:S(2)}) collective-permute-start(bf16[1,12,128,64]{2,3,1,0:T(8,128)(2,1)S(1)} %get-tuple-element.163), channel_id=1, source_target_pairs={{0,4},{1,5},{2,6},{3,7},{8,12},{9,13},{10,14},{11,15},{16,20},{17,... | collective-permute-start | bytes 589832 | tf_op jit(solution)/shard_map/ppermute | solution.py:31
  367.3 18.9 %collective-permute-start.3 = (bf16[1,12,128,64]{2,3,1,0:T(8,128)(2,1)S(1)}, bf16[1,12,128,64]{2,3,1,0:T(8,128)(2,1)S(1)}, u32[]{:S(2)}, u32[]{:S(2)}) collective-permute-start(bf16[1,12,128,64]{2,3,1,0:T(8,128)(2,1)S(1)} %get-tuple-element.164), channel_id=1, source_target_pairs={{4,0},{5,1},{6,2},{7,3},{12,8},{13,9},{14,10},{15,11},{20,16},{21,... | collective-permute-start | bytes 589832 | tf_op jit(solution)/shard_map/ppermute | solution.py:31
  424.1 195.5 %reduce-scatter.37.cloned.1.call-start = ((), (), s32[]{:S(2)}) async-start(), calls=%async_computation.26 | async-start | bytes 4915200
  570.8 254.2 %reduce-scatter.19.cloned.1.call-start = ((), (), s32[]{:S(2)}) async-start(), calls=%async_computation.16 | async-start | bytes 7864320 | tf_op jit(solution)/shard_map/reduce_scatter | solution.py:75
  570.9 85.2 %copy-start.102 = (f32[12,128]{1,0:T(8,128)}, f32[12,128]{1,0:T(8,128)S(1)}, u32[]{:S(2)}) copy-start(f32[12,128]{1,0:T(8,128)S(1)} %and_select_fusion.2) | copy-start | bytes 18436
  659.1 49.7 %collective-permute-start.5 = (bf16[1,12,128,64]{2,3,1,0:T(8,128)(2,1)S(1)}, bf16[1,12,128,64]{2,3,1,0:T(8,128)(2,1)S(1)}, u32[]{:S(2)}, u32[]{:S(2)}) collective-permute-start(bf16[1,12,128,64]{2,3,1,0:T(8,128)(2,1)S(1)} %get-tuple-element.199), channel_id=1, source_target_pairs={{0,4},{1,5},{2,6},{3,7},{8,12},{9,13},{10,14},{11,15},{16,20},{17,... | collective-permute-start | bytes 589832 | tf_op jit(solution)/shard_map/ppermute | solution.py:31
  661.4 47.5 %collective-permute-start.4 = (bf16[1,12,128,64]{2,3,1,0:T(8,128)(2,1)S(1)}, bf16[1,12,128,64]{2,3,1,0:T(8,128)(2,1)S(1)}, u32[]{:S(2)}, u32[]{:S(2)}) collective-permute-start(bf16[1,12,128,64]{2,3,1,0:T(8,128)(2,1)S(1)} %get-tuple-element.199), channel_id=1, source_target_pairs={{4,0},{5,1},{6,2},{7,3},{12,8},{13,9},{14,10},{15,11},{20,16},{21,... | collective-permute-start | bytes 589832 | tf_op jit(solution)/shard_map/ppermute | solution.py:31
  756.6 130.5 %reduce-scatter.39.cloned.1.call-start = ((), (), s32[]{:S(2)}) async-start(), calls=%async_computation.27 | async-start | bytes 1966080
  858.7 101.2 %reduce-scatter.41.cloned.1.call-start = ((), (), s32[]{:S(2)}) async-start(), calls=%async_computation.28 | async-start | bytes 1966080
  908.5 5.1 collective-permute-start.6
  909.8 4.0 collective-permute-start.7
  927.7 122.7 %reduce-scatter.35.cloned.1.call-start = ((), (), s32[]{:S(2)}) async-start(), calls=%async_computation.24 | async-start | bytes 1179648 | tf_op jit(solution)/shard_map/reduce_scatter | solution.py:458
  939.6 117.3 %reduce-scatter.23.cloned.1.call-start = ((), (), s32[]{:S(2)}) async-start(), calls=%async_computation.18 | async-start | bytes 1179648 | tf_op jit(solution)/shard_map/reduce_scatter | solution.py:452
  997.5 311.4 %reduce-scatter.31.cloned.1.call-start = ((), (), s32[]{:S(2)}) async-start(), calls=%async_computation.22 | async-start | bytes 15925248 | tf_op jit(solution)/shard_map/reduce_scatter | solution.py:456
  1022.6 360.8 %reduce-scatter.21.cloned.1.call-start = ((), (), s32[]{:S(2)}) async-start(), calls=%async_computation.17 | async-start | bytes 7864320 | tf_op jit(solution)/shard_map/reduce_scatter | solution.py:75
  1027.1 391.5 %reduce-scatter.33.cloned.1.call-start = ((), (), s32[]{:S(2)}) async-start(), calls=%async_computation.23 | async-start | bytes 589824 | tf_op jit(solution)/shard_map/reduce_scatter | solution.py:457
  1028.8 424.0 %reduce-scatter.29.cloned.1.call-start = ((), (), s32[]{:S(2)}) async-start(), calls=%async_computation.21 | async-start | bytes 589824 | tf_op jit(solution)/shard_map/reduce_scatter | solution.py:455
  1033.9 455.9 %reduce-scatter.27.cloned.1.call-start = ((), (), s32[]{:S(2)}) async-start(), calls=%async_computation.20 | async-start | bytes 1179648 | tf_op jit(solution)/shard_map/reduce_scatter | solution.py:454
  1037.4 508.5 %reduce-scatter.25.cloned.1.call-start = ((), (), s32[]{:S(2)}) async-start(), calls=%async_computation.19 | async-start | bytes 2654208 | tf_op jit(solution)/shard_map/reduce_scatter | solution.py:453
  (177 other events, 1970.5 us)
Sparse Core Ops, SparseCore 0:
  9.9 72.7 all-gather.6
  126.3 38.0 all-gather.8
  206.5 30.3 all-gather.14
  279.9 69.5 all-gather.10
  424.3 49.4 all-gather.12
  570.9 48.7 reduce-scatter.36
  756.7 68.1 reduce-scatter.18
  858.8 28.2 reduce-scatter.38
  927.8 28.1 reduce-scatter.40
  958.7 35.7 reduce-scatter.34
  997.6 34.8 reduce-scatter.22
  1034.7 274.2 reduce-scatter.30
  1311.9 71.4 reduce-scatter.20
  1386.1 32.4 reduce-scatter.32
  1421.4 31.4 reduce-scatter.28
  1455.5 34.2 reduce-scatter.26
  1492.6 53.2 reduce-scatter.24
where the time goes:
time: 1560 us; the launch traced here: 1550 us
  waiting for transfers between devices  864 us (55%)
  blocking collectives  265 us (17%)
  matrix products  205 us (13%)
  local copies, waits for them, and re-layouts  90.9 us (6%)
  other arithmetic  85.3 us (5%)
  between operations  25.7 us (2%)
  starting transfers between devices  16.9 us (1%)
    reduce_scatter x1, waiting for transfers between devices, local(): lax.psum_scatter(grad_rates_local, ('rows', 'batch'), scatter_dimension=4...  250 us
    all_gather x5, waiting for transfers between devices, widen(): return lax.all_gather(tensor, 'branch', axis=3, tiled=True)  242 us
    reduce_scatter x2, waiting for transfers between devices, narrow(): lax.psum_scatter(tensor.astype(jnp.bfloat16), 'branch', scatter_dimension...  140 us
    dot_general x23, matrix products, forward_dot(): return jnp.dot(lhs_arr, rhs_arr, preferred_element_type=jnp.float32)  111 us
    psum x5, blocking collectives, norm_ahead_pass(): summed = lax.psum(jnp.sum(tensor * weight, axis=0), ('rows', 'batch'))  85.1 us
    unnamed x20, waiting for transfers between devices  72 us
    psum x5, blocking collectives, norm_ahead_pass(): lax.psum(jnp.sum(weight * centered * centered, axis=0), ('rows', 'batch'))  69.1 us
    psum x4, blocking collectives, norm_reverse_pass(): lax.psum((jnp.sum(grad_out * weight_all, axis=0), jnp.sum(grad_out * norm...  64.9 us
  transfers between devices with their start and end apart: 25, of which 16 were waited for; matrix products, arithmetic and copies ran while one was open for 12% of the time, Pallas kernels for 0%

commit v1 on v0

--- a/solution.py
+++ b/solution.py
@@ -1,6 +1,8 @@
 import jax
 import jax.numpy as jnp
 from jax import lax
+from jax.experimental import pallas as pl
+from jax.experimental.pallas import tpu as pltpu
 from jax.sharding import PartitionSpec as P
 
 EPS = 1e-05
@@ -122,6 +124,385 @@
 
 def stacked_taps(kernels, col_tap):
     return jnp.concatenate([kernels[0, col_tap], kernels[1, col_tap], kernels[2, col_tap]], axis=0)
+
+
+MESH = pl.DeviceIdType.MESH
+F32 = jnp.float32
+BF16 = jnp.bfloat16
+VMEM_LIMIT = 60 * 2**20
+
+
+class Net:
+    def __init__(self, send_sems, recv_sems):
+        self.m = lax.axis_index("branch")
+        self.r = lax.axis_index("rows")
+        self.z = lax.axis_index("batch")
+        self.send_sems, self.recv_sems, self.count = send_sems, recv_sems, 0
+        self.side = (self.m ^ 1, self.r, self.z)
+        self.over = (self.m ^ 2, self.r, self.z)
+        self.diagonal = (self.m ^ 3, self.r, self.z)
+        self.core = (self.m, 1 - self.r, self.z)
+        self.slot = self.r * 4 + self.z
+        self.group = [
+            (self.m, lax.rem(self.r + i, 2), lax.rem(self.z + j, 4))
+            for i in range(2)
+            for j in range(4)
+            if i or j
+        ]
+
+    def send(self, src, dst, device):
+        i = self.count
+        self.count += 1
+        copy = pltpu.make_async_remote_copy(
+            src_ref=src,
+            dst_ref=dst,
+            send_sem=self.send_sems.at[i],
+            recv_sem=self.recv_sems.at[i],
+            device_id=device,
+            device_id_type=MESH,
+        )
+        copy.start()
+        return copy
+
+
+def greet(peers):
+    barrier = pltpu.get_barrier_semaphore()
+    for peer in peers:
+        pl.semaphore_signal(barrier, inc=1, device_id=peer, device_id_type=MESH)
+    pl.semaphore_wait(barrier, len(peers))
+
+
+def each_rows(total, step, body):
+    def run(i, carry):
+        body(pl.ds(pl.multiple_of(i * step, step), step))
+        return carry
+
+    lax.fori_loop(0, total // step, run, 0)
+
+
+def lane_block(index, width=128):
+    return pl.ds(pl.multiple_of(index * width, width), width)
+
+
+def wide(tile, width):
+    count = width // tile.shape[1]
+    return tile if count == 1 else jnp.concatenate([tile] * count, axis=1)
+
+
+def column_sums(fn, total, width, number):
+    step = 16384 // width
+
+    def run(i, sums):
+        terms = fn(pl.ds(pl.multiple_of(i * step, step), step))
+        return tuple(
+            s + jnp.sum(t.reshape(step // 8, 8, width), axis=0) for s, t in zip(sums, terms)
+        )
+
+    sums = lax.fori_loop(
+        0, total // step, run, tuple(jnp.zeros((8, width), F32) for _ in range(number))
+    )
+    return [jnp.sum(s, axis=0, keepdims=True) for s in sums]
+
+
+def fold(row):
+    return row + pltpu.roll(wide(row, 128), 64, 1)
+
+
+def exchange(net, outgoing, incoming):
+    copies = [net.send(outgoing, incoming.at[net.slot], peer) for peer in net.group]
+    incoming[net.slot] = outgoing[...]
+    for copy in copies:
+        copy.wait()
+
+
+def statistics(net, value_ref, mask_ref, outgoing, incoming, counted, folded=False):
+    total, width = value_ref.shape
+    same = fold if folded else (lambda row: row)
+    first, number = column_sums(
+        lambda at: (value_ref[at, :] * wide(mask_ref[at, :], width), wide(mask_ref[at, :], width)),
+        total,
+        width,
+        2,
+    )
+    first, number = same(first), same(number)
+    centre = first / jnp.maximum(number, 1.0)
+
+    def squares(at):
+        gap = value_ref[at, :] - centre
+        return (gap * gap * wide(mask_ref[at, :], width),)
+
+    second = same(column_sums(squares, total, width, 1)[0])
+    outgoing[0:1, :] = first
+    outgoing[1:2, :] = second
+    outgoing[2:3, :] = number
+    exchange(net, outgoing, incoming)
+    firsts, seconds, numbers = incoming[:, 0, :], incoming[:, 1, :], incoming[:, 2, :]
+    mean = jnp.sum(firsts, axis=0, keepdims=True) / counted
+    drift = firsts / jnp.maximum(numbers, 1.0) - mean
+    variance = jnp.sum(seconds + numbers * drift * drift, axis=0, keepdims=True) / counted
+    return mean, lax.rsqrt(variance + EPS)
+
+
+def gather_blocks(net, part, rows):
+    pieces, size = 4, rows // 4
+    own, side, over = net.m, net.m ^ 1, net.m ^ 2
+
+    def at(i):
+        return pl.ds(i * size, size)
+
+    to_side, to_over = [], []
+    for i in range(pieces):
+        j = pieces - 1 - i
+        to_side.append(net.send(part(own, at(i)), part(own, at(i)), net.side))
+        to_over.append(net.send(part(own, at(j)), part(own, at(j)), net.over))
+    passed = []
+    for i in range(pieces):
+        j = pieces - 1 - i
+        to_side[i].wait_recv()
+        if i < pieces // 2:
+            passed.append(net.send(part(side, at(i)), part(side, at(i)), net.over))
+        to_over[i].wait_recv()
+        if i < pieces // 2:
+            passed.append(net.send(part(over, at(j)), part(over, at(j)), net.side))
+    for copy in to_side + to_over:
+        copy.wait_send()
+    for copy in passed:
+        copy.wait()
+
+
+def sum_scatter(net, part, bufs, out):
+    far, to_side, to_over, far_side, far_over, from_side, from_over = bufs
+    rows, width = out.shape
+    half, step = rows // 2, 16384 // width
+    head, tail = pl.ds(0, half), pl.ds(half, half)
+    across, side, over = net.m ^ 3, net.m ^ 1, net.m ^ 2
+
+    def fill(target, index, base):
+        def body(at):
+            rows_at = pl.ds(pl.multiple_of(at.start + base, step), step)
+            target[rows_at, :] = part[index, rows_at, :].astype(BF16)
+
+        each_rows(half, step, body)
+
+    def combine(target, index, base, arrived):
+        def body(at):
+            rows_at = pl.ds(pl.multiple_of(at.start + base, step), step)
+            target[rows_at, :] = (part[index, rows_at, :] + arrived[at, :].astype(F32)).astype(BF16)
+
+        each_rows(half, step, body)
+
+    fill(far, across, 0)
+    first = net.send(far.at[head], far_side, net.side)
+    fill(far, across, half)
+    second = net.send(far.at[tail], far_over, net.over)
+    fill(to_side, side, 0)
+    third = net.send(to_side.at[head], from_side.at[head], net.side)
+    fill(to_over, over, half)
+    fourth = net.send(to_over.at[tail], from_over.at[tail], net.over)
+    second.wait_recv()
+    combine(to_side, side, half, far_over)
+    fifth = net.send(to_side.at[tail], from_side.at[tail], net.side)
+    first.wait_recv()
+    combine(to_over, over, 0, far_side)
+    sixth = net.send(to_over.at[head], from_over.at[head], net.over)
+    for copy in (third, fourth, fifth, sixth):
+        copy.wait_recv()
+
+    def body(at):
+        out[at, :] = (
+            part[net.m, at, :] + from_side[at, :].astype(F32) + from_over[at, :].astype(F32)
+        )
+
+    each_rows(rows, step, body)
+    for copy in (first, second, third, fourth, fifth, sixth):
+        copy.wait_send()
+
+
+def scatter_buffers(rows, width):
+    whole, half = pltpu.VMEM((rows, width), BF16), pltpu.VMEM((rows // 2, width), BF16)
+    return [whole, whole, whole, half, half, whole, whole]
+
+
+def sigmoid(u):
+    return 0.5 * jnp.tanh(0.5 * u) + 0.5
+
+
+def slope(u):
+    s = sigmoid(u)
+    return s * (1.0 + u * (1.0 - s))
+
+
+def mm(a, b):
+    return jnp.dot(a, b, preferred_element_type=F32)
+
+
+def mm_t(a, b):
+    return lax.dot_general(a, b, (((1,), (1,)), ((), ())), preferred_element_type=F32)
+
+
+def tm_m(a, b):
+    return lax.dot_general(a, b, (((0,), (0,)), ((), ())), preferred_element_type=F32)
+
+
+def bottleneck_forward(
+    x, w_reduce, w_dilated, w_expand, mask, affine_1, affine_2, affine_3, counted_ref,
+    reduced, stats_1, hidden, dilated, stats_2, hidden_two, expanded, stats_3, trunk,
+    w_taps, part, b0, b1, b2, b3, b4, b5, b6, left, right, out_1, in_1, out_2, in_2, out_3, in_3,
+    local_sems, send_sems, recv_sems,
+):
+    net = Net(send_sems, recv_sems)
+    counted = counted_ref[0, 0]
+    loads = []
+    for i in range(3):
+        for j in range(3):
+            loads.append(
+                pltpu.make_async_copy(
+                    w_dilated.at[i, j],
+                    w_taps.at[i, :, pl.ds(j * 128, 128)],
+                    local_sems.at[i * 3 + j],
+                )
+            )
+            loads[-1].start()
+    greet([net.side, net.over] + net.group)
+
+    def reduce_rows(at):
+        cells = x[at, :]
+        for b in range(4):
+            part[b, at, :] = mm(cells, w_reduce[b])
+
+    each_rows(1536, 384, reduce_rows)
+    sum_scatter(net, part, (b0, b1, b2, b3, b4, b5, b6), reduced)
+    mean, inverse = statistics(net, reduced, mask, out_1, in_1, counted)
+    stats_1[0:1, :] = mean
+    stats_1[1:2, :] = inverse
+    stats_1[2:8, :] = jnp.zeros((6, 128), F32)
+
+    def activate_1(at):
+        u = affine_1[0:1, :] * ((reduced[at, :] - mean) * inverse) + affine_1[1:2, :]
+        rows_at = pl.ds(pl.multiple_of(at.start + 512, 128), 128)
+        hidden[rows_at, lane_block(net.m)] = (u * sigmoid(u)).astype(BF16)
+
+    each_rows(1536, 128, activate_1)
+    hidden[pl.ds(pl.multiple_of(net.r * 2048, 128), 512), :] = jnp.zeros((512, 512), BF16)
+
+    def hidden_block(b, at):
+        return hidden.at[pl.ds(at.start + 512, at.size), lane_block(b)]
+
+    gather_blocks(net, hidden_block, 1536)
+    halo = net.send(
+        hidden.at[pl.ds(pl.multiple_of(1536 - net.r * 1024, 128), 512)],
+        hidden.at[pl.ds(pl.multiple_of(net.r * 2048, 128), 512)],
+        net.core,
+    )
+    for side in (left, right):
+        side[:, 0:8, :] = jnp.zeros((12, 8, 128), F32)
+        side[:, 136:144, :] = jnp.zeros((12, 8, 128), F32)
+    for load in loads:
+        load.wait()
+    halo.wait()
+
+    def dilated_rows(i, carry):
+        total = 0.0
+        for tap in range(3):
+            rows_at = pl.ds(pl.multiple_of((i * 3 + 4 * tap) * 128, 128), 384)
+            total = total + mm(hidden[rows_at, :], w_taps[tap])
+        dilated[pl.ds(pl.multiple_of(i * 384, 128), 384), :] = total[:, 128:256]
+        left[pl.ds(i * 3, 3), 8:136, :] = total[:, 0:128].reshape(3, 128, 128)
+        right[pl.ds(i * 3, 3), 8:136, :] = total[:, 256:384].reshape(3, 128, 128)
+        return carry
+
+    lax.fori_loop(0, 4, dilated_rows, 0)
+
+    def add_columns(i, carry):
+        at = pl.ds(pl.multiple_of(i * 128, 128), 128)
+        dilated[at, :] = dilated[at, :] + left[i, 4:132, :] + right[i, 12:140, :]
+        return carry
+
+    lax.fori_loop(0, 12, add_columns, 0)
+    mean, inverse = statistics(net, dilated, mask, out_2, in_2, counted)
+    stats_2[0:1, :] = mean
+    stats_2[1:2, :] = inverse
+    stats_2[2:8, :] = jnp.zeros((6, 128), F32)
+
+    def activate_2(at):
+        u = affine_2[0:1, :] * ((dilated[at, :] - mean) * inverse) + affine_2[1:2, :]
+        hidden_two[at, lane_block(net.m)] = (u * sigmoid(u)).astype(BF16)
+
+    each_rows(1536, 128, activate_2)
+    gather_blocks(net, lambda b, at: hidden_two.at[at, lane_block(b)], 1536)
+
+    def expand_rows(at):
+        expanded[at, :] = mm(hidden_two[at, :], w_expand[...])
+
+    each_rows(1536, 384, expand_rows)
+    mean_3, inverse_3 = statistics(net, expanded, mask, out_3, in_3, counted)
+    stats_3[0:1, :] = mean_3
+    stats_3[1:2, :] = inverse_3
+    stats_3[2:8, :] = jnp.zeros((6, 512), F32)
+
+    def activate_3(at):
+        u = affine_3[0:1, :] * ((expanded[at, :] - mean_3) * inverse_3) + affine_3[1:2, :]
+        u = u + x[at, :].astype(F32)
+        trunk[at, :] = (u * sigmoid(u)).astype(BF16)
+
+    each_rows(1536, 32, activate_3)
+
+
+def call_kernel(body, name, number, args, hbm, outs, scratch, sems):
+    vmem = pl.BlockSpec(memory_space=pltpu.VMEM)
+    specs = [pl.BlockSpec(memory_space=pl.ANY) if i in hbm else vmem for i in range(len(args))]
+    return pl.pallas_call(
+        body,
+        out_shape=[jax.ShapeDtypeStruct(s, d) for s, d in outs],
+        in_specs=specs,
+        out_specs=[vmem] * len(outs),
+        scratch_shapes=list(scratch)
+        + [pltpu.SemaphoreType.DMA((sems,)), pltpu.SemaphoreType.DMA((sems,))],
+        name=name,
+        compiler_params=pltpu.CompilerParams(
+            collective_id=number, has_side_effects=True, vmem_limit_bytes=VMEM_LIMIT
+        ),
+    )(*args)
+
+
+def padded_affine(affine):
+    return jnp.concatenate([affine, jnp.zeros((6, affine.shape[1]), F32)], axis=0)
+
+
+def run_bottleneck(x, w_reduce, w_dilated, w_expand, mask, affines, counted):
+    return call_kernel(
+        bottleneck_forward,
+        "bottleneck",
+        0,
+        [x, w_reduce, w_dilated, w_expand, mask, *[padded_affine(a) for a in affines], counted],
+        (2,),
+        [
+            ((1536, 128), F32),
+            ((8, 128), F32),
+            ((2560, 512), BF16),
+            ((1536, 128), F32),
+            ((8, 128), F32),
+            ((1536, 512), BF16),
+            ((1536, 512), F32),
+            ((8, 512), F32),
+            ((1536, 512), BF16),
+        ],
+        [
+            pltpu.VMEM((3, 512, 384), BF16),
+            pltpu.VMEM((4, 1536, 128), F32),
+            *scatter_buffers(1536, 128),
+            pltpu.VMEM((12, 144, 128), F32),
+            pltpu.VMEM((12, 144, 128), F32),
+            pltpu.VMEM((8, 128), F32),
+            pltpu.VMEM((8, 8, 128), F32),
+            pltpu.VMEM((8, 128), F32),
+            pltpu.VMEM((8, 8, 128), F32),
+            pltpu.VMEM((8, 512), F32),
+            pltpu.VMEM((8, 8, 512), F32),
+            pltpu.SemaphoreType.DMA((9,)),
+        ],
+        64,
+    )
 
 
 def local(
@@ -480,6 +861,367 @@
     )
 
 
+def fast_local(
+    trunk_input,
+    conv_reduce,
+    conv_dilated,
+    conv_expand,
+    reduction_norm_params,
+    dilated_norm_params,
+    expansion_norm_params,
+    aspp_point,
+    aspp_rates,
+    aspp_pool,
+    branch_norms,
+    pooling_norm_params,
+    aspp_project,
+    projection_norm_params,
+    head_weight,
+    head_bias,
+    log_vars,
+    crop_boxes,
+    seg_labels,
+    depth_target,
+    normal_target,
+):
+    image_inputs, tile_row_count, frame_columns, quarter = trunk_input.shape
+    pixels = image_inputs * tile_row_count * frame_columns
+    branch_part = aspp_point.shape[0]
+    branch_total = lax.axis_size("branch")
+    row_portion = 1.0 / lax.axis_size("rows")
+    image_overall_count = float(crop_boxes.shape[0])
+    first_image = lax.axis_index("batch") * image_inputs
+    first_row = lax.axis_index("rows") * tile_row_count
+    my_boxes = lax.dynamic_slice_in_dim(crop_boxes, first_image, image_inputs, 0)
+    row_ids = first_row + jnp.arange(tile_row_count, dtype=jnp.int32)
+    col_ids = jnp.arange(frame_columns, dtype=jnp.int32)
+    inside_rows = (row_ids[None, :] >= my_boxes[:, 0:1]) & (
+        row_ids[None, :] < my_boxes[:, 0:1] + my_boxes[:, 2:3]
+    )
+    inside_cols = (col_ids[None, :] >= my_boxes[:, 1:2]) & (
+        col_ids[None, :] < my_boxes[:, 1:2] + my_boxes[:, 3:4]
+    )
+    valid_mask = (inside_rows[:, :, None] & inside_cols[:, None, :]).astype(jnp.float32)
+    mask_column_vector = valid_mask.reshape(pixels, 1)
+    mask_flat = valid_mask.reshape(pixels)
+    pixel_number_count = jnp.sum((crop_boxes[:, 2] * crop_boxes[:, 3]).astype(jnp.float32))
+    image_areas = (my_boxes[:, 2] * my_boxes[:, 3]).astype(jnp.float32)
+    x_own = trunk_input.reshape(pixels, quarter)
+    w_reduce = lax.all_to_all(conv_reduce.reshape(4, 512, 128), "branch", 0, 0)
+    mask_lanes = jnp.broadcast_to(mask_column_vector, (pixels, 128))
+    counted_cell = pixel_number_count.reshape(1, 1)
+    (
+        reduced_output,
+        stats_1,
+        hidden_pad,
+        dilated_out,
+        stats_2,
+        hidden_two_full,
+        expanded_output,
+        stats_3,
+        trunk_out,
+    ) = run_bottleneck(
+        x_own,
+        w_reduce,
+        conv_dilated,
+        conv_expand,
+        mask_lanes,
+        (reduction_norm_params, dilated_norm_params, expansion_norm_params),
+        counted_cell,
+    )
+    input_full = widen(trunk_input)
+    hidden_full = hidden_pad.reshape(1, 20, 128, 512)
+    hidden_two_full = hidden_two_full.reshape(1, 12, 128, 512)
+
+    def again(value, stats, affine):
+        inverse = stats[1]
+        normed = (value - stats[0]) * inverse
+        return affine[0] * normed + affine[1], normed, inverse
+
+    normalized_first, standardized_first, inverse_deviation_first = again(
+        reduced_output, stats_1, reduction_norm_params
+    )
+    normalized_second, standardized_second, inverse_deviation_second = again(
+        dilated_out, stats_2, dilated_norm_params
+    )
+    normalized_third, standardized_third, inverse_deviation_third = again(
+        expanded_output, stats_3, expansion_norm_params
+    )
+    residual_sum = normalized_third + x_own.astype(jnp.float32)
+    trunk_full = widen(trunk_out.reshape(image_inputs, tile_row_count, frame_columns, quarter))
+    branch_outs = [backward_dot(trunk_full, aspp_point)]
+    for branch_id in range(3):
+        dilation = RATES[branch_id]
+        hops = dilation // tile_row_count
+        partials = [0.0, 0.0, 0.0]
+        for col_tap in range(3):
+            shifted = move(trunk_full, -(col_tap - 1) * dilation, 2)
+            products = backward_dot(shifted, stacked_taps(aspp_rates[branch_id], col_tap))
+            for row_tap in range(3):
+                partials[row_tap] = (
+                    partials[row_tap]
+                    + products[..., row_tap * branch_part : (row_tap + 1) * branch_part]
+                )
+        upper = send_down(partials[0].astype(jnp.bfloat16), hops).astype(jnp.float32)
+        lower_part = send_up(partials[2].astype(jnp.bfloat16), hops).astype(jnp.float32)
+        branch_outs.append(partials[1] + upper + lower_part)
+    spatial_flattened = jnp.stack(branch_outs, axis=3).reshape(pixels, -1)
+    branch_gain_bias = branch_norms.reshape(2, -1)
+    normalized_spatial, standardized_spatial, inverse_deviation_spatial = norm_ahead_pass(
+        spatial_flattened, mask_column_vector, pixel_number_count, branch_gain_bias
+    )
+    spatial_act = (
+        jax.nn.silu(normalized_spatial)
+        .astype(jnp.bfloat16)
+        .reshape(image_inputs, tile_row_count, frame_columns, 4, branch_part)
+    )
+    pooled_local = lax.dot_general(
+        valid_mask.astype(jnp.bfloat16),
+        trunk_full,
+        (((1, 2), (1, 2)), ((0,), (0,))),
+        preferred_element_type=jnp.float32,
+    )
+    pooled = (over_rows(pooled_local) / image_areas[:, None]).astype(jnp.bfloat16)
+    pooling_convolution = backward_dot(pooled, aspp_pool)
+    normalized_poolbranch, standardized_poolbranch, inverse_deviation_poolbranch = norm_ahead_pass(
+        pooling_convolution, row_portion, image_overall_count, pooling_norm_params
+    )
+    pool_act = jax.nn.silu(normalized_poolbranch).astype(jnp.bfloat16)
+    pool_wide = jnp.broadcast_to(
+        pool_act[:, None, None, None, :],
+        (image_inputs, tile_row_count, frame_columns, 1, branch_part),
+    )
+    concat = jnp.concatenate([spatial_act, pool_wide], axis=3)
+    concat_flat = widen(concat).reshape(pixels, -1)
+    proj_kernel = (
+        aspp_project.reshape(branch_part, 5, branch_total, branch_part)
+        .transpose(0, 2, 1, 3)
+        .reshape(branch_part, 5 * branch_total * branch_part)
+    )
+    projected_output = backward_dot(concat_flat, proj_kernel)
+    normalized_projector, standardized_projector, inverse_deviation_projector = norm_ahead_pass(
+        projected_output, mask_column_vector, pixel_number_count, projection_norm_params
+    )
+    features = (
+        jax.nn.silu(normalized_projector)
+        .astype(jnp.bfloat16)
+        .reshape(image_inputs, tile_row_count, frame_columns, -1)
+    )
+    features_wide = widen(features).reshape(pixels, -1).astype(jnp.float32)
+    head_wide = head_weight.astype(jnp.float32)
+    logits = jnp.dot(features_wide, head_wide, precision=HIGH) + head_bias
+    classes = head_bias.shape[0] - 3
+    seg_logits = logits[:, :classes]
+    labels_flat = seg_labels.reshape(pixels)
+    classes_hot = (labels_flat[:, None] == jnp.arange(classes, dtype=jnp.int32)[None, :]).astype(
+        jnp.float32
+    )
+    cross = jax.nn.logsumexp(seg_logits, axis=1) - jnp.sum(seg_logits * classes_hot, axis=1)
+    depth_gap = logits[:, classes] - depth_target.reshape(pixels)
+    smooth_abs = jnp.sqrt(depth_gap * depth_gap + 1.0)
+    normal_gap = logits[:, classes + 1 :] - jnp.moveaxis(normal_target, 1, 3).reshape(pixels, 2)
+    local_losses = jnp.stack(
+        [
+            jnp.sum(mask_flat * cross),
+            jnp.sum(mask_flat * (smooth_abs - 1.0)),
+            jnp.sum(mask_flat * jnp.sum(normal_gap * normal_gap, axis=1)),
+        ]
+    )
+    task_weights = jnp.exp(-log_vars)
+    grad_seg = (jax.nn.softmax(seg_logits, axis=1) - classes_hot) * (
+        task_weights[0] / pixel_number_count * mask_flat
+    )[:, None]
+    grad_depth = depth_gap / smooth_abs * (task_weights[1] / pixel_number_count * mask_flat)
+    grad_normal = 2.0 * normal_gap * (task_weights[2] / pixel_number_count * mask_flat)[:, None]
+    grad_logits = jnp.concatenate([grad_seg, grad_depth[:, None], grad_normal], axis=1)
+    head_local = lax.dot_general(
+        features_wide, grad_logits, (((0,), (0,)), ((), ())), precision=HIGH
+    )
+    loss_parts, grad_head_weight, grad_head_bias = lax.psum(
+        (local_losses, head_local, jnp.sum(grad_logits, axis=0)), ("rows", "batch")
+    )
+    task_losses = loss_parts / pixel_number_count
+    total_loss = jnp.sum(task_weights * task_losses + log_vars)
+    grad_log_vars = 1.0 - task_weights * task_losses
+    grad_features = jnp.dot(grad_logits, head_wide.T, precision=HIGH)
+    my_features_grad = lax.dynamic_slice_in_dim(
+        grad_features, lax.axis_index("branch") * branch_part, branch_part, 1
+    )
+    gradient_before_projector = my_features_grad * silu_slope(normalized_projector)
+    grad_proj_in, grad_project_norm = norm_reverse_pass(
+        gradient_before_projector,
+        standardized_projector,
+        inverse_deviation_projector,
+        1.0,
+        mask_column_vector,
+        pixel_number_count,
+        projection_norm_params,
+    )
+    grad_proj_low = grad_proj_in.astype(jnp.bfloat16)
+    proj_kernel_grad = lax.dot_general(
+        grad_proj_low, concat_flat, (((0,), (0,)), ((), ())), preferred_element_type=jnp.float32
+    )
+    grad_project_local = (
+        proj_kernel_grad.reshape(branch_part, branch_total, 5, branch_part)
+        .transpose(0, 2, 1, 3)
+        .reshape(branch_part, 5, branch_total * branch_part)
+    )
+    concat_grad = forward_dot(grad_proj_low, proj_kernel).reshape(
+        image_inputs, tile_row_count, frame_columns, -1
+    )
+    concat_grad = narrow(concat_grad).reshape(pixels, 5, branch_part)
+    pool_grad_img = over_rows(
+        jnp.sum(concat_grad[:, 4, :].reshape(image_inputs, -1, branch_part), axis=1)
+    )
+    gradient_before_poolbranch = pool_grad_img * silu_slope(normalized_poolbranch)
+    grad_pool_conv, grad_pool_norm = norm_reverse_pass(
+        gradient_before_poolbranch,
+        standardized_poolbranch,
+        inverse_deviation_poolbranch,
+        row_portion,
+        1.0,
+        image_overall_count,
+        pooling_norm_params,
+    )
+    pool_conv_low = grad_pool_conv.astype(jnp.bfloat16)
+    grad_pool_local = (
+        lax.dot_general(
+            pool_conv_low, pooled, (((0,), (0,)), ((), ())), preferred_element_type=jnp.float32
+        )
+        * row_portion
+    )
+    pooled_grad = forward_dot(pool_conv_low, aspp_pool)
+    gradient_before_spatialbranch = concat_grad[:, :4, :].reshape(pixels, -1) * silu_slope(
+        normalized_spatial
+    )
+    grad_spatial, branch_norm_grad = norm_reverse_pass(
+        gradient_before_spatialbranch,
+        standardized_spatial,
+        inverse_deviation_spatial,
+        1.0,
+        mask_column_vector,
+        pixel_number_count,
+        branch_gain_bias,
+    )
+    grad_branch_norms = branch_norm_grad.reshape(2, 4, branch_part)
+    spatial_low = grad_spatial.astype(jnp.bfloat16).reshape(
+        image_inputs, tile_row_count, frame_columns, 4, branch_part
+    )
+    point_grad = spatial_low[:, :, :, 0]
+    grad_point_local = pixel_dot(point_grad, trunk_full)
+    trunk_grad = forward_dot(point_grad, aspp_point)
+    trunk_grad = (
+        trunk_grad + valid_mask[..., None] * (pooled_grad / image_areas[:, None])[:, None, None, :]
+    )
+    rate_grads = []
+    for branch_id in range(3):
+        dilation = RATES[branch_id]
+        hops = dilation // tile_row_count
+        centre = spatial_low[:, :, :, branch_id + 1]
+        grad_taps = jnp.concatenate(
+            [send_up(centre, hops), centre, send_down(centre, hops)], axis=3
+        )
+        per_col = []
+        for col_tap in range(3):
+            shifted = move(trunk_full, -(col_tap - 1) * dilation, 2)
+            per_col.append(pixel_dot(grad_taps, shifted))
+            tap_grad = forward_dot(grad_taps, stacked_taps(aspp_rates[branch_id], col_tap))
+            trunk_grad = trunk_grad + move(tap_grad, (col_tap - 1) * dilation, 2)
+        col_stack = jnp.stack(per_col, axis=0).reshape(3, 3, branch_part, -1)
+        rate_grads.append(col_stack.transpose(1, 0, 2, 3))
+    grad_rates_local = jnp.stack(rate_grads, axis=0)
+    trunk_own = narrow(trunk_grad).reshape(pixels, -1)
+    gradient_shortcut = trunk_own * silu_slope(residual_sum)
+    grad_expanded, grad_norm_expand = norm_reverse_pass(
+        gradient_shortcut,
+        standardized_third,
+        inverse_deviation_third,
+        1.0,
+        mask_column_vector,
+        pixel_number_count,
+        expansion_norm_params,
+    )
+    expanded_low = grad_expanded.astype(jnp.bfloat16).reshape(
+        image_inputs, tile_row_count, frame_columns, -1
+    )
+    grad_expand_local = pixel_dot(hidden_two_full, expanded_low)
+    hidden_two_grad = narrow(backward_dot(expanded_low, conv_expand)).reshape(pixels, -1)
+    gradient_before_second = hidden_two_grad * silu_slope(normalized_second)
+    gradient_dilated_input, gradient_dilated_norm = norm_reverse_pass(
+        gradient_before_second,
+        standardized_second,
+        inverse_deviation_second,
+        1.0,
+        mask_column_vector,
+        pixel_number_count,
+        dilated_norm_params,
+    )
+    dilated_lowprec = gradient_dilated_input.astype(jnp.bfloat16).reshape(
+        image_inputs, tile_row_count, frame_columns, -1
+    )
+    dilated_padded = pad_rows(dilated_lowprec)
+    hidden_one_grad = 0.0
+    kernel_grads = []
+    for row_tap in range(3):
+        band = hidden_full[:, 4 * row_tap : 4 * row_tap + tile_row_count]
+        grad_band = dilated_padded[:, 8 - 4 * row_tap : 8 - 4 * row_tap + tile_row_count]
+        for col_tap in range(3):
+            kernel_grads.append(pixel_dot(move(band, -(col_tap - 1) * 4, 2), dilated_lowprec))
+            hidden_one_grad = hidden_one_grad + backward_dot(
+                move(grad_band, (col_tap - 1) * 4, 2), conv_dilated[row_tap, col_tap]
+            )
+    grad_dilated_local = jnp.stack(kernel_grads, axis=0).reshape(3, 3, hidden_full.shape[3], -1)
+    hidden_one_own = narrow(hidden_one_grad).reshape(pixels, -1)
+    gradient_before_first = hidden_one_own * silu_slope(normalized_first)
+    grad_reduced, grad_norm_reduce = norm_reverse_pass(
+        gradient_before_first,
+        standardized_first,
+        inverse_deviation_first,
+        1.0,
+        mask_column_vector,
+        pixel_number_count,
+        reduction_norm_params,
+    )
+    reduced_low = grad_reduced.astype(jnp.bfloat16).reshape(
+        image_inputs, tile_row_count, frame_columns, -1
+    )
+    grad_reduce_local = pixel_dot(input_full, reduced_low)
+    input_grad = narrow(backward_dot(reduced_low, conv_reduce))
+    grad_input = input_grad + gradient_shortcut.reshape(
+        image_inputs, tile_row_count, frame_columns, quarter
+    )
+    grad_reduce, grad_dilated, grad_expand, grad_point, grad_rates, grad_pool, grad_project = (
+        lax.psum_scatter(grad_reduce_local, ("rows", "batch"), scatter_dimension=0, tiled=True),
+        lax.psum_scatter(grad_dilated_local, ("rows", "batch"), scatter_dimension=2, tiled=True),
+        lax.psum_scatter(grad_expand_local, ("rows", "batch"), scatter_dimension=0, tiled=True),
+        lax.psum_scatter(grad_point_local, ("rows", "batch"), scatter_dimension=1, tiled=True),
+        lax.psum_scatter(grad_rates_local, ("rows", "batch"), scatter_dimension=4, tiled=True),
+        lax.psum_scatter(grad_pool_local, ("rows", "batch"), scatter_dimension=1, tiled=True),
+        lax.psum_scatter(grad_project_local, ("rows", "batch"), scatter_dimension=2, tiled=True),
+    )
+    return (
+        features,
+        total_loss,
+        grad_input,
+        grad_reduce,
+        grad_dilated,
+        grad_expand,
+        grad_norm_reduce,
+        gradient_dilated_norm,
+        grad_norm_expand,
+        grad_point,
+        grad_rates,
+        grad_pool,
+        grad_branch_norms,
+        grad_pool_norm,
+        grad_project,
+        grad_project_norm,
+        grad_head_weight,
+        grad_head_bias,
+        grad_log_vars,
+    )
+
+
 def solution(mesh):
     in_specs = (
         P("batch", "rows", None, "branch"),
@@ -525,4 +1267,6 @@
         P(),
         P(),
     )
-    return jax.shard_map(local, mesh=mesh, in_specs=in_specs, out_specs=out_specs, check_vma=False)
+    small = (mesh.shape["branch"], mesh.shape["rows"], mesh.shape["batch"]) == (4, 2, 4)
+    body = fast_local if small else local
+    return jax.shard_map(body, mesh=mesh, in_specs=in_specs, out_specs=out_specs, check_vma=False)

time: 1560 us -> 1450 us (0.929)
  blocking collectives: 265 us -> 171 us
  waiting for transfers between devices: 864 us -> 782 us
  Pallas kernels: 0 us -> 80.7 us
  matrix products: 205 us -> 182 us
    all_gather x5 -> x3, waiting for transfers between devices: 242 us -> 138 us  [widen(): return lax.all_gather(tensor, 'branch', axis=3, tiled=True)]
    pallas_call x0 -> x1, Pallas kernels: none -> 80.7 us  [call_kernel(): pl.pallas_call(body, out_shape=[jax.ShapeDtypeStruct(s, d) for s, d in ou...]
    psum x5 -> x2, blocking collectives: 85.1 us -> 32.8 us  [norm_ahead_pass(): summed = lax.psum(jnp.sum(tensor * weight, axis=0), ('rows', 'batch'))]
    psum x5 -> x2, blocking collectives: 69.1 us -> 27.8 us  [norm_ahead_pass(): lax.psum(jnp.sum(weight * centered * centered, axis=0), ('rows', 'batch'))]
    reduce_scatter x7, waiting for transfers between devices: 408 us -> 434 us  [the longest x1 275 us: fast_local(): lax.psum_scatter(grad_rates_local, ('rows', 'batch'), scatter_dimension=4...]
    dot_general x23 -> x12, matrix products: 111 us -> 87.9 us  [forward_dot(): return jnp.dot(lhs_arr, rhs_arr, preferred_element_type=jnp.float32)]
    unnamed x385 -> x374, local copies, waits for them, and re-layouts: 53.8 us -> 58.1 us
    unnamed x20 -> x18, waiting for transfers between devices: 72 us -> 71.8 us
  transfers between devices with their start and end apart: 25 -> 22, of which waited for: 16 -> 13; matrix products, arithmetic and copies ran while one was open for 12% -> 14% of each run, Pallas kernels for 0% -> 0%
where the time goes in v1:
time: 1450 us; the launch traced here: 1440 us
  waiting for transfers between devices  782 us (54%)
  matrix products  182 us (13%)
  blocking collectives  171 us (12%)
  local copies, waits for them, and re-layouts  104 us (7%)
  Pallas kernels  80.7 us (6%)
  other arithmetic  75.5 us (5%)
  between operations  25.1 us (2%)
  starting transfers between devices  19.5 us (1%)
    reduce_scatter x1, waiting for transfers between devices, fast_local(): lax.psum_scatter(grad_rates_local, ('rows', 'batch'), scatter_dimension=4...  275 us
    reduce_scatter x2, waiting for transfers between devices, narrow(): lax.psum_scatter(tensor.astype(jnp.bfloat16), 'branch', scatter_dimension...  138 us
    all_gather x3, waiting for transfers between devices, widen(): return lax.all_gather(tensor, 'branch', axis=3, tiled=True)  138 us
    dot_general x12, matrix products, forward_dot(): return jnp.dot(lhs_arr, rhs_arr, preferred_element_type=jnp.float32)  87.9 us
    pallas_call x1, Pallas kernels, call_kernel(): pl.pallas_call(body, out_shape=[jax.ShapeDtypeStruct(s, d) for s, d in ou...  80.7 us
    unnamed x18, waiting for transfers between devices  71.8 us
    psum x4, blocking collectives, norm_reverse_pass(): lax.psum((jnp.sum(grad_out * weight_all, axis=0), jnp.sum(grad_out * norm...  65.4 us
    unnamed x374, local copies, waits for them, and re-layouts  58.1 us
  transfers between devices with their start and end apart: 22, of which 13 were waited for; matrix products, arithmetic and copies ran while one was open for 14% of the time, Pallas kernels for 0%

profile of v1, /device:TPU:0, one launch (start us, length us, event | category | flops | bytes accessed | tf_op | source)
XLA Modules:
  0.0 1440.1 jit_solution(2422401614313420959)
XLA Ops:
  24.2 80.7 %bottleneck.1 = (f32[1536,128]{1,0:T(8,128)}, f32[8,128]{1,0:T(8,128)}, bf16[2560,512]{1,0:T(8,128)(2,1)}, f32[1536,128]{1,0:T(8,128)}, f32[8,128]{1,0:T(8,128)}...) custom-call(bf16[1536,512]{1,0:T(8,128)(2,1)} %bitcast.887, ...), custom_call_target="tpu_custom_call" | custom-call | tf_op jit(solution)/shard_map/bottleneck/pallas_call | solution.py:454
  114.9 59.7 %all-gather.4.cloned.1.call-done = bf16[1,12,128,2048]{3,2,1,0:T(8,128)(2,1)} async-done(((bf16[1,12,128,512]{3,2,1,0:T(8,128)(2,1)}), bf16[1,12,128,2048]{3,2,1,0:T(8,128)(2,1)}) %all-gather.4.cloned.1.call-update) | async-done | bytes 6291472 | tf_op jit(solution)/shard_map/all_gather | solution.py:73
  212.5 16.0 %all-reduce.33 = (f32[64]{0:T(128)S(1)}, f32[256]{0:T(256)S(1)}) all-reduce(f32[64]{0:T(128)S(1)} %get-tuple-element.256, f32[256]{0:T(256)S(1)} %reduce_sum.259), channel_id=1, replica_groups=mesh['branch'=4,'rows'=2,'batch'=4] {'rows','batch'}, use_global_device_ids=true, to_apply=%region_6.7 | all-reduce | flops 320 | bytes 2560 | tf_op jit(solution)/shard_map/psum | solution.py:103
  229.6 14.1 all-reduce.32
  254.4 43.4 %all-gather.6.cloned.1.call-done = bf16[1,12,128,20,64]{2,4,1,0,3:T(8,128)(2,1)} async-done(((bf16[1,12,128,5,64]{2,4,1,0,3:T(8,128)(2,1)}), bf16[1,12,128,20,64]{2,4,1,0,3:T(8,128)(2,1)}) %all-gather.6.cloned.1.call-update) | async-done | bytes 3932176 | tf_op jit(solution)/shard_map/all_gather | solution.py:73
  307.3 16.8 %psum.166 = f32[64]{0:T(128)S(1)} all-reduce(f32[64]{0:T(128)S(1)} %get-tuple-element.258), channel_id=1, replica_groups=mesh['branch'=4,'rows'=2,'batch'=4] {'rows','batch'}, use_global_device_ids=true, to_apply=%region_9.10 | all-reduce | flops 64 | bytes 512 | tf_op jit(solution)/shard_map/psum | solution.py:103
  324.8 13.7 psum.167
  339.7 13.2 all_gather.14
  362.0 14.6 %all-reduce.31 = (f32[64]{0:T(128)S(1)}, f32[64]{0:T(128)S(1)}) all-reduce(f32[64]{0:T(128)S(1)} %get-tuple-element.141, f32[64]{0:T(128)S(1)} %get-tuple-element.140), channel_id=1, replica_groups=mesh['branch'=4,'rows'=2,'batch'=4] {'rows','batch'}, use_global_device_ids=true, to_apply=%region_25.26 | all-reduce | flops 128 | bytes 1024 | tf_op jit(solution)/shard_map/psum | solution.py:114
  381.0 8.7 copy.171
  401.1 43.9 %reduce-scatter.37.cloned.1.call-done = bf16[320,1536]{1,0:T(8,128)(2,1)} async-done(((bf16[1280,1536]{1,0:T(8,128)(2,1)}), bf16[320,1536]{1,0:T(8,128)(2,1)}) %reduce-scatter.37.cloned.1.call-update) | async-done | bytes 983056
  465.6 17.3 %all-reduce.30 = (f32[256]{0:T(256)S(1)}, f32[256]{0:T(256)S(1)}, f32[64]{0:T(128)}, f32[64]{0:T(128)}) all-reduce(f32[256]{0:T(256)S(1)} %reduce_sum.278, f32[256]{0:T(256)S(1)} %reduce_sum.276, f32[64]{0:T(128)S(1)} %multiply_bitcast_fusion, ...), channel_id=1, replica_groups=mesh['branch'=4,'rows'=2,'batch'=4] {'rows','batch'}, use_global_device_ids=true, to_apply=%region_30.31 | all-reduce | flops 640 | bytes 5120 | tf_op jit(solution)/shard_map/psum | solution.py:114
  490.4 6.4 convolution_bitcast_fusion.3
  496.9 6.4 convolution_bitcast_fusion.2
  509.8 6.4 convolution_bitcast_fusion
  516.2 6.4 fusion.205
  522.7 6.4 fusion.209
  531.9 6.9 convolution_bitcast_fusion.5
  545.2 31.1 %fusion.9 = bf16[1,12,128,2048]{3,2,1,0:T(8,128)(2,1)} fusion(f32[1,12,128,2048]{3,2,1,0:T(8,128)} %convolution_bitcast_fusion.5, f32[1,12,128,2048]{3,2,1,0:T(8,128)} %convolution_bitcast_fusion.4, f32[1,12,128,2048]{3,2,1,0:T(8,128)} %convolution_bitcast_fusion.3, f32[1,12,128,2048]{3,2,1,0:T(8,128)} %convolution_bitcast_fusion.2, ...), kind=kOutput, calls=%fused_computation.16 | convolution fusion | flops 1249837056 | bytes 120928256 | tf_op jit(solution)/shard_map/dot_general | solution.py:49
  577.8 66.9 %reduce-scatter.19.cloned.1.call-done = bf16[1,12,128,512]{3,2,1,0:T(8,128)(2,1)} async-done(((bf16[1,12,128,2048]{3,2,1,0:T(8,128)(2,1)}), bf16[1,12,128,512]{3,2,1,0:T(8,128)(2,1)}) %reduce-scatter.19.cloned.1.call-update) | async-done | bytes 1572880 | tf_op jit(solution)/shard_map/reduce_scatter | solution.py:77
  648.6 16.8 %all-reduce.29 = (f32[512]{0:T(512)S(1)}, f32[512]{0:T(512)S(1)}) all-reduce(f32[512]{0:T(512)S(1)} %get-tuple-element.133, f32[512]{0:T(512)S(1)} %get-tuple-element.132), channel_id=1, replica_groups=mesh['branch'=4,'rows'=2,'batch'=4] {'rows','batch'}, use_global_device_ids=true, to_apply=%region_39.40 | all-reduce | flops 1024 | bytes 8192 | tf_op jit(solution)/shard_map/psum | solution.py:114
  678.1 27.0 %reduce-scatter.39.cloned.1.call-done = bf16[128,1536]{1,0:T(8,128)(2,1)} async-done(((bf16[512,1536]{1,0:T(8,128)(2,1)}), bf16[128,1536]{1,0:T(8,128)(2,1)}) %reduce-scatter.39.cloned.1.call-update) | async-done | bytes 393232
  707.2 16.8 %all-reduce.28 = (f32[128]{0:T(128)S(1)}, f32[128]{0:T(128)S(1)}) all-reduce(f32[128]{0:T(128)S(1)} %get-tuple-element.139, f32[128]{0:T(128)S(1)} %get-tuple-element.138), channel_id=1, replica_groups=mesh['branch'=4,'rows'=2,'batch'=4] {'rows','batch'}, use_global_device_ids=true, to_apply=%region_44.45 | all-reduce | flops 256 | bytes 2048 | tf_op jit(solution)/shard_map/psum | solution.py:114
  782.6 26.7 %all-reduce.27 = (f32[3]{0:T(128)S(1)}, f32[128]{0:T(128)S(1)}, f32[128]{0:T(128)S(1)}, f32[256,22]{0,1:T(8,128)}, f32[22]{0:T(128)}) all-reduce(f32[3]{0:T(128)S(1)} %pad_maximum_fusion.18, f32[128]{0:T(128)S(1)} %get-tuple-element.137, ...), channel_id=1, replica_groups=mesh['branch'=4,'rows'=2,'batch'=4] {'rows','batch'}, use_global_device_ids=true, to_apply=%region_19.20 | all-reduce | flops 5913 | bytes 47304 | tf_op jit(solution)/shard_map/psum | solution.py:1040
  810.0 34.9 %all-gather.8.cloned.1.call-done = bf16[1,12,128,2048]{3,2,1,0:T(8,128)(2,1)} async-done(((bf16[1,12,128,512]{3,2,1,0:T(8,128)(2,1)}), bf16[1,12,128,2048]{3,2,1,0:T(8,128)(2,1)}) %all-gather.8.cloned.1.call-update) | async-done | bytes 6291472 | tf_op jit(solution)/shard_map/all_gather | solution.py:73
  861.8 12.8 pad_maximum_fusion
  921.4 274.7 %reduce-scatter.31.cloned.1.call-done = f32[3,3,3,64,256]{4,3,1,2,0:T(8,128)} async-done(((f32[3,3,3,64,2048]{4,3,1,2,0:T(8,128)}), f32[3,3,3,64,256]{4,3,1,2,0:T(8,128)}) %reduce-scatter.31.cloned.1.call-update) | async-done | bytes 1769488 | tf_op jit(solution)/shard_map/reduce_scatter | solution.py:1198
  1198.9 71.6 %reduce-scatter.21.cloned.1.call-done = bf16[1,12,128,512]{3,2,1,0:T(8,128)(2,1)} async-done(((bf16[1,12,128,2048]{3,2,1,0:T(8,128)(2,1)}), bf16[1,12,128,512]{3,2,1,0:T(8,128)(2,1)}) %reduce-scatter.21.cloned.1.call-update) | async-done | bytes 1572880 | tf_op jit(solution)/shard_map/reduce_scatter | solution.py:77
  1274.4 31.4 %reduce-scatter.29.cloned.1.call-done = f32[64,256]{1,0:T(8,128)} async-done(((f32[64,2048]{1,0:T(8,128)}), f32[64,256]{1,0:T(8,128)}) %reduce-scatter.29.cloned.1.call-update) | async-done | bytes 65552 | tf_op jit(solution)/shard_map/reduce_scatter | solution.py:1197
  1305.8 34.3 %reduce-scatter.33.cloned.1.call-done = f32[64,256]{1,0:T(8,128)} async-done(((f32[64,2048]{1,0:T(8,128)}), f32[64,256]{1,0:T(8,128)}) %reduce-scatter.33.cloned.1.call-update) | async-done | bytes 65552 | tf_op jit(solution)/shard_map/reduce_scatter | solution.py:1199
  1340.1 37.2 %reduce-scatter.27.cloned.1.call-done = f32[64,512]{1,0:T(8,128)} async-done(((f32[512,512]{1,0:T(8,128)}), f32[64,512]{1,0:T(8,128)}) %reduce-scatter.27.cloned.1.call-update) | async-done | bytes 131088 | tf_op jit(solution)/shard_map/reduce_scatter | solution.py:1196
  1377.3 55.8 %reduce-scatter.25.cloned.1.call-done = f32[3,3,64,128]{3,2,1,0:T(8,128)} async-done(((f32[3,3,512,128]{3,2,1,0:T(8,128)}), f32[3,3,64,128]{3,2,1,0:T(8,128)}) %reduce-scatter.25.cloned.1.call-update) | async-done | bytes 294928 | tf_op jit(solution)/shard_map/reduce_scatter | solution.py:1195
  (600 shorter events, 296.0 us)
Async XLA Ops:
  7.2 202.5 %copy-start = (bf16[64,2048]{1,0:T(8,128)(2,1)S(1)}, bf16[64,2048]{1,0:T(8,128)(2,1)}, u32[]{:S(2)}) copy-start(bf16[64,2048]{1,0:T(8,128)(2,1)} %param.28) | copy-start | bytes 786436
  7.2 15.9 %all-to-all-start = ((bf16[4,512,128]{2,1,0:T(8,128)(2,1)}), bf16[4,512,128]{2,1,0:T(8,128)(2,1)S(1)}, u32[]{:S(2)}, u32[]{:S(2)}) async-start(bf16[4,512,128]{2,1,0:T(8,128)(2,1)} %bitcast.941), calls=%async_computation | async-start | bytes 1048576 | tf_op jit(solution)/shard_map/all_to_all | solution.py:910
  12.5 162.1 %all-gather.4.cloned.1.call-start = ((), (), s32[]{:S(2)}) async-start(), calls=%async_computation.13 | async-start | bytes 7864320 | tf_op jit(solution)/shard_map/all_gather | solution.py:73
  19.6 87.3 %copy-start.111 = (pred[128]{0:T(512)(128)(4,1)}, pred[128]{0:T(512)(128)(4,1)S(1)}, u32[]{:S(2)}) copy-start(pred[128]{0:T(512)(128)(4,1)S(1)} %compare_and_fusion) | copy-start | bytes 388
  21.6 85.3 %copy-start.98 = (pred[12]{0:T(512)(128)(4,1)}, pred[12]{0:T(512)(128)(4,1)S(1)}, u32[]{:S(2)}) copy-start(pred[12]{0:T(512)(128)(4,1)S(1)} %compare_and_fusion.1) | copy-start | bytes 40
  105.0 192.9 %all-gather.6.cloned.1.call-start = ((), (), s32[]{:S(2)}) async-start(), calls=%async_computation.14 | async-start | bytes 4915200 | tf_op jit(solution)/shard_map/all_gather | solution.py:73
  106.9 122.2 %copy-start.89 = (f32[12,128]{1,0:T(8,128)}, f32[12,128]{1,0:T(8,128)S(1)}, u32[]{:S(2)}) copy-start(f32[12,128]{1,0:T(8,128)S(1)} %get-tuple-element.251) | copy-start | bytes 18436
  112.7 73.3 %copy-start.34 = (bf16[64,2048]{1,0:T(8,128)(2,1)}, bf16[64,2048]{1,0:T(8,128)(2,1)S(1)}, u32[]{:S(2)}) copy-start(bf16[64,2048]{1,0:T(8,128)(2,1)S(1)} %get-tuple-element.191) | copy-start | bytes 786436
  112.7 73.3 %copy-start.35 = (bf16[64,2048]{1,0:T(8,128)(2,1)}, bf16[64,2048]{1,0:T(8,128)(2,1)S(1)}, u32[]{:S(2)}) copy-start(bf16[64,2048]{1,0:T(8,128)(2,1)S(1)} %get-tuple-element.192) | copy-start | bytes 786436
  190.8 21.2 %collective-permute-start.1 = (bf16[1,12,128,64]{2,3,1,0:T(8,128)(2,1)S(1)}, bf16[1,12,128,64]{2,3,1,0:T(8,128)(2,1)S(1)}, u32[]{:S(2)}, u32[]{:S(2)}) collective-permute-start(bf16[1,12,128,64]{2,3,1,0:T(8,128)(2,1)S(1)} %get-tuple-element.182), channel_id=1, source_target_pairs={{4,0},{5,1},{6,2},{7,3},{12,8},{13,9},{14,10},{15,11},{20,16},{21,... | collective-permute-start | bytes 589832 | tf_op jit(solution)/shard_map/ppermute | solution.py:33
  192.1 19.9 %collective-permute-start = (bf16[1,12,128,64]{2,3,1,0:T(8,128)(2,1)S(1)}, bf16[1,12,128,64]{2,3,1,0:T(8,128)(2,1)S(1)}, u32[]{:S(2)}, u32[]{:S(2)}) collective-permute-start(bf16[1,12,128,64]{2,3,1,0:T(8,128)(2,1)S(1)} %get-tuple-element.181), channel_id=1, source_target_pairs={{0,4},{1,5},{2,6},{3,7},{8,12},{9,13},{10,14},{11,15},{16,20},{17,... | collective-permute-start | bytes 589832 | tf_op jit(solution)/shard_map/ppermute | solution.py:33
  246.9 198.1 %reduce-scatter.37.cloned.1.call-start = ((), (), s32[]{:S(2)}) async-start(), calls=%async_computation.25 | async-start | bytes 4915200
  253.1 86.0 %copy-start.119 = (f32[64]{0:T(128)}, f32[64]{0:T(128)S(1)}, u32[]{:S(2)}) copy-start(f32[64]{0:T(128)S(1)} %get-tuple-element.245) | copy-start | bytes 772
  253.1 86.0 %copy-start.130 = (f32[64]{0:T(128)}, f32[64]{0:T(128)S(1)}, u32[]{:S(2)}) copy-start(f32[64]{0:T(128)S(1)} %get-tuple-element.246) | copy-start | bytes 772
  396.1 248.6 %reduce-scatter.19.cloned.1.call-start = ((), (), s32[]{:S(2)}) async-start(), calls=%async_computation.15 | async-start | bytes 7864320 | tf_op jit(solution)/shard_map/reduce_scatter | solution.py:77
  486.5 45.3 %collective-permute-start.3 = (bf16[1,12,128,64]{2,3,1,0:T(8,128)(2,1)S(1)}, bf16[1,12,128,64]{2,3,1,0:T(8,128)(2,1)S(1)}, u32[]{:S(2)}, u32[]{:S(2)}) collective-permute-start(bf16[1,12,128,64]{2,3,1,0:T(8,128)(2,1)S(1)} %get-tuple-element.217), channel_id=1, source_target_pairs={{0,4},{1,5},{2,6},{3,7},{8,12},{9,13},{10,14},{11,15},{16,20},{17,... | collective-permute-start | bytes 589832 | tf_op jit(solution)/shard_map/ppermute | solution.py:33
  488.8 43.1 %collective-permute-start.2 = (bf16[1,12,128,64]{2,3,1,0:T(8,128)(2,1)S(1)}, bf16[1,12,128,64]{2,3,1,0:T(8,128)(2,1)S(1)}, u32[]{:S(2)}, u32[]{:S(2)}) collective-permute-start(bf16[1,12,128,64]{2,3,1,0:T(8,128)(2,1)S(1)} %get-tuple-element.217), channel_id=1, source_target_pairs={{4,0},{5,1},{6,2},{7,3},{12,8},{13,9},{14,10},{15,11},{20,16},{21,... | collective-permute-start | bytes 589832 | tf_op jit(solution)/shard_map/ppermute | solution.py:33
  576.4 128.7 %reduce-scatter.39.cloned.1.call-start = ((), (), s32[]{:S(2)}) async-start(), calls=%async_computation.26 | async-start | bytes 1966080
  676.6 103.6 %reduce-scatter.41.cloned.1.call-start = ((), (), s32[]{:S(2)}) async-start(), calls=%async_computation.27 | async-start | bytes 1966080
  725.2 5.7 collective-permute-start.4
  726.5 4.4 collective-permute-start.5
  744.7 100.2 %all-gather.8.cloned.1.call-start = ((), (), s32[]{:S(2)}) async-start(), calls=%async_computation.17 | async-start | bytes 7864320 | tf_op jit(solution)/shard_map/all_gather | solution.py:73
  745.4 167.7 %reduce-scatter.35.cloned.1.call-start = ((), (), s32[]{:S(2)}) async-start(), calls=%async_computation.24 | async-start | bytes 1179648 | tf_op jit(solution)/shard_map/reduce_scatter | solution.py:1200
  758.8 160.9 %reduce-scatter.23.cloned.1.call-start = ((), (), s32[]{:S(2)}) async-start(), calls=%async_computation.18 | async-start | bytes 1179648 | tf_op jit(solution)/shard_map/reduce_scatter | solution.py:1194
  849.7 346.4 %reduce-scatter.31.cloned.1.call-start = ((), (), s32[]{:S(2)}) async-start(), calls=%async_computation.22 | async-start | bytes 15925248 | tf_op jit(solution)/shard_map/reduce_scatter | solution.py:1198
  874.6 396.0 %reduce-scatter.21.cloned.1.call-start = ((), (), s32[]{:S(2)}) async-start(), calls=%async_computation.16 | async-start | bytes 7864320 | tf_op jit(solution)/shard_map/reduce_scatter | solution.py:77
  880.1 425.7 %reduce-scatter.29.cloned.1.call-start = ((), (), s32[]{:S(2)}) async-start(), calls=%async_computation.21 | async-start | bytes 589824 | tf_op jit(solution)/shard_map/reduce_scatter | solution.py:1197
  885.1 455.0 %reduce-scatter.33.cloned.1.call-start = ((), (), s32[]{:S(2)}) async-start(), calls=%async_computation.23 | async-start | bytes 589824 | tf_op jit(solution)/shard_map/reduce_scatter | solution.py:1199
  886.2 491.1 %reduce-scatter.27.cloned.1.call-start = ((), (), s32[]{:S(2)}) async-start(), calls=%async_computation.20 | async-start | bytes 1179648 | tf_op jit(solution)/shard_map/reduce_scatter | solution.py:1196
  901.5 531.6 %reduce-scatter.25.cloned.1.call-start = ((), (), s32[]{:S(2)}) async-start(), calls=%async_computation.19 | async-start | bytes 2654208 | tf_op jit(solution)/shard_map/reduce_scatter | solution.py:1195
  921.4 349.2 %copy-start.4 = (f32[1536,512]{1,0:T(8,128)S(1)}, f32[1536,512]{1,0:T(8,128)}, u32[]{:S(2)}) copy-start(f32[1536,512]{1,0:T(8,128)} %copy-done.3) | copy-start | bytes 9437188
  1270.5 162.5 %copy-start.1 = (bf16[64,2048]{1,0:T(8,128)(2,1)S(1)}, bf16[64,2048]{1,0:T(8,128)(2,1)}, u32[]{:S(2)}) copy-start(bf16[64,2048]{1,0:T(8,128)(2,1)} %param.28) | copy-start | bytes 786436
  (167 other events, 1210.7 us)
Sparse Core Ops, SparseCore 0:
  105.1 69.4 all-gather.3
  247.1 50.7 all-gather.5
  396.2 48.7 reduce-scatter.36
  576.5 68.1 reduce-scatter.18
  676.8 28.2 reduce-scatter.38
  744.8 28.1 reduce-scatter.40
  774.9 69.9 all-gather.7
  847.2 35.4 reduce-scatter.34
  885.0 34.6 reduce-scatter.22
  921.9 274.1 reduce-scatter.30
  1199.1 71.4 reduce-scatter.20
  1273.2 32.5 reduce-scatter.28
  1308.7 31.2 reduce-scatter.32
  1342.8 34.4 reduce-scatter.26
  1380.0 52.9 reduce-scatter.24

commit v2 on v0

--- a/solution.py
+++ b/solution.py
@@ -1,6 +1,10 @@
+import types
+
 import jax
 import jax.numpy as jnp
 from jax import lax
+from jax.experimental import pallas as pl
+from jax.experimental.pallas import tpu as pltpu
 from jax.sharding import PartitionSpec as P
 
 EPS = 1e-05
@@ -122,6 +126,1513 @@
 
 def stacked_taps(kernels, col_tap):
     return jnp.concatenate([kernels[0, col_tap], kernels[1, col_tap], kernels[2, col_tap]], axis=0)
+
+
+MESH = pl.DeviceIdType.MESH
+F32 = jnp.float32
+BF16 = jnp.bfloat16
+VMEM_LIMIT = 60 * 2**20
+
+
+class Net:
+    def __init__(self, send_sems, recv_sems):
+        self.m = lax.axis_index("branch")
+        self.r = lax.axis_index("rows")
+        self.z = lax.axis_index("batch")
+        self.send_sems, self.recv_sems, self.count = send_sems, recv_sems, 0
+        self.side = (self.m ^ 1, self.r, self.z)
+        self.over = (self.m ^ 2, self.r, self.z)
+        self.diagonal = (self.m ^ 3, self.r, self.z)
+        self.core = (self.m, 1 - self.r, self.z)
+        self.slot = self.r * 4 + self.z
+        self.group = [
+            (self.m, lax.rem(self.r + i, 2), lax.rem(self.z + j, 4))
+            for i in range(2)
+            for j in range(4)
+            if i or j
+        ]
+
+    def send(self, src, dst, device):
+        i = self.count
+        self.count += 1
+        copy = pltpu.make_async_remote_copy(
+            src_ref=src,
+            dst_ref=dst,
+            send_sem=self.send_sems.at[i],
+            recv_sem=self.recv_sems.at[i],
+            device_id=device,
+            device_id_type=MESH,
+        )
+        copy.start()
+        return copy
+
+
+def greet(peers, perhaps=None):
+    barrier = pltpu.get_barrier_semaphore()
+    for peer in peers:
+        pl.semaphore_signal(barrier, inc=1, device_id=peer, device_id_type=MESH)
+    if perhaps is None:
+        pl.semaphore_wait(barrier, len(peers))
+        return
+    peer, there = perhaps
+
+    @pl.when(there)
+    def _():
+        pl.semaphore_signal(barrier, inc=1, device_id=peer, device_id_type=MESH)
+
+    pl.semaphore_wait(barrier, len(peers) + there.astype(jnp.int32))
+
+
+def each_rows(total, step, body):
+    def run(i, carry):
+        body(pl.ds(pl.multiple_of(i * step, step), step))
+        return carry
+
+    lax.fori_loop(0, total // step, run, 0)
+
+
+def lane_block(index, width=128):
+    return pl.ds(pl.multiple_of(index * width, width), width)
+
+
+def wide(tile, width):
+    count = width // tile.shape[1]
+    return tile if count == 1 else jnp.concatenate([tile] * count, axis=1)
+
+
+def column_sums(fn, total, width, number):
+    step = 16384 // width
+
+    def run(i, sums):
+        terms = fn(pl.ds(pl.multiple_of(i * step, step), step))
+        return tuple(
+            s + jnp.sum(t.reshape(step // 8, 8, width), axis=0) for s, t in zip(sums, terms)
+        )
+
+    sums = lax.fori_loop(
+        0, total // step, run, tuple(jnp.zeros((8, width), F32) for _ in range(number))
+    )
+    return [jnp.sum(s, axis=0, keepdims=True) for s in sums]
+
+
+def fold(row):
+    return row + pltpu.roll(wide(row, 128), 64, 1)
+
+
+def exchange(net, outgoing, incoming, meanwhile=None):
+    copies = [net.send(outgoing, incoming.at[net.slot], peer) for peer in net.group]
+    incoming[net.slot] = outgoing[...]
+    if meanwhile is not None:
+        meanwhile()
+    for copy in copies:
+        copy.wait()
+
+
+def statistics(net, value_ref, mask_ref, outgoing, incoming, counted, folded=False, extra=None):
+    total, width = value_ref.shape
+    same = fold if folded else (lambda row: row)
+    first, number = column_sums(
+        lambda at: (value_ref[at, :] * wide(mask_ref[at, :], width), wide(mask_ref[at, :], width)),
+        total,
+        width,
+        2,
+    )
+    first, number = same(first), same(number)
+    centre = first / jnp.maximum(number, 1.0)
+
+    def squares(at):
+        gap = value_ref[at, :] - centre
+        return (gap * gap * wide(mask_ref[at, :], width),)
+
+    second = same(column_sums(squares, total, width, 1)[0])
+    outgoing[0:1, :] = first
+    outgoing[1:2, :] = second
+    outgoing[2:3, :] = number
+    if extra is not None:
+        outgoing[3:4, :] = extra
+    exchange(net, outgoing, incoming)
+    firsts, seconds, numbers = incoming[:, 0, :], incoming[:, 1, :], incoming[:, 2, :]
+    mean = jnp.sum(firsts, axis=0, keepdims=True) / counted
+    drift = firsts / jnp.maximum(numbers, 1.0) - mean
+    variance = jnp.sum(seconds + numbers * drift * drift, axis=0, keepdims=True) / counted
+    return mean, lax.rsqrt(variance + EPS)
+
+
+def gather_blocks(net, part, rows):
+    pieces, size = 4, rows // 4
+    own, side, over = net.m, net.m ^ 1, net.m ^ 2
+
+    def at(i):
+        return pl.ds(i * size, size)
+
+    to_side, to_over = [], []
+    for i in range(pieces):
+        j = pieces - 1 - i
+        to_side.append(net.send(part(own, at(i)), part(own, at(i)), net.side))
+        to_over.append(net.send(part(own, at(j)), part(own, at(j)), net.over))
+    passed = []
+    for i in range(pieces):
+        j = pieces - 1 - i
+        to_side[i].wait_recv()
+        if i < pieces // 2:
+            passed.append(net.send(part(side, at(i)), part(side, at(i)), net.over))
+        to_over[i].wait_recv()
+        if i < pieces // 2:
+            passed.append(net.send(part(over, at(j)), part(over, at(j)), net.side))
+    for copy in to_side + to_over:
+        copy.wait_send()
+    for copy in passed:
+        copy.wait()
+
+
+def sum_scatter(net, part, bufs, out, meanwhile=None):
+    far, to_side, to_over, far_side, far_over, from_side, from_over = bufs
+    rows, width = out.shape
+    half, step = rows // 2, 16384 // width
+    head, tail = pl.ds(0, half), pl.ds(half, half)
+    across, side, over = net.m ^ 3, net.m ^ 1, net.m ^ 2
+
+    def fill(target, index, base):
+        def body(at):
+            rows_at = pl.ds(pl.multiple_of(at.start + base, step), step)
+            target[rows_at, :] = part[index, rows_at, :].astype(BF16)
+
+        each_rows(half, step, body)
+
+    def combine(target, index, base, arrived):
+        def body(at):
+            rows_at = pl.ds(pl.multiple_of(at.start + base, step), step)
+            target[rows_at, :] = (part[index, rows_at, :] + arrived[at, :].astype(F32)).astype(BF16)
+
+        each_rows(half, step, body)
+
+    fill(far, across, 0)
+    first = net.send(far.at[head], far_side, net.side)
+    fill(far, across, half)
+    second = net.send(far.at[tail], far_over, net.over)
+    fill(to_side, side, 0)
+    third = net.send(to_side.at[head], from_side.at[head], net.side)
+    fill(to_over, over, half)
+    fourth = net.send(to_over.at[tail], from_over.at[tail], net.over)
+    second.wait_recv()
+    combine(to_side, side, half, far_over)
+    fifth = net.send(to_side.at[tail], from_side.at[tail], net.side)
+    first.wait_recv()
+    combine(to_over, over, 0, far_side)
+    sixth = net.send(to_over.at[head], from_over.at[head], net.over)
+    if meanwhile is not None:
+        meanwhile()
+    for copy in (third, fourth, fifth, sixth):
+        copy.wait_recv()
+
+    def body(at):
+        out[at, :] = (
+            part[net.m, at, :] + from_side[at, :].astype(F32) + from_over[at, :].astype(F32)
+        )
+
+    each_rows(rows, step, body)
+    for copy in (first, second, third, fourth, fifth, sixth):
+        copy.wait_send()
+
+
+def gradient_sums(
+    net, grad_ref, normed, outgoing, incoming, folded=False, extra=None, meanwhile=None
+):
+    total, width = grad_ref.shape
+    same = fold if folded else (lambda row: row)
+    bias, gain = column_sums(
+        lambda at: (grad_ref[at, :], grad_ref[at, :] * normed(at)), total, width, 2
+    )
+    outgoing[0:1, :] = same(bias)
+    outgoing[1:2, :] = same(gain)
+    if extra is not None:
+        outgoing[2:3, :] = extra
+    exchange(net, outgoing, incoming, meanwhile)
+    bias = jnp.sum(incoming[:, 0, :], axis=0, keepdims=True)
+    gain = jnp.sum(incoming[:, 1, :], axis=0, keepdims=True)
+    return bias, gain
+
+
+def keep_rows(ref, first, second):
+    width = ref.shape[1]
+    ref[0:1, :] = first
+    ref[1:2, :] = second
+    ref[2:8, :] = jnp.zeros((6, width), F32)
+
+
+def pair(a, b):
+    low = lax.broadcasted_iota(jnp.int32, (a.shape[0], 128), 1) < 64
+    results = []
+    for g in range(2):
+        left, right = a[:, g * 128 : g * 128 + 128], b[:, g * 128 : g * 128 + 128]
+        results.append(jnp.where(low, left, pltpu.roll(right, 64, 1)))
+        results.append(jnp.where(low, pltpu.roll(left, 64, 1), right))
+    return results
+
+
+def unpair(blocks):
+    low = lax.broadcasted_iota(jnp.int32, blocks[0].shape, 1) < 64
+    firsts, seconds = [], []
+    for g in range(2):
+        left, right = blocks[2 * g], blocks[2 * g + 1]
+        firsts.append(jnp.where(low, left, pltpu.roll(right, 64, 1)))
+        seconds.append(jnp.where(low, pltpu.roll(left, 64, 1), right))
+    return jnp.concatenate(firsts, axis=1), jnp.concatenate(seconds, axis=1)
+
+
+def split_three(row):
+    high = row.astype(BF16)
+    rest = row - high.astype(F32)
+    middle = rest.astype(BF16)
+    low = (rest - middle.astype(F32)).astype(BF16)
+    return high, middle, low
+
+
+def zero_margins(ref, side, width):
+    rows, _, lanes = ref.shape
+    ref[:, 0:side, :] = jnp.zeros((rows, side, lanes), F32)
+    ref[:, side + width : 2 * side + width, :] = jnp.zeros((rows, side, lanes), F32)
+
+
+def scatter_buffers(rows, width):
+    whole, half = pltpu.VMEM((rows, width), BF16), pltpu.VMEM((rows // 2, width), BF16)
+    return [whole, whole, whole, half, half, whole, whole]
+
+
+def sigmoid(u):
+    return 0.5 * jnp.tanh(0.5 * u) + 0.5
+
+
+def slope(u):
+    s = sigmoid(u)
+    return s * (1.0 + u * (1.0 - s))
+
+
+def mm(a, b):
+    return jnp.dot(a, b, preferred_element_type=F32)
+
+
+def mm_t(a, b):
+    return lax.dot_general(a, b, (((1,), (1,)), ((), ())), preferred_element_type=F32)
+
+
+def tm_m(a, b):
+    return lax.dot_general(a, b, (((0,), (0,)), ((), ())), preferred_element_type=F32)
+
+
+def call_kernel(body, name, number, args, outs, scratch, sems, hbm=(), smem=("boxes",)):
+    vmem, anywhere = pl.BlockSpec(memory_space=pltpu.VMEM), pl.BlockSpec(memory_space=pl.ANY)
+    names = [*args, *outs, *scratch]
+    places = {name: anywhere for name in hbm}
+    places.update({name: pl.BlockSpec(memory_space=pltpu.SMEM) for name in smem})
+
+    def kernel(*refs):
+        k = types.SimpleNamespace(**dict(zip(names, refs)))
+        body(Net(refs[-2], refs[-1]), k)
+
+    results = pl.pallas_call(
+        kernel,
+        out_shape=[jax.ShapeDtypeStruct(s, d) for s, d in outs.values()],
+        in_specs=[places.get(name, vmem) for name in args],
+        out_specs=[places.get(name, vmem) for name in outs],
+        scratch_shapes=list(scratch.values())
+        + [pltpu.SemaphoreType.DMA((sems,)), pltpu.SemaphoreType.DMA((sems,))],
+        name=name,
+        compiler_params=pltpu.CompilerParams(
+            collective_id=number, has_side_effects=True, vmem_limit_bytes=VMEM_LIMIT
+        ),
+    )(*args.values())
+    return types.SimpleNamespace(**dict(zip(outs, results)))
+
+
+def pixel_count(boxes):
+    total = boxes[0, 2] * boxes[0, 3]
+    for b in range(1, 4):
+        total = total + boxes[b, 2] * boxes[b, 3]
+    return total.astype(F32)
+
+
+def exchange_scratch(label, width):
+    return {
+        f"out_{label}": pltpu.VMEM((8, width), F32),
+        f"in_{label}": pltpu.VMEM((8, 8, width), F32),
+    }
+
+
+def scatter_scratch(label, rows, width):
+    return {f"{label}_{i}": b for i, b in enumerate(scatter_buffers(rows, width))}
+
+
+def scatter_refs(k, label):
+    return [getattr(k, f"{label}_{i}") for i in range(7)]
+
+
+def load_taps(k):
+    loads = []
+    for i in range(3):
+        for j in range(3):
+            loads.append(
+                pltpu.make_async_copy(
+                    k.w_dilated.at[i, j],
+                    k.w_taps.at[i, :, pl.ds(j * 128, 128)],
+                    k.local_sems.at[i * 3 + j],
+                )
+            )
+            loads[-1].start()
+    return loads
+
+
+def send_halo(net, padded):
+    lanes = padded.shape[1]
+    padded[pl.ds(pl.multiple_of(net.r * 2048, 128), 512), :] = jnp.zeros((512, lanes), BF16)
+    return net.send(
+        padded.at[pl.ds(pl.multiple_of(1536 - net.r * 1024, 128), 512)],
+        padded.at[pl.ds(pl.multiple_of(net.r * 2048, 128), 512)],
+        net.core,
+    )
+
+
+def bottleneck_forward(net, k):
+    counted = pixel_count(k.boxes)
+    loads = load_taps(k)
+    own_reduce = pltpu.make_async_copy(
+        k.conv_reduce.at[lane_block(net.m, 512)], k.w_reduce.at[net.m], k.local_sems.at[9]
+    )
+    own_reduce.start()
+    greet([net.side, net.over, net.diagonal] + net.group)
+    branches = [(net.m ^ 3, net.diagonal), (net.m ^ 1, net.side), (net.m ^ 2, net.over)]
+    arrivals = [
+        net.send(k.conv_reduce.at[lane_block(b, 512)], k.w_reduce.at[net.m], peer)
+        for b, peer in branches
+    ]
+
+    top, left_edge = k.boxes[net.z, 0], k.boxes[net.z, 1]
+    bottom, right_edge = top + k.boxes[net.z, 2], left_edge + k.boxes[net.z, 3]
+    column = lax.broadcasted_iota(jnp.int32, (128, 128), 0)
+    column_inside = jnp.where((column >= left_edge) & (column < right_edge), 1.0, 0.0)
+
+    def mask_rows(i, carry):
+        row = jnp.full((128, 128), net.r * 12 + i, jnp.int32)
+        inside = jnp.where((row >= top) & (row < bottom), column_inside, 0.0)
+        k.mask[pl.ds(pl.multiple_of(i * 128, 128), 128), :] = inside
+        return carry
+
+    lax.fori_loop(0, 12, mask_rows, 0)
+
+    def reduce_for(b):
+        def reduce_rows(at):
+            k.part[b, at, :] = mm(k.x[at, :], k.w_reduce[b])
+
+        each_rows(1536, 384, reduce_rows)
+
+    own_reduce.wait()
+    reduce_for(net.m)
+    arrivals[1].wait()
+    reduce_for(net.m ^ 1)
+    arrivals[2].wait()
+    reduce_for(net.m ^ 2)
+    arrivals[0].wait()
+    reduce_for(net.m ^ 3)
+    sum_scatter(net, k.part, scatter_refs(k, "sum"), k.reduced)
+
+    half = pl.ds(pl.multiple_of(net.r * 32, 32), 32)
+    late = []
+
+    def weight_block(kind, b):
+        lanes = lane_block(b, 512)
+        if kind == "edge":
+            return k.aspp_rates.at[0, 2 * net.r, :, :, lanes], k.w_pyramid.at[pl.ds(10, 3), net.m]
+        if kind == "point":
+            return k.aspp_point.at[half, lanes], k.w_pyramid.at[0, net.m, half]
+        if kind == "project":
+            return k.project.at[half], k.w_project.at[net.m, half]
+        return (
+            k.aspp_rates.at[kind, 1, :, half, lanes],
+            k.w_pyramid.at[pl.ds(1 + 3 * kind, 3), net.m, half],
+        )
+
+    def spread_weights(*kinds):
+        for kind in kinds:
+            src, dst = weight_block(kind, net.m)
+            late.append(pltpu.make_async_copy(src, dst, k.local_sems.at[10 + len(late) // 4]))
+            late[-1].start()
+            for b, peer in branches:
+                src, dst = weight_block(kind, b)
+                late.append(net.send(src, dst, peer))
+
+    spread_weights("edge")
+    mean, inverse = statistics(net, k.reduced, k.mask, k.out_1, k.in_1, counted)
+    keep_rows(k.stats_1, mean, inverse)
+
+    def activate_1(at):
+        u = k.affine_1[0:1, :] * ((k.reduced[at, :] - mean) * inverse) + k.affine_1[1:2, :]
+        rows_at = pl.ds(pl.multiple_of(at.start + 512, 128), 128)
+        k.hidden[rows_at, lane_block(net.m)] = (u * sigmoid(u)).astype(BF16)
+
+    each_rows(1536, 128, activate_1)
+    gather_blocks(
+        net, lambda b, at: k.hidden.at[pl.ds(at.start + 512, at.size), lane_block(b)], 1536
+    )
+    halo = send_halo(net, k.hidden)
+    spread_weights("project", "point", 0)
+    zero_margins(k.left, 8, 128)
+    zero_margins(k.right, 8, 128)
+    for load in loads:
+        load.wait()
+    halo.wait()
+
+    def dilated_rows(i, carry):
+        total = 0.0
+        for tap in range(3):
+            rows_at = pl.ds(pl.multiple_of((i * 3 + 4 * tap) * 128, 128), 384)
+            total = total + mm(k.hidden[rows_at, :], k.w_taps[tap])
+        k.dilated[pl.ds(pl.multiple_of(i * 384, 128), 384), :] = total[:, 128:256]
+        k.left[pl.ds(i * 3, 3), 8:136, :] = total[:, 0:128].reshape(3, 128, 128)
+        k.right[pl.ds(i * 3, 3), 8:136, :] = total[:, 256:384].reshape(3, 128, 128)
+        return carry
+
+    lax.fori_loop(0, 4, dilated_rows, 0)
+
+    def add_columns(i, carry):
+        at = pl.ds(pl.multiple_of(i * 128, 128), 128)
+        k.dilated[at, :] = k.dilated[at, :] + k.left[i, 4:132, :] + k.right[i, 12:140, :]
+        return carry
+
+    lax.fori_loop(0, 12, add_columns, 0)
+    mean_2, inverse_2 = statistics(net, k.dilated, k.mask, k.out_2, k.in_2, counted)
+    keep_rows(k.stats_2, mean_2, inverse_2)
+
+    def activate_2(at):
+        u = k.affine_2[0:1, :] * ((k.dilated[at, :] - mean_2) * inverse_2) + k.affine_2[1:2, :]
+        k.hidden_two[at, lane_block(net.m)] = (u * sigmoid(u)).astype(BF16)
+
+    each_rows(1536, 128, activate_2)
+    gather_blocks(net, lambda b, at: k.hidden_two.at[at, lane_block(b)], 1536)
+    spread_weights(1, 2)
+
+    def expand_rows(at):
+        k.expanded[at, :] = mm(k.hidden_two[at, :], k.w_expand[...])
+
+    each_rows(1536, 384, expand_rows)
+    mean_3, inverse_3 = statistics(net, k.expanded, k.mask, k.out_3, k.in_3, counted)
+    keep_rows(k.stats_3, mean_3, inverse_3)
+    for copy in late:
+        copy.wait()
+    swaps = [
+        net.send(ref.at[..., half, :], ref.at[..., half, :], net.core)
+        for ref in (k.w_pyramid.at[pl.ds(0, 10)], k.w_project)
+    ]
+
+    def activate_3(at):
+        u = k.affine_3[0:1, :] * ((k.expanded[at, :] - mean_3) * inverse_3) + k.affine_3[1:2, :]
+        u = u + k.x[at, :].astype(F32)
+        k.trunk[at, :] = (u * sigmoid(u)).astype(BF16)
+
+    each_rows(1536, 32, activate_3)
+    for copy in swaps:
+        copy.wait()
+
+
+def run_bottleneck(args):
+    return call_kernel(
+        bottleneck_forward,
+        "bottleneck",
+        0,
+        args,
+        dict(
+            mask=((1536, 128), F32),
+            w_reduce=((4, 512, 128), BF16),
+            w_pyramid=((13, 4, 64, 512), BF16),
+            w_project=((4, 64, 1280), BF16),
+            reduced=((1536, 128), F32),
+            stats_1=((8, 128), F32),
+            hidden=((2560, 512), BF16),
+            dilated=((1536, 128), F32),
+            stats_2=((8, 128), F32),
+            hidden_two=((1536, 512), BF16),
+            expanded=((1536, 512), F32),
+            stats_3=((8, 512), F32),
+            trunk=((1536, 512), BF16),
+        ),
+        dict(
+            w_taps=pltpu.VMEM((3, 512, 384), BF16),
+            part=pltpu.VMEM((4, 1536, 128), F32),
+            **scatter_scratch("sum", 1536, 128),
+            left=pltpu.VMEM((12, 144, 128), F32),
+            right=pltpu.VMEM((12, 144, 128), F32),
+            **exchange_scratch(1, 128),
+            **exchange_scratch(2, 128),
+            **exchange_scratch(3, 512),
+            local_sems=pltpu.SemaphoreType.DMA((16,)),
+        ),
+        96,
+        hbm=(
+            "conv_reduce",
+            "w_dilated",
+            "aspp_point",
+            "aspp_rates",
+            "project",
+            "w_pyramid",
+            "w_project",
+        ),
+    )
+
+
+def pyramid_forward(net, k):
+    counted = pixel_count(k.boxes)
+    area = (k.boxes[net.z, 2] * k.boxes[net.z, 3]).astype(F32)
+    near = [
+        (lax.rem(net.m + a, 4), lax.rem(net.r + b, 2), net.z)
+        for a in range(4)
+        for b in range(2)
+        if a or b
+    ]
+    greet(net.group + [peer for i, peer in enumerate(near) if i])
+
+    (own_sum,) = column_sums(
+        lambda at: (k.trunk[at, :].astype(F32) * wide(k.mask[at, :], 512),), 1536, 512, 1
+    )
+    k.out_pool[...] = jnp.broadcast_to(own_sum, (8, 512))
+    place = net.m * 2 + net.r
+    pool_copies = [net.send(k.out_pool, k.in_pool.at[place], peer) for peer in near]
+    k.in_pool[place] = k.out_pool[...]
+
+    zero_margins(k.cells, 40, 128)
+
+    def fill(i, carry):
+        at = pl.ds(pl.multiple_of(i * 128, 128), 128)
+        k.cells[i, 40:168, :] = k.trunk[at, :].astype(F32)
+        return carry
+
+    lax.fori_loop(0, 12, fill, 0)
+
+    def shifted(i, offset):
+        cells = k.cells[pl.ds(i * 3, 3), 40 + offset : 168 + offset, :]
+        return cells.reshape(384, 512).astype(BF16)
+
+    def rows_of(i):
+        return pl.ds(pl.multiple_of(i * 384, 128), 384)
+
+    def edge_rows(i, carry):
+        total = 0.0
+        for j in range(3):
+            total = total + mm_t(shifted(i, 12 * (j - 1)), k.w_pyramid[10 + j])
+        k.edge_out[rows_of(i), :] = total.astype(BF16)
+        return carry
+
+    lax.fori_loop(0, 4, edge_rows, 0)
+    edge = net.send(k.edge_out, k.edge_in, net.core)
+
+    def outer_rows(i, carry):
+        second, third = 0.0, 0.0
+        for j in range(3):
+            second = second + mm_t(shifted(i, 24 * (j - 1)), k.w_pyramid[4 + j])
+        for j in range(3):
+            third = third + mm_t(shifted(i, 36 * (j - 1)), k.w_pyramid[7 + j])
+        for b, block in enumerate(pair(second, third)):
+            k.part[b, rows_of(i), 128:256] = block
+        return carry
+
+    lax.fori_loop(0, 4, outer_rows, 0)
+    edge.wait()
+
+    def inner_rows(i, carry):
+        point = mm_t(k.trunk[rows_of(i), :], k.w_pyramid[0])
+        first = k.edge_in[rows_of(i), :].astype(F32)
+        for j in range(3):
+            first = first + mm_t(shifted(i, 12 * (j - 1)), k.w_pyramid[1 + j])
+        for b, block in enumerate(pair(point, first)):
+            k.part[b, rows_of(i), 0:128] = block
+        return carry
+
+    lax.fori_loop(0, 4, inner_rows, 0)
+    sum_scatter(net, k.part, scatter_refs(k, "sum"), k.branches)
+
+    low_256 = lax.broadcasted_iota(jnp.int32, (256, 128), 1) < 64
+    odd = lax.rem(net.m, 2) == 1
+
+    def slot(s):
+        lanes = pl.ds(pl.multiple_of(s * 256 + (net.m // 2) * 128, 128), 128)
+        block = k.w_slots[:, lanes].astype(F32)
+        return jnp.where(odd, pltpu.roll(block, 64, 1), block)
+
+    for s in range(0, 4, 2):
+        both = jnp.where(low_256, slot(s), pltpu.roll(slot(s + 1), 64, 1))
+        k.w_project[:, s * 64 : s * 64 + 128] = both.astype(BF16)
+    k.w_slot[...] = jnp.where(low_256, slot(4), 0.0).astype(BF16)
+    k.w_pool[0:64, :] = k.aspp_pool[...]
+    k.w_pool[64:128, :] = k.aspp_pool[...]
+
+    for copy in pool_copies:
+        copy.wait()
+    for b in range(4):
+        pooled = (k.in_pool[2 * b, 0:1, :] + k.in_pool[2 * b + 1, 0:1, :]) / area
+        k.pooled[:, b * 512 : b * 512 + 512] = jnp.broadcast_to(pooled, (16, 512)).astype(BF16)
+    pool_conv = mm_t(k.pooled[...], k.w_pool[...])[0:1, :]
+    mean, inverse = statistics(
+        net, k.branches, k.mask, k.out_1, k.in_1, counted, extra=wide(pool_conv, 256)
+    )
+    every = k.in_1[0:4, 3, 0:128]
+    pool_mean = jnp.sum(every, axis=0, keepdims=True) / 4.0
+    pool_gap = every - pool_mean
+    pool_inverse = lax.rsqrt(jnp.sum(pool_gap * pool_gap, axis=0, keepdims=True) / 4.0 + EPS)
+    pool_normed = pool_gap * pool_inverse
+    pool_gain, pool_bias = k.affine_p[2:3, :], k.affine_p[3:4, :]
+    pool_u = pool_gain * pool_normed + pool_bias
+    k.rows_scratch[0:4, :] = pool_u * sigmoid(pool_u)
+    pool_act = jnp.broadcast_to(k.rows_scratch[pl.ds(net.z, 1), :], (16, 128)).astype(BF16)
+
+    def normed_branch(at):
+        return (k.branches[at, :] - mean) * inverse
+
+    gain_b, bias_b = k.affine_b[0:1, :], k.affine_b[1:2, :]
+
+    def activate_branches(at):
+        u = gain_b * normed_branch(at) + bias_b
+        k.spatial[at, :] = (u * sigmoid(u)).astype(BF16)
+
+    each_rows(1536, 64, activate_branches)
+
+    pool_row = mm_t(pool_act, k.w_slot[...])[0:1, :]
+
+    def project_rows(i, carry):
+        at = pl.ds(pl.multiple_of(i * 384, 128), 384)
+        below = pl.ds(pl.multiple_of(i * 384 + 768, 128), 384)
+        first = mm_t(k.spatial[at, :], k.w_project[...]) + pool_row
+        second = mm_t(k.spatial[below, :], k.w_project[...]) + pool_row
+        for b, block in enumerate(pair(first, second)):
+            k.part_2[b, at, :] = block
+        return carry
+
+    lax.fori_loop(0, 2, project_rows, 0)
+    low_128 = lax.broadcasted_iota(jnp.int32, (128, 128), 1) < 64
+
+    def pair_mask(at):
+        below = pl.ds(pl.multiple_of(at.start + 768, 128), 128)
+        k.mask_pairs[at, :] = jnp.where(low_128, k.mask[at, :], k.mask[below, :])
+
+    each_rows(768, 128, pair_mask)
+    sum_scatter(net, k.part_2, scatter_refs(k, "sum2"), k.projected)
+    mean_p, inverse_p = statistics(
+        net, k.projected, k.mask_pairs, k.out_2, k.in_2, counted, folded=True
+    )
+    gain_p, bias_p = k.affine_p[0:1, :], k.affine_p[1:2, :]
+
+    def normed_projected(at):
+        return (k.projected[at, :] - mean_p) * inverse_p
+
+    def activate_projected(at):
+        u = gain_p * normed_projected(at) + bias_p
+        k.gathered[net.m, at, :] = (u * sigmoid(u)).astype(BF16)
+
+    each_rows(768, 128, activate_projected)
+    gather_blocks(net, lambda b, at: k.gathered.at[b, at], 768)
+
+    def spread(source, target):
+        def body(at):
+            first, second = unpair([source[b, at, :].astype(F32) for b in range(4)])
+            target[at, :] = first.astype(BF16)
+            target[pl.ds(pl.multiple_of(at.start + 768, 128), 128), :] = second.astype(BF16)
+
+        each_rows(768, 128, body)
+
+    k.features[...] = k.gathered[net.m]
+    spread(k.gathered, k.wide_features)
+
+    class_row = lax.broadcasted_iota(jnp.int32, (32, 512), 0)
+    is_class, is_depth = class_row < 19, class_row == 19
+    is_normal = (class_row == 20) | (class_row == 21)
+    bias_column = wide(k.head_columns[0], 512)
+    weight_column = wide(k.head_columns[1], 512)
+    top_row, left_edge = k.boxes[net.z, 0], k.boxes[net.z, 1]
+    bottom_row, right_edge = top_row + k.boxes[net.z, 2], left_edge + k.boxes[net.z, 3]
+    lane = lax.broadcasted_iota(jnp.int32, (1, 512), 1)
+
+    def four_rows(rows):
+        return jnp.concatenate(rows, axis=1)
+    loss_sums, bias_sums = 0.0, 0.0
+    for chunk in range(3):
+        at = pl.ds(chunk * 512, 512)
+        logits = mm_t(k.head[...], k.wide_features[at, :]) + bias_column
+        row_id, column_id = net.r * 12 + chunk * 4 + lane // 128, lane % 128
+        inside = (row_id >= top_row) & (row_id < bottom_row)
+        inside = inside & (column_id >= left_edge) & (column_id < right_edge)
+        inside = jnp.where(inside, 1.0, 0.0)
+        span = range(chunk * 4, chunk * 4 + 4)
+        label = four_rows([k.labels[0, y : y + 1, :] for y in span])
+        target = jnp.where(is_depth, four_rows([k.depth[0, y : y + 1, :] for y in span]), 0.0)
+        for n in range(2):
+            normal = four_rows([k.normal[0, n, y : y + 1, :] for y in span])
+            target = jnp.where(class_row == 20 + n, normal, target)
+        top = jnp.max(jnp.where(is_class, logits, -jnp.inf), axis=0, keepdims=True)
+        powers = jnp.where(is_class, jnp.exp(jnp.where(is_class, logits - top, 0.0)), 0.0)
+        power_sum = jnp.sum(powers, axis=0, keepdims=True)
+        onehot = jnp.where(class_row == label, 1.0, 0.0)
+        cross = jnp.log(power_sum) + top - jnp.sum(logits * onehot, axis=0, keepdims=True)
+        gap = logits - target
+        smooth = jnp.sqrt(gap * gap + 1.0)
+        loss = jnp.where(class_row == 0, cross, 0.0)
+        loss = jnp.where(is_depth, smooth - 1.0, loss)
+        loss = jnp.where(is_normal, gap * gap, loss) * inside
+        grad = jnp.where(is_class, powers / power_sum - onehot, 0.0)
+        grad = jnp.where(is_depth, gap / smooth, grad)
+        grad = jnp.where(is_normal, 2.0 * gap, grad) * (weight_column * inside)
+        loss_sums = loss_sums + jnp.sum(loss, axis=1, keepdims=True)
+        bias_sums = bias_sums + jnp.sum(grad, axis=1, keepdims=True)
+        high = grad.astype(BF16)
+        k.grad_logits[0:32, at] = high
+        k.grad_logits[32:64, at] = (grad - high.astype(F32)).astype(BF16)
+    head_terms = mm(k.grad_logits[...], k.wide_features[...])
+    k.out_head[0:32, :] = head_terms[0:32, :] + head_terms[32:64, :]
+    k.out_head[32:64, :] = jnp.broadcast_to(bias_sums, (32, 256))
+    k.out_head[64:96, :] = jnp.broadcast_to(loss_sums, (32, 256))
+    head_copies = [net.send(k.out_head, k.in_head.at[net.slot], peer) for peer in net.group]
+    k.in_head[net.slot] = k.out_head[...]
+
+    own_head = k.head[:, lane_block(net.m // 2)].astype(F32)
+    own_head = jnp.where(odd, pltpu.roll(own_head, 64, 1), own_head)
+    own_head = jnp.where(low_128[0:32, :], own_head, 0.0)
+    head_low = jnp.concatenate([own_head, own_head], axis=0).astype(BF16)
+    own_head = pltpu.roll(own_head, 64, 1)
+    head_high = jnp.concatenate([own_head, own_head], axis=0).astype(BF16)
+    k.grad_p[...] = tm_m(k.grad_logits[:, 0:768], head_low) + tm_m(
+        k.grad_logits[:, 768:1536], head_high
+    )
+
+    def back_features(at):
+        k.grad_p[at, :] = k.grad_p[at, :] * slope(gain_p * normed_projected(at) + bias_p)
+
+    each_rows(768, 128, back_features)
+    bias_grad, gain_grad = gradient_sums(
+        net, k.grad_p, normed_projected, k.out_3, k.in_3, folded=True
+    )
+    keep_rows(k.norm_p, gain_grad, bias_grad)
+
+    def back_projected(at):
+        shared = k.mask_pairs[at, :] / counted * gain_p
+        grad = gain_p * k.grad_p[at, :] - shared * (bias_grad + normed_projected(at) * gain_grad)
+        k.gathered_grad[net.m, at, :] = (inverse_p * grad).astype(BF16)
+
+    each_rows(768, 128, back_projected)
+    gather_blocks(net, lambda b, at: k.gathered_grad.at[b, at], 768)
+    spread(k.gathered_grad, k.grad_projected)
+    (pixel_sum,) = column_sums(lambda at: (k.grad_projected[at, :].astype(F32),), 1536, 256, 1)
+    row_16 = lax.broadcasted_iota(jnp.int32, (16, 256), 0)
+    terms = jnp.zeros((16, 256), F32)
+    for i, term in enumerate(split_three(pixel_sum)):
+        terms = jnp.where(row_16 == i, term.astype(F32), terms)
+    terms = terms.astype(BF16)
+    pool_grad = jnp.sum(mm(terms, k.w_slot[...]), axis=0, keepdims=True)
+
+    def project_gradient():
+        for b in range(2):
+            lanes = slice(b * 128, b * 128 + 128)
+            grad = tm_m(k.grad_projected[:, lanes], k.spatial[...])
+            k.grad_project[b * 4 : b * 4 + 4, :, 0:256] = grad.reshape(4, 32, 256).astype(BF16)
+        grad = tm_m(terms, pool_act)
+        k.grad_project[:, :, 256:384] = grad.reshape(8, 32, 128).astype(BF16)
+
+    def back_spatial(at):
+        grad = mm(k.grad_projected[at, :], k.w_project[...])
+        k.grad_b[at, :] = grad * slope(gain_b * normed_branch(at) + bias_b)
+
+    each_rows(1536, 128, back_spatial)
+    bias_grad_b, gain_grad_b = gradient_sums(
+        net,
+        k.grad_b,
+        normed_branch,
+        k.out_4,
+        k.in_4,
+        extra=wide(pool_grad, 256),
+        meanwhile=project_gradient,
+    )
+    keep_rows(k.norm_b, gain_grad_b, bias_grad_b)
+
+    pool_terms = k.in_4[0:4, 2, 0:128] + k.in_4[4:8, 2, 0:128]
+    pool_terms = pool_terms * slope(pool_u)
+    pool_bias_grad = jnp.sum(pool_terms, axis=0, keepdims=True)
+    pool_gain_grad = jnp.sum(pool_terms * pool_normed, axis=0, keepdims=True)
+    keep_rows(k.norm_pool, pool_gain_grad, pool_bias_grad)
+    pool_back = pool_inverse * (
+        pool_gain * pool_terms
+        - pool_gain / 4.0 * (pool_bias_grad + pool_normed * pool_gain_grad)
+    )
+    low = lax.broadcasted_iota(jnp.int32, (4, 128), 1) < 64
+    k.rows_scratch[4:8, :] = jnp.where(low, pool_back, 0.0)
+    grad_conv = jnp.broadcast_to(k.rows_scratch[pl.ds(net.z + 4, 1), :], (16, 128)).astype(BF16)
+    spread_back = mm(grad_conv, k.w_pool[...])[0:8, :]
+    for b in range(4):
+        k.out_back[b] = spread_back[:, b * 512 : b * 512 + 512]
+    back_copies = [
+        net.send(k.out_back.at[lax.rem(net.m + a, 4)], k.in_back.at[a], (lax.rem(net.m + a, 4), net.r, net.z))
+        for a in range(1, 4)
+    ]
+
+    only_first = lax.broadcasted_iota(jnp.int32, (16, 128), 0) == 0
+    one_row = jnp.where(only_first, grad_conv.astype(F32) * 0.5, 0.0).astype(BF16)
+    for e in range(8):
+        grad = tm_m(one_row, k.pooled[:, e * 256 : e * 256 + 256])
+        k.grad_pool[e] = grad[0:64, :].astype(BF16)
+
+    def back_branches(at):
+        shared = wide(k.mask[at, :], 256) / counted * gain_b
+        grad = gain_b * k.grad_b[at, :] - shared * (bias_grad_b + normed_branch(at) * gain_grad_b)
+        k.grad_branches[at, :] = (inverse * grad).astype(BF16)
+
+    each_rows(1536, 64, back_branches)
+    for copy in back_copies:
+        copy.wait()
+    k.grad_pooled[...] = (k.out_back[net.m] + k.in_back[1] + k.in_back[2] + k.in_back[3]) / area
+    for copy in head_copies:
+        copy.wait()
+    k.head_sums[...] = jnp.sum(k.in_head[...], axis=0)
+
+
+def run_pyramid(args):
+    return call_kernel(
+        pyramid_forward,
+        "pyramid",
+        1,
+        args,
+        dict(
+            features=((768, 128), BF16),
+            norm_p=((8, 128), F32),
+            grad_project=((8, 32, 384), BF16),
+            grad_pool=((8, 64, 256), BF16),
+            norm_b=((8, 256), F32),
+            norm_pool=((8, 128), F32),
+            grad_branches=((1536, 256), BF16),
+            grad_pooled=((8, 512), F32),
+            head_sums=((96, 256), F32),
+        ),
+        dict(
+            pooled=pltpu.VMEM((16, 2048), BF16),
+            spatial=pltpu.VMEM((1536, 256), BF16),
+            grad_projected=pltpu.VMEM((1536, 256), BF16),
+            w_project=pltpu.VMEM((256, 256), BF16),
+            w_slot=pltpu.VMEM((256, 128), BF16),
+            w_pool=pltpu.VMEM((128, 2048), BF16),
+            mask_pairs=pltpu.VMEM((768, 128), F32),
+            out_pool=pltpu.VMEM((8, 512), F32),
+            in_pool=pltpu.VMEM((8, 8, 512), F32),
+            cells=pltpu.VMEM((12, 208, 512), F32),
+            edge_out=pltpu.VMEM((1536, 256), BF16),
+            edge_in=pltpu.VMEM((1536, 256), BF16),
+            part=pltpu.VMEM((4, 1536, 256), F32),
+            **scatter_scratch("sum", 1536, 256),
+            branches=pltpu.VMEM((1536, 256), F32),
+            rows_scratch=pltpu.VMEM((8, 128), F32),
+            part_2=pltpu.VMEM((4, 768, 128), F32),
+            **scatter_scratch("sum2", 768, 128),
+            projected=pltpu.VMEM((768, 128), F32),
+            gathered=pltpu.VMEM((4, 768, 128), BF16),
+            wide_features=pltpu.VMEM((1536, 256), BF16),
+            grad_logits=pltpu.VMEM((64, 1536), BF16),
+            out_head=pltpu.VMEM((96, 256), F32),
+            in_head=pltpu.VMEM((8, 96, 256), F32),
+            grad_p=pltpu.VMEM((768, 128), F32),
+            gathered_grad=pltpu.VMEM((4, 768, 128), BF16),
+            grad_b=pltpu.VMEM((1536, 256), F32),
+            out_back=pltpu.VMEM((4, 8, 512), F32),
+            in_back=pltpu.VMEM((4, 8, 512), F32),
+            **exchange_scratch(1, 256),
+            **exchange_scratch(2, 128),
+            **exchange_scratch(3, 128),
+            **exchange_scratch(4, 256),
+        ),
+        96,
+    )
+
+
+def core_halves(net, whole, arrived):
+    away = pl.ds(pl.multiple_of(4 - 4 * net.r, 4), 4)
+    return net.send(whole.at[away], arrived, net.core)
+
+
+def add_halves(net, whole, arrived, target):
+    for z in range(4):
+        total = whole[4 * net.r + z].astype(F32) + arrived[z].astype(F32)
+        target[z] = total.astype(target.dtype)
+
+
+def pyramid_backward(net, k):
+    counted = pixel_count(k.boxes)
+    greet([net.side, net.over] + net.group)
+    k.blocks[net.m] = k.grad_branches[...]
+    gather_blocks(net, lambda b, at: k.blocks.at[b, at], 1536)
+    beside = net.send(k.blocks.at[:, :, pl.ds(0, 128)], k.other, net.core)
+    zero_margins(k.cells, 40, 128)
+
+    def rows_of(i, size=384):
+        return pl.ds(pl.multiple_of(i * size, 128), size)
+
+    def taps(source, lane, second, rate, base):
+        def fill(i, carry):
+            blocks = [
+                source[b, rows_of(i, 128), lane * 128 : lane * 128 + 128].astype(F32)
+                for b in range(4)
+            ]
+            k.cells[i, 40:168, :] = unpair(blocks)[second]
+            return carry
+
+        lax.fori_loop(0, 12, fill, 0)
+
+        def cut(i, carry):
+            for j in range(3):
+                start = 40 - rate * (j - 1)
+                k.shifts[base + j, rows_of(i, 128), :] = k.cells[i, start : start + 128, :].astype(
+                    BF16
+                )
+            return carry
+
+        lax.fori_loop(0, 12, cut, 0)
+
+    def point(i, carry):
+        blocks = [k.blocks[b, rows_of(i, 128), 0:128].astype(F32) for b in range(4)]
+        k.shifts[0, rows_of(i, 128), :] = unpair(blocks)[0].astype(BF16)
+        return carry
+
+    lax.fori_loop(0, 12, point, 0)
+    taps(k.blocks, 0, 1, 12, 1)
+    taps(k.blocks, 1, 0, 24, 4)
+    taps(k.blocks, 1, 1, 36, 7)
+    beside.wait()
+    taps(k.other, 0, 1, 12, 10)
+
+    def trunk_rows(i, carry):
+        total = 0.0
+        for t in range(13):
+            total = total + mm(k.shifts[t, rows_of(i), :], k.w_pyramid[t])
+        k.shortcut[rows_of(i), :] = total
+        return carry
+
+    lax.fori_loop(0, 4, trunk_rows, 0)
+    mean, inverse = k.stats_3[0:1, :], k.stats_3[1:2, :]
+    gain, bias = k.affine_3[0:1, :], k.affine_3[1:2, :]
+    pooled = k.grad_pooled[0:1, :]
+
+    def normed(at):
+        return (k.expanded[at, :] - mean) * inverse
+
+    def back_trunk(at):
+        u = gain * normed(at) + bias + k.x[at, :].astype(F32)
+        grad = k.shortcut[at, :] + wide(k.mask[at, :], 512) * pooled
+        k.shortcut[at, :] = grad * slope(u)
+
+    each_rows(1536, 32, back_trunk)
+
+    def weight_gradient(t, slot):
+        grad = tm_m(k.shifts[t], k.trunk[...])
+        k.grad_pyramid[:, slot] = grad.reshape(8, 32, 512).astype(BF16)
+
+    def run(low, high, shift):
+        def body(t, carry):
+            weight_gradient(t, t + shift)
+            return carry
+
+        lax.fori_loop(low, high, body, 0)
+
+    swaps = []
+
+    def weight_gradients():
+        weight_gradient(0, 0)
+        run(1, 4, 3)
+        run(4, 10, 6)
+        run(10, 13, net.r * 6 - 9)
+        for j in range(3):
+            k.grad_pyramid[:, 7 - net.r * 6 + j] = jnp.zeros((8, 32, 512), BF16)
+        swaps.append(core_halves(net, k.grad_pyramid, k.core_pyramid))
+        swaps.append(core_halves(net, k.grad_project, k.core_project))
+        swaps.append(core_halves(net, k.grad_pool, k.core_pool))
+
+    bias_grad, gain_grad = gradient_sums(
+        net, k.shortcut, normed, k.out_1, k.in_1, meanwhile=weight_gradients
+    )
+    keep_rows(k.norm_3, gain_grad, bias_grad)
+
+    def back_expanded(at):
+        shared = wide(k.mask[at, :], 512) / counted * gain
+        grad = gain * k.shortcut[at, :] - shared * (bias_grad + normed(at) * gain_grad)
+        k.grad_expanded[at, :] = (inverse * grad).astype(BF16)
+
+    each_rows(1536, 32, back_expanded)
+    for swap in swaps:
+        swap.wait()
+
+    def add_pyramid(i, carry):
+        for z in range(4):
+            total = k.grad_pyramid[4 * net.r + z, i].astype(F32) + k.core_pyramid[z, i].astype(F32)
+            k.half_pyramid[z, i] = total.astype(BF16)
+        return carry
+
+    lax.fori_loop(0, 16, add_pyramid, 0)
+    add_halves(net, k.grad_project, k.core_project, k.half_project)
+    add_halves(net, k.grad_pool, k.core_pool, k.half_pool)
+
+
+def run_pyramid_backward(args):
+    return call_kernel(
+        pyramid_backward,
+        "pyramid_back",
+        2,
+        args,
+        dict(
+            shortcut=((1536, 512), F32),
+            grad_expanded=((1536, 512), BF16),
+            norm_3=((8, 512), F32),
+            half_pyramid=((4, 16, 32, 512), BF16),
+            half_project=((4, 32, 384), BF16),
+            half_pool=((4, 64, 256), BF16),
+        ),
+        dict(
+            grad_pyramid=pltpu.VMEM((8, 16, 32, 512), BF16),
+            core_pyramid=pltpu.VMEM((4, 16, 32, 512), BF16),
+            core_project=pltpu.VMEM((4, 32, 384), BF16),
+            core_pool=pltpu.VMEM((4, 64, 256), BF16),
+            blocks=pltpu.VMEM((4, 1536, 256), BF16),
+            other=pltpu.VMEM((4, 1536, 128), BF16),
+            cells=pltpu.VMEM((12, 208, 256), F32),
+            shifts=pltpu.VMEM((13, 1536, 256), BF16),
+            **exchange_scratch(1, 512),
+        ),
+        32,
+    )
+
+
+def bottleneck_backward(net, k):
+    counted = pixel_count(k.boxes)
+    loads = load_taps(k)
+    odd = lax.rem(net.slot, 2)
+    owners = []
+    for which in (odd, 1 - odd):
+        part = 2 * net.m + which
+        owners.append((net.slot // 2, part // 4, lax.rem(part, 4)))
+    stays = net.slot // 2 == net.m
+    moves = jnp.logical_not(stays)
+    greet([net.side, net.over] + net.group + [owners[1]], (owners[0], moves))
+
+    def along_z(source, target):
+        return [
+            net.send(
+                source.at[lax.rem(net.z + d, 4)],
+                target.at[d - 1],
+                (net.m, net.r, lax.rem(net.z + d, 4)),
+            )
+            for d in (1, 2, 3)
+        ]
+
+    def to_owners(views, arrived, sem):
+        first = pltpu.make_async_remote_copy(
+            src_ref=views(0),
+            dst_ref=arrived.at[0],
+            send_sem=net.send_sems.at[net.count],
+            recv_sem=net.recv_sems.at[net.count],
+            device_id=owners[0],
+            device_id_type=MESH,
+        )
+        net.count += 1
+        kept = pltpu.make_async_copy(views(0), arrived.at[0], sem)
+        pl.when(moves)(first.start)
+        pl.when(stays)(kept.start)
+        second = net.send(views(1), arrived.at[1], owners[1])
+
+        def wait():
+            pl.when(moves)(first.wait)
+            pl.when(stays)(kept.wait)
+            second.wait()
+
+        return wait
+
+    pyramid_moves = along_z(k.half_pyramid, k.z_pyramid)
+    small_moves = along_z(k.half_project, k.z_project) + along_z(k.half_pool, k.z_pool)
+
+    def rows_of(i, size=384):
+        return pl.ds(pl.multiple_of(i * size, 128), size)
+
+    def expand_rows(at):
+        total = mm_t(k.grad_expanded[at, :], k.w_expand[...])
+        for b in range(4):
+            k.part[b, at, :] = total[:, b * 128 : b * 128 + 128]
+
+    each_rows(1536, 384, expand_rows)
+
+    def expand_gradient():
+        def body(b, carry):
+            grad = tm_m(k.hidden_two[:, lane_block(b)], k.grad_expanded[...])
+            k.grad_expand[pl.ds(2 * b, 2)] = grad.reshape(2, 64, 512).astype(BF16)
+            return carry
+
+        lax.fori_loop(0, 4, body, 0)
+
+    sum_scatter(net, k.part, scatter_refs(k, "sum"), k.grad_2, meanwhile=expand_gradient)
+
+    def norm_back(grad, value, stats, affine, outgoing, incoming, store, kept, meanwhile=None):
+        mean, inverse = stats[0:1, :], stats[1:2, :]
+        gain, bias = affine[0:1, :], affine[1:2, :]
+
+        def normed(at):
+            return (value[at, :] - mean) * inverse
+
+        def through(at):
+            grad[at, :] = grad[at, :] * slope(gain * normed(at) + bias)
+
+        each_rows(1536, 128, through)
+        bias_grad, gain_grad = gradient_sums(
+            net, grad, normed, outgoing, incoming, meanwhile=meanwhile
+        )
+        keep_rows(kept, gain_grad, bias_grad)
+
+        def back(at):
+            shared = k.mask[at, :] / counted * gain
+            result = gain * grad[at, :] - shared * (bias_grad + normed(at) * gain_grad)
+            store(at, (inverse * result).astype(BF16))
+
+        each_rows(1536, 128, back)
+
+    def store_2(at, value):
+        k.grad_pad[pl.ds(pl.multiple_of(at.start + 512, 128), 128), :] = value
+
+    norm_back(k.grad_2, k.dilated, k.stats_2, k.affine_2, k.out_2, k.in_2, store_2, k.norm_2)
+    halo = send_halo(net, k.grad_pad)
+    zero_margins(k.cells, 8, 128)
+    halo.wait()
+
+    def spread(i, carry):
+        k.cells[i, 8:136, :] = k.grad_pad[rows_of(i, 128), :].astype(F32)
+        for j in range(3):
+            start = 8 - 4 * (j - 1)
+            k.grad_taps[rows_of(i, 128), j * 128 : j * 128 + 128] = k.cells[
+                i, start : start + 128, :
+            ].astype(BF16)
+        return carry
+
+    lax.fori_loop(0, 20, spread, 0)
+    for load in loads:
+        load.wait()
+
+    def dilated_rows(i, carry):
+        total = 0.0
+        for tap in range(3):
+            at = pl.ds(pl.multiple_of((i * 3 + 8 - 4 * tap) * 128, 128), 384)
+            total = total + mm_t(k.grad_taps[at, :], k.w_taps[tap])
+        for b in range(4):
+            k.part[b, rows_of(i), :] = total[:, b * 128 : b * 128 + 128]
+        return carry
+
+    lax.fori_loop(0, 4, dilated_rows, 0)
+    swaps = []
+
+    def dilated_gradient():
+        for i in range(3):
+
+            def body(b, carry):
+                band = k.hidden[pl.ds(i * 512, 1536), lane_block(b)]
+                grad = tm_m(band, k.grad_taps[pl.ds(512, 1536), :])
+                for j in range(3):
+                    block = grad[:, j * 128 : j * 128 + 128].reshape(2, 64, 128)
+                    rows = slice((i * 3 + j) * 64, (i * 3 + j) * 64 + 64)
+                    k.grad_dilated[pl.ds(2 * b, 2), rows, :] = block.astype(BF16)
+                return carry
+
+            lax.fori_loop(0, 4, body, 0)
+        swaps.append(core_halves(net, k.grad_dilated, k.core_dilated))
+        swaps.append(core_halves(net, k.grad_expand, k.core_expand))
+
+    sum_scatter(net, k.part, scatter_refs(k, "sum2"), k.grad_1, meanwhile=dilated_gradient)
+
+    def store_1(at, value):
+        k.grad_reduced[at, lane_block(net.m)] = value
+
+    late_moves = []
+
+    def pass_halves():
+        for swap in swaps:
+            swap.wait()
+        add_halves(net, k.grad_dilated, k.core_dilated, k.half_dilated)
+        add_halves(net, k.grad_expand, k.core_expand, k.half_expand)
+        late_moves.extend(along_z(k.half_dilated, k.z_dilated))
+        late_moves.extend(along_z(k.half_expand, k.z_expand))
+
+    norm_back(
+        k.grad_1,
+        k.reduced,
+        k.stats_1,
+        k.affine_1,
+        k.out_1,
+        k.in_1,
+        store_1,
+        k.norm_1,
+        meanwhile=pass_halves,
+    )
+    gather_blocks(net, lambda b, at: k.grad_reduced.at[at, lane_block(b)], 1536)
+
+    def reduce_gradient(b, carry):
+        grad = tm_m(k.grad_reduced[:, lane_block(b)], k.x[...])
+        k.grad_reduce[pl.ds(2 * b, 2)] = grad.reshape(2, 64, 512).astype(BF16)
+        return carry
+
+    lax.fori_loop(0, 4, reduce_gradient, 0)
+    swap = core_halves(net, k.grad_reduce, k.core_reduce)
+
+    def finish(half, arrived):
+        return half[net.z].astype(F32) + sum(arrived[d].astype(F32) for d in range(3))
+
+    for move_ in pyramid_moves + small_moves:
+        move_.wait()
+
+    def sum_pyramid(i, carry):
+        total = k.half_pyramid[net.z, i].astype(F32)
+        for d in range(3):
+            total = total + k.z_pyramid[d, i].astype(F32)
+        k.sum_pyramid[i] = total.astype(BF16)
+        return carry
+
+    lax.fori_loop(0, 16, sum_pyramid, 0)
+    k.sum_project[...] = finish(k.half_project, k.z_project)
+    k.sum_pool[...] = finish(k.half_pool, k.z_pool)
+
+    def lanes_for(i):
+        return lane_block(odd if i == 0 else 1 - odd, 256)
+
+    wait_pyramid = to_owners(
+        lambda i: k.sum_pyramid.at[:, :, lanes_for(i)], k.own_pyramid, k.local_sems.at[9]
+    )
+    wait_project = to_owners(lambda i: k.sum_project, k.own_project, k.local_sems.at[10])
+    swap.wait()
+    add_halves(net, k.grad_reduce, k.core_reduce, k.half_reduce)
+    reduce_moves = along_z(k.half_reduce, k.z_reduce)
+
+    def input_rows(at):
+        total = k.shortcut[at, :]
+        for b in range(4):
+            total = total + mm_t(k.grad_reduced[at, b * 128 : b * 128 + 128], k.w_reduce[b])
+        k.grad_input[at, :] = total
+
+    each_rows(1536, 384, input_rows)
+    for move_ in reduce_moves:
+        move_.wait()
+    k.sum_reduce[...] = finish(k.half_reduce, k.z_reduce)
+    wait_reduce = to_owners(
+        lambda i: k.sum_reduce.at[:, lanes_for(i)], k.own_reduce, k.local_sems.at[11]
+    )
+    for move_ in late_moves:
+        move_.wait()
+    k.sum_dilated[...] = finish(k.half_dilated, k.z_dilated)
+    k.sum_expand[...] = finish(k.half_expand, k.z_expand)
+    wait_pyramid()
+
+    def rows_for(i):
+        return pl.ds(pl.multiple_of((odd if i == 0 else 1 - odd) * 32, 32), 32)
+
+    nothing = jnp.zeros((64, 256), F32)
+    for tap in (9, 10, 11, 15, 16, 17, 18, 19, 20, 24, 25, 26):
+        k.grad_rates[tap] = nothing
+    for slot in range(16):
+        for i in range(2):
+            block = k.own_pyramid[i, slot].astype(F32)
+            if slot == 0:
+                k.grad_point[rows_for(i), :] = block
+            else:
+                tap = slot - 1 if slot < 10 else slot + 2 if slot < 13 else slot + 8
+                k.grad_rates[tap, rows_for(i), :] = block
+    wait_project()
+    wait_reduce()
+
+
+def run_bottleneck_backward(args):
+    return call_kernel(
+        bottleneck_backward,
+        "bottleneck_back",
+        3,
+        args,
+        dict(
+            grad_input=((1536, 512), F32),
+            norm_2=((8, 128), F32),
+            norm_1=((8, 128), F32),
+            grad_rates=((27, 64, 256), F32),
+            grad_point=((64, 256), F32),
+            own_project=((2, 32, 384), F32),
+            sum_pool=((64, 256), F32),
+            sum_dilated=((576, 128), F32),
+            sum_expand=((64, 512), F32),
+            own_reduce=((2, 64, 256), F32),
+        ),
+        dict(
+            grad_taps=pltpu.VMEM((2560, 384), BF16),
+            grad_reduced=pltpu.VMEM((1536, 512), BF16),
+            z_pyramid=pltpu.VMEM((3, 16, 32, 512), BF16),
+            z_project=pltpu.VMEM((3, 32, 384), BF16),
+            z_pool=pltpu.VMEM((3, 64, 256), BF16),
+            sum_pyramid=pltpu.VMEM((16, 32, 512), BF16),
+            own_pyramid=pltpu.VMEM((2, 16, 32, 256), BF16),
+            sum_project=pltpu.VMEM((32, 384), F32),
+            sum_reduce=pltpu.VMEM((64, 512), F32),
+            grad_expand=pltpu.VMEM((8, 64, 512), BF16),
+            core_expand=pltpu.VMEM((4, 64, 512), BF16),
+            half_expand=pltpu.VMEM((4, 64, 512), BF16),
+            z_expand=pltpu.VMEM((3, 64, 512), BF16),
+            grad_reduce=pltpu.VMEM((8, 64, 512), BF16),
+            core_reduce=pltpu.VMEM((4, 64, 512), BF16),
+            half_reduce=pltpu.VMEM((4, 64, 512), BF16),
+            z_reduce=pltpu.VMEM((3, 64, 512), BF16),
+            grad_dilated=pltpu.VMEM((8, 576, 128), BF16),
+            core_dilated=pltpu.VMEM((4, 576, 128), BF16),
+            half_dilated=pltpu.VMEM((4, 576, 128), BF16),
+            z_dilated=pltpu.VMEM((3, 576, 128), BF16),
+            w_taps=pltpu.VMEM((3, 512, 384), BF16),
+            part=pltpu.VMEM((4, 1536, 128), F32),
+            **scatter_scratch("sum", 1536, 128),
+            **scatter_scratch("sum2", 1536, 128),
+            grad_2=pltpu.VMEM((1536, 128), F32),
+            grad_1=pltpu.VMEM((1536, 128), F32),
+            grad_pad=pltpu.VMEM((2560, 128), BF16),
+            cells=pltpu.VMEM((20, 144, 128), F32),
+            **exchange_scratch(2, 128),
+            **exchange_scratch(1, 128),
+            local_sems=pltpu.SemaphoreType.DMA((12,)),
+        ),
+        96,
+        hbm=("w_dilated",),
+    )
+
+
+def fast_local(
+    trunk_input,
+    conv_reduce,
+    conv_dilated,
+    conv_expand,
+    reduction_norm_params,
+    dilated_norm_params,
+    expansion_norm_params,
+    aspp_point,
+    aspp_rates,
+    aspp_pool,
+    branch_norms,
+    pooling_norm_params,
+    aspp_project,
+    projection_norm_params,
+    head_weight,
+    head_bias,
+    log_vars,
+    crop_boxes,
+    seg_labels,
+    depth_target,
+    normal_target,
+):
+    x = trunk_input.reshape(1536, 512)
+    forward = run_bottleneck(
+        dict(
+            x=x,
+            conv_reduce=conv_reduce,
+            w_dilated=conv_dilated,
+            w_expand=conv_expand,
+            aspp_point=aspp_point,
+            aspp_rates=aspp_rates,
+            project=aspp_project.reshape(64, 1280),
+            affine_1=reduction_norm_params,
+            affine_2=dilated_norm_params,
+            affine_3=expansion_norm_params,
+            boxes=crop_boxes,
+        )
+    )
+    w_pyramid = forward.w_pyramid.reshape(13, 256, 512)
+
+    count = jnp.sum((crop_boxes[:, 2] * crop_boxes[:, 3]).astype(F32))
+    task_weights = jnp.exp(-log_vars)
+    by_row = jnp.concatenate(
+        [jnp.full((19,), task_weights[0]), task_weights[1:2], jnp.full((2,), task_weights[2])]
+    )
+    columns = jnp.pad(jnp.stack([head_bias, by_row / count]), ((0, 0), (0, 10)))
+    both = jnp.concatenate([projection_norm_params, pooling_norm_params], axis=0)
+    middle = run_pyramid(
+        dict(
+            trunk=forward.trunk,
+            mask=forward.mask,
+            w_pyramid=w_pyramid,
+            affine_b=branch_norms.reshape(2, 256),
+            affine_p=jnp.concatenate([both, both], axis=1),
+            aspp_pool=aspp_pool,
+            w_slots=forward.w_project.reshape(256, 1280),
+            head=jnp.pad(head_weight.T, ((0, 10), (0, 0))),
+            head_columns=jnp.broadcast_to(columns[:, :, None], (2, 32, 128)),
+            labels=seg_labels,
+            depth=depth_target,
+            normal=normal_target,
+            boxes=crop_boxes,
+        )
+    )
+    features = jnp.concatenate([middle.features[:, :64], middle.features[:, 64:]], axis=0)
+    sums = middle.head_sums
+    losses = jnp.stack([sums[64, 0], sums[83, 0], sums[84, 0] + sums[85, 0]]) / count
+
+    back = run_pyramid_backward(
+        dict(
+            grad_branches=middle.grad_branches,
+            w_pyramid=w_pyramid,
+            x=x,
+            trunk=forward.trunk,
+            expanded=forward.expanded,
+            stats_3=forward.stats_3,
+            affine_3=expansion_norm_params,
+            mask=forward.mask,
+            grad_pooled=middle.grad_pooled,
+            grad_project=middle.grad_project,
+            grad_pool=middle.grad_pool,
+            boxes=crop_boxes,
+        )
+    )
+    last = run_bottleneck_backward(
+        dict(
+            grad_expanded=back.grad_expanded,
+            shortcut=back.shortcut,
+            half_pyramid=back.half_pyramid,
+            half_project=back.half_project,
+            half_pool=back.half_pool,
+            x=x,
+            hidden=forward.hidden,
+            hidden_two=forward.hidden_two,
+            w_expand=conv_expand,
+            w_dilated=conv_dilated,
+            w_reduce=forward.w_reduce,
+            dilated=forward.dilated,
+            stats_2=forward.stats_2,
+            affine_2=dilated_norm_params,
+            reduced=forward.reduced,
+            stats_1=forward.stats_1,
+            affine_1=reduction_norm_params,
+            mask=forward.mask,
+            boxes=crop_boxes,
+        )
+    )
+    odd = lax.rem(lax.axis_index("batch"), 2)
+
+    def in_order(blocks):
+        return jnp.where(odd == 0, blocks, blocks[::-1])
+
+    project_rows = in_order(last.own_project).reshape(64, 6, 64)[:, :5]
+    grad_project = jnp.where(odd == 0, project_rows[:, :, :32], project_rows[:, :, 32:])
+    grad_reduce = in_order(last.own_reduce).reshape(128, 256).T
+    return (
+        features.reshape(1, 12, 128, 64),
+        jnp.sum(task_weights * losses + log_vars),
+        last.grad_input.reshape(1, 12, 128, 512),
+        grad_reduce,
+        last.sum_dilated.reshape(3, 3, 64, 128),
+        last.sum_expand,
+        last.norm_1[:2],
+        last.norm_2[:2],
+        back.norm_3[:2],
+        last.grad_point,
+        last.grad_rates.reshape(3, 3, 3, 64, 256),
+        last.sum_pool,
+        middle.norm_b[:2].reshape(2, 4, 64),
+        middle.norm_pool[:2, :64],
+        grad_project,
+        middle.norm_p[:2, :64],
+        sums[:22, :].T,
+        sums[32:54, 0],
+        1.0 - task_weights * losses,
+    )
 
 
 def local(
@@ -525,4 +2036,6 @@
         P(),
         P(),
     )
-    return jax.shard_map(local, mesh=mesh, in_specs=in_specs, out_specs=out_specs, check_vma=False)
+    small = (mesh.shape["branch"], mesh.shape["rows"], mesh.shape["batch"]) == (4, 2, 4)
+    body = fast_local if small else local
+    return jax.shard_map(body, mesh=mesh, in_specs=in_specs, out_specs=out_specs, check_vma=False)

time: 1560 us -> 465 us (0.30)
  waiting for transfers between devices: 864 us -> 0 us
  Pallas kernels: 0 us -> 424 us
  blocking collectives: 265 us -> 0 us
  matrix products: 205 us -> 0 us
  other arithmetic: 85.3 us -> 8.74 us
  local copies, waits for them, and re-layouts: 90.9 us -> 29.1 us
  between operations: 25.7 us -> 2.16 us
  starting transfers between devices: 16.9 us -> 0 us
    reduce_scatter x9 -> x0, waiting for transfers between devices: 548 us -> none  [the longest x1 250 us: local(): lax.psum_scatter(grad_rates_local, ('rows', 'batch'), scatter_dimension=4...]
    pallas_call x0 -> x4, Pallas kernels: none -> 424 us  [call_kernel(): pl.pallas_call(kernel, out_shape=[jax.ShapeDtypeStruct(s, d) for s, d in...]
    psum x17 -> x0, blocking collectives: 252 us -> none  [the longest x5 85.1 us: norm_ahead_pass(): summed = lax.psum(jnp.sum(tensor * weight, axis=0), ('rows', 'batch'))]
    all_gather x5 -> x0, waiting for transfers between devices: 242 us -> none  [widen(): return lax.all_gather(tensor, 'branch', axis=3, tiled=True)]
    dot_general x72 -> x0, matrix products: 205 us -> none  [the longest x23 111 us: forward_dot(): return jnp.dot(lhs_arr, rhs_arr, preferred_element_type=jnp.float32)]
    unnamed x20 -> x0, waiting for transfers between devices: 72 us -> none
    unnamed x385 -> x43, local copies, waits for them, and re-layouts: 53.8 us -> 10 us
    another operation x13 -> x1, other arithmetic: 26.9 us -> 0.01 us  [fast_local(): columns = jnp.pad(jnp.stack([head_bias, by_row / count]), ((0, 0), (0, 10)))]
  transfers between devices with their start and end apart: 25 -> 0, of which waited for: 16 -> 0; matrix products, arithmetic and copies ran while one was open for 12% -> 0% of each run, Pallas kernels for 0% -> 0%
where the time goes in v2:
time: 465 us; the launch traced here: 464 us
  Pallas kernels  424 us (91%)
  local copies, waits for them, and re-layouts  29.1 us (6%)
  other arithmetic  8.74 us (2%)
    pallas_call x4, Pallas kernels, call_kernel(): pl.pallas_call(kernel, out_shape=[jax.ShapeDtypeStruct(s, d) for s, d in...  424 us
    unnamed x43, local copies, waits for them, and re-layouts  10 us

profile of v2, /device:TPU:0, one launch (start us, length us, event | category | flops | bytes accessed | tf_op | source)
XLA Modules:
  0.0 464.1 jit_solution(242081688546664400)
XLA Ops:
  0.7 1.6 copy.55
  2.3 98.6 %bottleneck.1 = (f32[1536,128]{1,0:T(8,128)}, bf16[4,512,128]{2,1,0:T(8,128)(2,1)}, bf16[13,4,64,512]{3,2,1,0:T(8,128)(2,1)}, bf16[4,64,1280]{2,1,0:T(8,128)(2,1...) custom-call(bf16[1536,512]{1,0:T(8,128)(2,1)} %bitcast.29, ...), custom_call_target="tpu_custom_call" | custom-call | tf_op jit(solution)/shard_map/bottleneck/pallas_call | solution.py:433
  102.8 0.7 convert_reduce_fusion
  103.5 1.4 fusion
  104.9 0.7 broadcast_in_dim.14.refs_8_
  108.0 0.7 maximum_maximum_fusion.refs_4_
  108.7 0.7 reshape.112.refs_3_
  109.3 113.4 %pyramid.1 = (bf16[768,128]{1,0:T(8,128)(2,1)}, f32[8,128]{1,0:T(8,128)}, bf16[8,32,384]{2,1,0:T(8,128)(2,1)}, bf16[8,64,256]{2,1,0:T(8,128)(2,1)}, f32[8,256]{1...) custom-call(bf16[1536,512]{1,0:T(8,128)(2,1)} %get-tuple-element.57.refs_0_.re, ...), custom_call_target="tpu_custom_call" | custom-call | tf_op jit(solution)/shard_map/pyramid/pallas_call | solution.py:433
  222.7 65.3 %pyramid_back.1 = (f32[1536,512]{1,0:T(8,128)}, bf16[1536,512]{1,0:T(8,128)(2,1)}, f32[8,512]{1,0:T(8,128)}, bf16[4,16,32,512]{3,2,1,0:T(8,128)(2,1)}, bf16[4,32...) custom-call(bf16[1536,256]{1,0:T(8,128)(2,1)} %get-tuple-element.63.refs_0_, bf16[13,256,512]{2,1,0:T(8,128)(2,1)} %bitcast.33, ...), custom_call_target="tpu_custom_call" | custom-call | tf_op jit(solution)/shard_map/pyramid_back/pallas_call | solution.py:433
  288.1 146.9 %bottleneck_back.1 = (f32[1536,512]{1,0:T(8,128)}, f32[8,128]{1,0:T(8,128)}, f32[8,128]{1,0:T(8,128)}, f32[27,64,256]{2,1,0:T(8,128)}, f32[64,256]{1,0:T(8,128)}...) custom-call(bf16[1536,512]{1,0:T(8,128)(2,1)} %get-tuple-element.69., ...), custom_call_target="tpu_custom_call" | custom-call | tf_op jit(solution)/shard_map/bottleneck_back/pallas_call | solution.py:433
  435.0 1.0 reverse_select_fusion.1
  436.1 0.8 slice_select_fusion
  436.9 1.8 copy.54
  438.7 1.0 reverse_select_fusion
  439.7 0.8 copy.52
  440.5 1.2 slice.77
  441.7 1.2 slice.78
  442.9 1.3 slice.79
  444.3 1.3 fusion.2
  446.9 2.5 broadcast_subtract_fusion
  450.0 1.1 fusion.1
  451.2 0.8 copy.53
  452.1 1.3 slice_bitcast_fusion
  453.4 1.3 slice_reduce_fusion
  454.8 0.7 slice.80
  455.5 0.7 reshape.119
  456.1 1.2 slice.81
  457.4 1.2 slice.84
  458.6 1.7 copy.62
  460.3 0.7 copy.63
  461.0 0.7 copy.64
  462.3 1.2 copy.66
  (46 shorter events, 6.4 us)
Async XLA Ops:
  2.2 98.7 %copy-start.14 = (f32[3]{0:T(128)S(1)}, f32[3]{0:T(128)}, u32[]{:S(2)}) copy-start(f32[3]{0:T(128)} %param.37) | copy-start | bytes 40
  2.3 100.6 %copy-start.4 = (s32[4,4]{1,0:T(4,128)S(1)}, s32[4,4]{1,0:T(4,128)}, u32[]{:S(2)}) copy-start(s32[4,4]{1,0:T(4,128)} %refs_18_.1) | copy-start | bytes 196
  2.3 102.6 %copy-start.15 = (f32[22]{0:T(128)S(1)}, f32[22]{0:T(128)}, u32[]{:S(2)}) copy-start(f32[22]{0:T(128)} %param.36) | copy-start | bytes 268
  2.3 103.3 %copy-start.7 = (f32[1,2,12,128]{3,1,2,0:T(2,128)S(1)}, f32[1,2,12,128]{3,1,2,0:T(2,128)}, u32[]{:S(2)}) copy-start(f32[1,2,12,128]{3,1,2,0:T(2,128)} %param.41) | copy-start | bytes 36868
  2.3 103.9 %copy-start.8 = (bf16[256,22]{0,1:T(8,128)(2,1)S(1)}, bf16[256,22]{0,1:T(8,128)(2,1)}, u32[]{:S(2)}) copy-start(bf16[256,22]{0,1:T(8,128)(2,1)} %param.35) | copy-start | bytes 33796
  2.3 104.5 %copy-start.9 = (s32[1,12,128]{2,0,1:T(1,128)S(1)}, s32[1,12,128]{2,0,1:T(1,128)}, u32[]{:S(2)}) copy-start(s32[1,12,128]{2,0,1:T(1,128)} %param.39) | copy-start | bytes 18436
  2.3 105.1 %copy-start.10 = (f32[1,12,128]{2,0,1:T(1,128)S(1)}, f32[1,12,128]{2,0,1:T(1,128)}, u32[]{:S(2)}) copy-start(f32[1,12,128]{2,0,1:T(1,128)} %param.40) | copy-start | bytes 18436
  2.3 105.7 %copy-start.12 = (f32[2,64]{1,0:T(2,128)S(1)}, f32[2,64]{1,0:T(2,128)}, u32[]{:S(2)}) copy-start(f32[2,64]{1,0:T(2,128)} %param.32) | copy-start | bytes 1540
  2.3 105.7 %copy-start.13 = (f32[2,64]{1,0:T(2,128)S(1)}, f32[2,64]{1,0:T(2,128)}, u32[]{:S(2)}) copy-start(f32[2,64]{1,0:T(2,128)} %param.34) | copy-start | bytes 1540
  2.3 106.4 %copy-start.11 = (f32[2,4,64]{2,1,0:T(4,128)S(1)}, f32[2,4,64]{2,1,0:T(4,128)}, u32[]{:S(2)}) copy-start(f32[2,4,64]{2,1,0:T(4,128)} %param.31) | copy-start | bytes 6148
  436.0 22.6 %copy-start = (f32[1536,512]{1,0:T(8,128)S(1)}, f32[1536,512]{1,0:T(8,128)}, u32[]{:S(2)}) copy-start(f32[1536,512]{1,0:T(8,128)} %get-tuple-element.81) | copy-start | bytes 9437188
  458.6 1.7 copy-start.2
  458.6 2.4 copy-start.3
  458.6 3.1 copy-start.6
  458.6 3.7 copy-start.1
  461.0 2.5 copy-start.5

commit v3 on v2

--- a/solution.py
+++ b/solution.py
@@ -228,37 +228,49 @@
         copy.wait()
 
 
-def statistics(net, value_ref, mask_ref, outgoing, incoming, counted, folded=False, extra=None):
+def pack(outgoing, first, second, extra=None):
+    for i in range(first.shape[1] // 128):
+        outgoing[2 * i : 2 * i + 1, :] = first[:, i * 128 : i * 128 + 128]
+        outgoing[2 * i + 1 : 2 * i + 2, :] = second[:, i * 128 : i * 128 + 128]
+    if extra is not None:
+        outgoing[4:5, :] = extra
+
+
+def unpack(incoming, width):
+    count = width // 128
+    firsts = [incoming[:, 2 * i, :] for i in range(count)]
+    seconds = [incoming[:, 2 * i + 1, :] for i in range(count)]
+    return jnp.concatenate(firsts, axis=1), jnp.concatenate(seconds, axis=1)
+
+
+def statistics(
+    net, value_ref, mask_ref, counts, outgoing, incoming, counted, folded=False, extra=None
+):
     total, width = value_ref.shape
     same = fold if folded else (lambda row: row)
-    first, number = column_sums(
-        lambda at: (value_ref[at, :] * wide(mask_ref[at, :], width), wide(mask_ref[at, :], width)),
-        total,
-        width,
-        2,
-    )
-    first, number = same(first), same(number)
-    centre = first / jnp.maximum(number, 1.0)
+    (first,) = column_sums(
+        lambda at: (value_ref[at, :] * wide(mask_ref[at, :], width),), total, width, 1
+    )
+    first = same(first)
+    own = jnp.sum(jnp.where(lax.broadcasted_iota(jnp.int32, (8, 128), 0) == net.slot, counts, 0.0), axis=0, keepdims=True)
+    centre = first / jnp.maximum(wide(own, width), 1.0)
 
     def squares(at):
         gap = value_ref[at, :] - centre
         return (gap * gap * wide(mask_ref[at, :], width),)
 
     second = same(column_sums(squares, total, width, 1)[0])
-    outgoing[0:1, :] = first
-    outgoing[1:2, :] = second
-    outgoing[2:3, :] = number
-    if extra is not None:
-        outgoing[3:4, :] = extra
+    pack(outgoing, first, second, extra)
     exchange(net, outgoing, incoming)
-    firsts, seconds, numbers = incoming[:, 0, :], incoming[:, 1, :], incoming[:, 2, :]
+    firsts, seconds = unpack(incoming, width)
+    numbers = wide(counts, width)
     mean = jnp.sum(firsts, axis=0, keepdims=True) / counted
     drift = firsts / jnp.maximum(numbers, 1.0) - mean
     variance = jnp.sum(seconds + numbers * drift * drift, axis=0, keepdims=True) / counted
     return mean, lax.rsqrt(variance + EPS)
 
 
-def gather_blocks(net, part, rows):
+def gather_blocks(net, part, rows, meanwhile=None):
     pieces, size = 4, rows // 4
     own, side, over = net.m, net.m ^ 1, net.m ^ 2
 
@@ -279,6 +291,8 @@
         to_over[i].wait_recv()
         if i < pieces // 2:
             passed.append(net.send(part(over, at(j)), part(over, at(j)), net.side))
+    if meanwhile is not None:
+        meanwhile()
     for copy in to_side + to_over:
         copy.wait_send()
     for copy in passed:
@@ -343,14 +357,10 @@
     bias, gain = column_sums(
         lambda at: (grad_ref[at, :], grad_ref[at, :] * normed(at)), total, width, 2
     )
-    outgoing[0:1, :] = same(bias)
-    outgoing[1:2, :] = same(gain)
-    if extra is not None:
-        outgoing[2:3, :] = extra
+    pack(outgoing, same(bias), same(gain), extra)
     exchange(net, outgoing, incoming, meanwhile)
-    bias = jnp.sum(incoming[:, 0, :], axis=0, keepdims=True)
-    gain = jnp.sum(incoming[:, 1, :], axis=0, keepdims=True)
-    return bias, gain
+    biases, gains = unpack(incoming, width)
+    return jnp.sum(biases, axis=0, keepdims=True), jnp.sum(gains, axis=0, keepdims=True)
 
 
 def keep_rows(ref, first, second):
@@ -428,18 +438,17 @@
 
     def kernel(*refs):
         k = types.SimpleNamespace(**dict(zip(names, refs)))
-        body(Net(refs[-2], refs[-1]), k)
+        body(Net(refs[-2], refs[-1]) if sems else None, k)
 
     results = pl.pallas_call(
         kernel,
         out_shape=[jax.ShapeDtypeStruct(s, d) for s, d in outs.values()],
         in_specs=[places.get(name, vmem) for name in args],
         out_specs=[places.get(name, vmem) for name in outs],
-        scratch_shapes=list(scratch.values())
-        + [pltpu.SemaphoreType.DMA((sems,)), pltpu.SemaphoreType.DMA((sems,))],
+        scratch_shapes=list(scratch.values()) + [pltpu.SemaphoreType.DMA((sems,))] * (2 if sems else 0),
         name=name,
         compiler_params=pltpu.CompilerParams(
-            collective_id=number, has_side_effects=True, vmem_limit_bytes=VMEM_LIMIT
+            collective_id=number, has_side_effects=bool(sems), vmem_limit_bytes=VMEM_LIMIT
         ),
     )(*args.values())
     return types.SimpleNamespace(**dict(zip(outs, results)))
@@ -452,10 +461,21 @@
     return total.astype(F32)
 
 
-def exchange_scratch(label, width):
+def tile_counts(net, boxes):
+    slot = lax.broadcasted_iota(jnp.int32, (8, 128), 0)
+    result = jnp.zeros((8, 128), F32)
+    for s in range(8):
+        top, height, width = boxes[s % 4, 0], boxes[s % 4, 2], boxes[s % 4, 3]
+        first, last = (s // 4) * 12, (s // 4) * 12 + 12
+        rows = jnp.minimum(top + height, last) - jnp.maximum(top, first)
+        result = jnp.where(slot == s, (jnp.maximum(rows, 0) * width).astype(F32), result)
+    return result
+
+
+def exchange_scratch(label):
     return {
-        f"out_{label}": pltpu.VMEM((8, width), F32),
-        f"in_{label}": pltpu.VMEM((8, 8, width), F32),
+        f"out_{label}": pltpu.VMEM((8, 128), F32),
+        f"in_{label}": pltpu.VMEM((8, 8, 128), F32),
     }
 
 
@@ -493,7 +513,7 @@
 
 
 def bottleneck_forward(net, k):
-    counted = pixel_count(k.boxes)
+    counted, counts = pixel_count(k.boxes), tile_counts(net, k.boxes)
     loads = load_taps(k)
     own_reduce = pltpu.make_async_copy(
         k.conv_reduce.at[lane_block(net.m, 512)], k.w_reduce.at[net.m], k.local_sems.at[9]
@@ -561,7 +581,7 @@
                 late.append(net.send(src, dst, peer))
 
     spread_weights("edge")
-    mean, inverse = statistics(net, k.reduced, k.mask, k.out_1, k.in_1, counted)
+    mean, inverse = statistics(net, k.reduced, k.mask, counts, k.out_1, k.in_1, counted)
     keep_rows(k.stats_1, mean, inverse)
 
     def activate_1(at):
@@ -599,7 +619,7 @@
         return carry
 
     lax.fori_loop(0, 12, add_columns, 0)
-    mean_2, inverse_2 = statistics(net, k.dilated, k.mask, k.out_2, k.in_2, counted)
+    mean_2, inverse_2 = statistics(net, k.dilated, k.mask, counts, k.out_2, k.in_2, counted)
     keep_rows(k.stats_2, mean_2, inverse_2)
 
     def activate_2(at):
@@ -614,7 +634,7 @@
         k.expanded[at, :] = mm(k.hidden_two[at, :], k.w_expand[...])
 
     each_rows(1536, 384, expand_rows)
-    mean_3, inverse_3 = statistics(net, k.expanded, k.mask, k.out_3, k.in_3, counted)
+    mean_3, inverse_3 = statistics(net, k.expanded, k.mask, counts, k.out_3, k.in_3, counted)
     keep_rows(k.stats_3, mean_3, inverse_3)
     for copy in late:
         copy.wait()
@@ -660,9 +680,9 @@
             **scatter_scratch("sum", 1536, 128),
             left=pltpu.VMEM((12, 144, 128), F32),
             right=pltpu.VMEM((12, 144, 128), F32),
-            **exchange_scratch(1, 128),
-            **exchange_scratch(2, 128),
-            **exchange_scratch(3, 512),
+            **exchange_scratch(1),
+            **exchange_scratch(2),
+            **exchange_scratch(3),
             local_sems=pltpu.SemaphoreType.DMA((16,)),
         ),
         96,
@@ -679,7 +699,7 @@
 
 
 def pyramid_forward(net, k):
-    counted = pixel_count(k.boxes)
+    counted, counts = pixel_count(k.boxes), tile_counts(net, k.boxes)
     area = (k.boxes[net.z, 2] * k.boxes[net.z, 3]).astype(F32)
     near = [
         (lax.rem(net.m + a, 4), lax.rem(net.r + b, 2), net.z)
@@ -688,6 +708,14 @@
         if a or b
     ]
     greet(net.group + [peer for i, peer in enumerate(near) if i])
+
+    for b in range(4):
+        k.affine_b[0:2, b * 64 : b * 64 + 64] = k.branch_norms[:, b, :]
+    for i in range(2):
+        k.affine_p[0:2, i * 64 : i * 64 + 64] = k.norm_project[...]
+        k.affine_p[2:4, i * 64 : i * 64 + 64] = k.norm_pooling[...]
+    k.head_rows[...] = jnp.zeros((32, 256), F32)
+    k.head_rows[0:22, :] = k.head_weight[...].astype(F32).T
 
     (own_sum,) = column_sums(
         lambda at: (k.trunk[at, :].astype(F32) * wide(k.mask[at, :], 512),), 1536, 512, 1
@@ -770,9 +798,9 @@
         k.pooled[:, b * 512 : b * 512 + 512] = jnp.broadcast_to(pooled, (16, 512)).astype(BF16)
     pool_conv = mm_t(k.pooled[...], k.w_pool[...])[0:1, :]
     mean, inverse = statistics(
-        net, k.branches, k.mask, k.out_1, k.in_1, counted, extra=wide(pool_conv, 256)
-    )
-    every = k.in_1[0:4, 3, 0:128]
+        net, k.branches, k.mask, counts, k.out_1, k.in_1, counted, extra=pool_conv
+    )
+    every = k.in_1[0:4, 4, :]
     pool_mean = jnp.sum(every, axis=0, keepdims=True) / 4.0
     pool_gap = every - pool_mean
     pool_inverse = lax.rsqrt(jnp.sum(pool_gap * pool_gap, axis=0, keepdims=True) / 4.0 + EPS)
@@ -814,7 +842,7 @@
     each_rows(768, 128, pair_mask)
     sum_scatter(net, k.part_2, scatter_refs(k, "sum2"), k.projected)
     mean_p, inverse_p = statistics(
-        net, k.projected, k.mask_pairs, k.out_2, k.in_2, counted, folded=True
+        net, k.projected, k.mask_pairs, counts, k.out_2, k.in_2, counted, folded=True
     )
     gain_p, bias_p = k.affine_p[0:1, :], k.affine_p[1:2, :]
 
@@ -842,8 +870,14 @@
     class_row = lax.broadcasted_iota(jnp.int32, (32, 512), 0)
     is_class, is_depth = class_row < 19, class_row == 19
     is_normal = (class_row == 20) | (class_row == 21)
-    bias_column = wide(k.head_columns[0], 512)
-    weight_column = wide(k.head_columns[1], 512)
+    tile_row = lax.broadcasted_iota(jnp.int32, (32, 128), 0)
+    bias_column = jnp.zeros((32, 128), F32)
+    for c in range(22):
+        bias_column = jnp.where(tile_row == c, k.head_bias[c], bias_column)
+    task = [jnp.exp(jnp.full((32, 128), -k.log_vars[t], F32)) / counted for t in range(3)]
+    weight_column = jnp.where(tile_row < 19, task[0], jnp.where(tile_row == 19, task[1], task[2]))
+    bias_column, weight_column = wide(bias_column, 512), wide(weight_column, 512)
+    k.head[...] = k.head_rows[...].astype(BF16)
     top_row, left_edge = k.boxes[net.z, 0], k.boxes[net.z, 1]
     bottom_row, right_edge = top_row + k.boxes[net.z, 2], left_edge + k.boxes[net.z, 3]
     lane = lax.broadcasted_iota(jnp.int32, (1, 512), 1)
@@ -883,13 +917,16 @@
         k.grad_logits[0:32, at] = high
         k.grad_logits[32:64, at] = (grad - high.astype(F32)).astype(BF16)
     head_terms = mm(k.grad_logits[...], k.wide_features[...])
-    k.out_head[0:32, :] = head_terms[0:32, :] + head_terms[32:64, :]
-    k.out_head[32:64, :] = jnp.broadcast_to(bias_sums, (32, 256))
-    k.out_head[64:96, :] = jnp.broadcast_to(loss_sums, (32, 256))
-    head_copies = [net.send(k.out_head, k.in_head.at[net.slot], peer) for peer in net.group]
-    k.in_head[net.slot] = k.out_head[...]
-
-    own_head = k.head[:, lane_block(net.m // 2)].astype(F32)
+    k.out_head[:, 0:256] = head_terms[0:32, :] + head_terms[32:64, :]
+    first_lane = lax.broadcasted_iota(jnp.int32, (32, 128), 1) == 0
+    k.out_head[:, 256:384] = jnp.where(first_lane, bias_sums, loss_sums)
+    quarter = pl.ds(pl.multiple_of(net.m * 8, 8), 8)
+    head_copies = [
+        net.send(k.out_head.at[quarter], k.in_head.at[net.slot], peer) for peer in net.group
+    ]
+    k.in_head[net.slot] = k.out_head[quarter, :]
+
+    own_head = k.head_rows[:, lane_block(net.m // 2)]
     own_head = jnp.where(odd, pltpu.roll(own_head, 64, 1), own_head)
     own_head = jnp.where(low_128[0:32, :], own_head, 0.0)
     head_low = jnp.concatenate([own_head, own_head], axis=0).astype(BF16)
@@ -922,7 +959,8 @@
     for i, term in enumerate(split_three(pixel_sum)):
         terms = jnp.where(row_16 == i, term.astype(F32), terms)
     terms = terms.astype(BF16)
-    pool_grad = jnp.sum(mm(terms, k.w_slot[...]), axis=0, keepdims=True)
+    tall = jnp.concatenate([terms] * 8, axis=0)
+    pool_grad = jnp.sum(mm(tall, k.w_slot[...]), axis=0, keepdims=True) * 0.125
 
     def project_gradient():
         for b in range(2):
@@ -943,12 +981,12 @@
         normed_branch,
         k.out_4,
         k.in_4,
-        extra=wide(pool_grad, 256),
+        extra=pool_grad,
         meanwhile=project_gradient,
     )
     keep_rows(k.norm_b, gain_grad_b, bias_grad_b)
 
-    pool_terms = k.in_4[0:4, 2, 0:128] + k.in_4[4:8, 2, 0:128]
+    pool_terms = k.in_4[0:4, 4, :] + k.in_4[4:8, 4, :]
     pool_terms = pool_terms * slope(pool_u)
     pool_bias_grad = jnp.sum(pool_terms, axis=0, keepdims=True)
     pool_gain_grad = jnp.sum(pool_terms * pool_normed, axis=0, keepdims=True)
@@ -979,13 +1017,19 @@
         grad = gain_b * k.grad_b[at, :] - shared * (bias_grad_b + normed_branch(at) * gain_grad_b)
         k.grad_branches[at, :] = (inverse * grad).astype(BF16)
 
-    each_rows(1536, 64, back_branches)
     for copy in back_copies:
         copy.wait()
     k.grad_pooled[...] = (k.out_back[net.m] + k.in_back[1] + k.in_back[2] + k.in_back[3]) / area
     for copy in head_copies:
         copy.wait()
-    k.head_sums[...] = jnp.sum(k.in_head[...], axis=0)
+    k.head_sums[quarter, :] = jnp.sum(k.in_head[...], axis=0)
+    head_copies = [
+        net.send(k.head_sums.at[quarter], k.head_sums.at[quarter], (lax.rem(net.m + a, 4), net.r, net.z))
+        for a in range(1, 4)
+    ]
+    each_rows(1536, 64, back_branches)
+    for copy in head_copies:
+        copy.wait()
 
 
 def run_pyramid(args):
@@ -1003,9 +1047,13 @@
             norm_pool=((8, 128), F32),
             grad_branches=((1536, 256), BF16),
             grad_pooled=((8, 512), F32),
-            head_sums=((96, 256), F32),
+            head_sums=((32, 384), F32),
         ),
         dict(
+            affine_b=pltpu.VMEM((8, 256), F32),
+            affine_p=pltpu.VMEM((8, 128), F32),
+            head_rows=pltpu.VMEM((32, 256), F32),
+            head=pltpu.VMEM((32, 256), BF16),
             pooled=pltpu.VMEM((16, 2048), BF16),
             spatial=pltpu.VMEM((1536, 256), BF16),
             grad_projected=pltpu.VMEM((1536, 256), BF16),
@@ -1028,19 +1076,20 @@
             gathered=pltpu.VMEM((4, 768, 128), BF16),
             wide_features=pltpu.VMEM((1536, 256), BF16),
             grad_logits=pltpu.VMEM((64, 1536), BF16),
-            out_head=pltpu.VMEM((96, 256), F32),
-            in_head=pltpu.VMEM((8, 96, 256), F32),
+            out_head=pltpu.VMEM((32, 384), F32),
+            in_head=pltpu.VMEM((8, 8, 384), F32),
             grad_p=pltpu.VMEM((768, 128), F32),
             gathered_grad=pltpu.VMEM((4, 768, 128), BF16),
             grad_b=pltpu.VMEM((1536, 256), F32),
             out_back=pltpu.VMEM((4, 8, 512), F32),
             in_back=pltpu.VMEM((4, 8, 512), F32),
-            **exchange_scratch(1, 256),
-            **exchange_scratch(2, 128),
-            **exchange_scratch(3, 128),
-            **exchange_scratch(4, 256),
+            **exchange_scratch(1),
+            **exchange_scratch(2),
+            **exchange_scratch(3),
+            **exchange_scratch(4),
         ),
         96,
+        smem=("boxes", "head_bias", "log_vars"),
     )
 
 
@@ -1055,49 +1104,185 @@
         target[z] = total.astype(target.dtype)
 
 
+def z_copies(net, source, target):
+    copies = []
+    for d in (1, 2, 3):
+        i = net.count
+        net.count += 1
+        there = lax.rem(net.z + d, 4)
+        copies.append(
+            pltpu.make_async_remote_copy(
+                src_ref=source.at[there],
+                dst_ref=target.at[d - 1],
+                send_sem=net.send_sems.at[i],
+                recv_sem=net.recv_sems.at[i],
+                device_id=(net.m, net.r, there),
+                device_id_type=MESH,
+            )
+        )
+    return copies
+
+
+def along_z(net, source, target):
+    copies = z_copies(net, source, target)
+    for copy in copies:
+        copy.start()
+    return copies
+
+
+def finish_z(net, half, arrived):
+    return half[net.z].astype(F32) + sum(arrived[d].astype(F32) for d in range(3))
+
+
+def add_z(net, half, arrived, target):
+    def body(i, carry):
+        total = half[net.z, i].astype(F32)
+        for d in range(3):
+            total = total + arrived[d, i].astype(F32)
+        target[i] = total.astype(BF16)
+        return carry
+
+    lax.fori_loop(0, 16, body, 0)
+
+
 def pyramid_backward(net, k):
     counted = pixel_count(k.boxes)
     greet([net.side, net.over] + net.group)
     k.blocks[net.m] = k.grad_branches[...]
-    gather_blocks(net, lambda b, at: k.blocks.at[b, at], 1536)
-    beside = net.send(k.blocks.at[:, :, pl.ds(0, 128)], k.other, net.core)
-    zero_margins(k.cells, 40, 128)
+    small = [
+        core_halves(net, k.grad_project, k.core_project),
+        core_halves(net, k.grad_pool, k.core_pool),
+    ]
+    for c in range(4):
+        zero_margins(k.cells.at[c], 40, 128)
 
     def rows_of(i, size=384):
         return pl.ds(pl.multiple_of(i * size, 128), size)
 
-    def taps(source, lane, second, rate, base):
+    low = lax.broadcasted_iota(jnp.int32, (128, 128), 1) < 64
+    near = net.m // 2
+    far = 1 - near
+    mine_first = net.r == near
+    mine_second = net.r == far
+
+    def both(source, pair_of, i, lane):
+        at = slice(lane * 128, lane * 128 + 128)
+        left = source[2 * pair_of, rows_of(i, 128), at].astype(F32)
+        right = source[2 * pair_of + 1, rows_of(i, 128), at].astype(F32)
+        first = jnp.where(low, left, pltpu.roll(right, 64, 1))
+        return first, jnp.where(low, pltpu.roll(left, 64, 1), right)
+
+    def shift_rows(pair_of, i, cell, rate, base):
+        for j in range(3):
+            start = 40 - rate * (j - 1)
+            block = k.cells[cell, i, start : start + 128, :].astype(BF16)
+            k.shifts[base + j, rows_of(i, 128), lane_block(pair_of)] = block
+
+    def build(pair_of):
         def fill(i, carry):
-            blocks = [
-                source[b, rows_of(i, 128), lane * 128 : lane * 128 + 128].astype(F32)
-                for b in range(4)
-            ]
-            k.cells[i, 40:168, :] = unpair(blocks)[second]
+            point, first = both(k.blocks, pair_of, i, 0)
+            k.shifts[0, rows_of(i, 128), lane_block(pair_of)] = point.astype(BF16)
+            second, third = both(k.blocks, pair_of, i, 1)
+            k.cells[0, i, 40:168, :] = first
+            k.cells[1, i, 40:168, :] = second
+            k.cells[2, i, 40:168, :] = third
             return carry
 
         lax.fori_loop(0, 12, fill, 0)
 
-        def cut(i, carry):
-            for j in range(3):
-                start = 40 - rate * (j - 1)
-                k.shifts[base + j, rows_of(i, 128), :] = k.cells[i, start : start + 128, :].astype(
-                    BF16
-                )
+        def spread(i, carry):
+            for cell, rate, base in ((0, 12, 1), (1, 24, 4), (2, 36, 7)):
+                shift_rows(pair_of, i, cell, rate, base)
             return carry
 
-        lax.fori_loop(0, 12, cut, 0)
-
-    def point(i, carry):
-        blocks = [k.blocks[b, rows_of(i, 128), 0:128].astype(F32) for b in range(4)]
-        k.shifts[0, rows_of(i, 128), :] = unpair(blocks)[0].astype(BF16)
-        return carry
-
-    lax.fori_loop(0, 12, point, 0)
-    taps(k.blocks, 0, 1, 12, 1)
-    taps(k.blocks, 1, 0, 24, 4)
-    taps(k.blocks, 1, 1, 36, 7)
-    beside.wait()
-    taps(k.other, 0, 1, 12, 10)
+        lax.fori_loop(0, 12, spread, 0)
+
+    def build_edge(pair_of):
+        def fill(i, carry):
+            k.cells[3, i, 40:168, :] = both(k.other, pair_of, i, 0)[1]
+            return carry
+
+        lax.fori_loop(0, 12, fill, 0)
+
+        def spread(i, carry):
+            shift_rows(pair_of, i, 3, 12, 10)
+            return carry
+
+        lax.fori_loop(0, 12, spread, 0)
+
+    def weight_gradients(pair_of):
+        owners = pl.ds(4 * pair_of, 4)
+
+        def run(start, stop, shift):
+            def body(t, carry):
+                grad = tm_m(k.shifts[t, :, lane_block(pair_of)], k.trunk[...])
+                k.grad_pyramid[owners, t + shift] = grad.reshape(4, 32, 512).astype(BF16)
+                return carry
+
+            lax.fori_loop(start, stop, body, 0)
+
+        run(0, 1, 0)
+        run(1, 4, 3)
+        run(4, 10, 6)
+        run(10, 13, net.r * 6 - 9)
+        for j in range(3):
+            k.grad_pyramid[owners, 7 - net.r * 6 + j] = jnp.zeros((4, 32, 512), BF16)
+
+    def beside(pair_of):
+        view = (pl.ds(2 * pair_of, 2), slice(None), pl.ds(0, 128))
+        return net.send(k.blocks.at[view], k.other.at[pl.ds(2 * pair_of, 2)], net.core)
+
+    def to_core(pair_of):
+        i = net.count
+        net.count += 1
+        return pltpu.make_async_remote_copy(
+            src_ref=k.grad_pyramid.at[pl.ds(4 * pair_of, 4)],
+            dst_ref=k.core_pyramid,
+            send_sem=net.send_sems.at[i],
+            recv_sem=net.recv_sems.at[i],
+            device_id=net.core,
+            device_id_type=MESH,
+        )
+
+    def add_core(pair_of):
+        def body(i, carry):
+            for z in range(4):
+                total = k.grad_pyramid[4 * pair_of + z, i].astype(F32)
+                total = total + k.core_pyramid[z, i].astype(F32)
+                k.half_pyramid[z, i] = total.astype(BF16)
+            return carry
+
+        lax.fori_loop(0, 16, body, 0)
+
+    first_swap = []
+
+    def near_pair():
+        copy = beside(near)
+        build(near)
+        copy.wait()
+        build_edge(near)
+        weight_gradients(near)
+        first_swap.append(to_core(near))
+        pl.when(mine_second)(first_swap[0].start)
+
+    gather_blocks(net, lambda b, at: k.blocks.at[b, at], 1536, meanwhile=near_pair)
+    copy = beside(far)
+    build(far)
+    for swap in small:
+        swap.wait()
+    add_halves(net, k.grad_project, k.core_project, k.half_project)
+    add_halves(net, k.grad_pool, k.core_pool, k.half_pool)
+    small_moves = along_z(net, k.half_project, k.z_project) + along_z(net, k.half_pool, k.z_pool)
+    copy.wait()
+    build_edge(far)
+    z_moves = z_copies(net, k.half_pyramid, k.z_pyramid)
+
+    @pl.when(mine_first)
+    def _():
+        first_swap[0].wait_recv()
+        add_core(near)
+        for move_ in z_moves:
+            move_.start()
 
     def trunk_rows(i, carry):
         total = 0.0
@@ -1121,32 +1306,14 @@
 
     each_rows(1536, 32, back_trunk)
 
-    def weight_gradient(t, slot):
-        grad = tm_m(k.shifts[t], k.trunk[...])
-        k.grad_pyramid[:, slot] = grad.reshape(8, 32, 512).astype(BF16)
-
-    def run(low, high, shift):
-        def body(t, carry):
-            weight_gradient(t, t + shift)
-            return carry
-
-        lax.fori_loop(low, high, body, 0)
-
-    swaps = []
-
-    def weight_gradients():
-        weight_gradient(0, 0)
-        run(1, 4, 3)
-        run(4, 10, 6)
-        run(10, 13, net.r * 6 - 9)
-        for j in range(3):
-            k.grad_pyramid[:, 7 - net.r * 6 + j] = jnp.zeros((8, 32, 512), BF16)
-        swaps.append(core_halves(net, k.grad_pyramid, k.core_pyramid))
-        swaps.append(core_halves(net, k.grad_project, k.core_project))
-        swaps.append(core_halves(net, k.grad_pool, k.core_pool))
+    second_swap = to_core(far)
+
+    def far_gradients():
+        weight_gradients(far)
+        pl.when(mine_first)(second_swap.start)
 
     bias_grad, gain_grad = gradient_sums(
-        net, k.shortcut, normed, k.out_1, k.in_1, meanwhile=weight_gradients
+        net, k.shortcut, normed, k.out_1, k.in_1, meanwhile=far_gradients
     )
     keep_rows(k.norm_3, gain_grad, bias_grad)
 
@@ -1156,18 +1323,23 @@
         k.grad_expanded[at, :] = (inverse * grad).astype(BF16)
 
     each_rows(1536, 32, back_expanded)
-    for swap in swaps:
-        swap.wait()
-
-    def add_pyramid(i, carry):
-        for z in range(4):
-            total = k.grad_pyramid[4 * net.r + z, i].astype(F32) + k.core_pyramid[z, i].astype(F32)
-            k.half_pyramid[z, i] = total.astype(BF16)
-        return carry
-
-    lax.fori_loop(0, 16, add_pyramid, 0)
-    add_halves(net, k.grad_project, k.core_project, k.half_project)
-    add_halves(net, k.grad_pool, k.core_pool, k.half_pool)
+    for move_ in small_moves:
+        move_.wait()
+    k.sum_project[...] = finish_z(net, k.half_project, k.z_project)
+    k.sum_pool[...] = finish_z(net, k.half_pool, k.z_pool)
+
+    @pl.when(mine_second)
+    def _():
+        first_swap[0].wait_send()
+        second_swap.wait_recv()
+        add_core(far)
+
+    @pl.when(mine_first)
+    def _():
+        second_swap.wait_send()
+        for move_ in z_moves:
+            move_.wait()
+        add_z(net, k.half_pyramid, k.z_pyramid, k.sum_pyramid)
 
 
 def run_pyramid_backward(args):
@@ -1181,21 +1353,27 @@
             grad_expanded=((1536, 512), BF16),
             norm_3=((8, 512), F32),
             half_pyramid=((4, 16, 32, 512), BF16),
-            half_project=((4, 32, 384), BF16),
-            half_pool=((4, 64, 256), BF16),
+            sum_pyramid=((16, 32, 512), BF16),
+            sum_project=((32, 384), F32),
+            sum_pool=((64, 256), F32),
         ),
         dict(
+            half_project=pltpu.VMEM((4, 32, 384), BF16),
+            half_pool=pltpu.VMEM((4, 64, 256), BF16),
+            z_pyramid=pltpu.VMEM((3, 16, 32, 512), BF16),
+            z_project=pltpu.VMEM((3, 32, 384), BF16),
+            z_pool=pltpu.VMEM((3, 64, 256), BF16),
             grad_pyramid=pltpu.VMEM((8, 16, 32, 512), BF16),
             core_pyramid=pltpu.VMEM((4, 16, 32, 512), BF16),
             core_project=pltpu.VMEM((4, 32, 384), BF16),
             core_pool=pltpu.VMEM((4, 64, 256), BF16),
             blocks=pltpu.VMEM((4, 1536, 256), BF16),
             other=pltpu.VMEM((4, 1536, 128), BF16),
-            cells=pltpu.VMEM((12, 208, 256), F32),
+            cells=pltpu.VMEM((4, 12, 208, 128), F32),
             shifts=pltpu.VMEM((13, 1536, 256), BF16),
-            **exchange_scratch(1, 512),
+            **exchange_scratch(1),
         ),
-        32,
+        48,
     )
 
 
@@ -1211,17 +1389,7 @@
     moves = jnp.logical_not(stays)
     greet([net.side, net.over] + net.group + [owners[1]], (owners[0], moves))
 
-    def along_z(source, target):
-        return [
-            net.send(
-                source.at[lax.rem(net.z + d, 4)],
-                target.at[d - 1],
-                (net.m, net.r, lax.rem(net.z + d, 4)),
-            )
-            for d in (1, 2, 3)
-        ]
-
-    def to_owners(views, arrived, sem):
+    def to_owners(views, arrived, sem, start=True):
         first = pltpu.make_async_remote_copy(
             src_ref=views(0),
             dst_ref=arrived.at[0],
@@ -1232,19 +1400,54 @@
         )
         net.count += 1
         kept = pltpu.make_async_copy(views(0), arrived.at[0], sem)
-        pl.when(moves)(first.start)
-        pl.when(stays)(kept.start)
-        second = net.send(views(1), arrived.at[1], owners[1])
+        i = net.count
+        net.count += 1
+        second = pltpu.make_async_remote_copy(
+            src_ref=views(1),
+            dst_ref=arrived.at[1],
+            send_sem=net.send_sems.at[i],
+            recv_sem=net.recv_sems.at[i],
+            device_id=owners[1],
+            device_id_type=MESH,
+        )
+
+        def begin():
+            pl.when(moves)(first.start)
+            pl.when(stays)(kept.start)
+            second.start()
 
         def wait():
             pl.when(moves)(first.wait)
             pl.when(stays)(kept.wait)
             second.wait()
 
-        return wait
-
-    pyramid_moves = along_z(k.half_pyramid, k.z_pyramid)
-    small_moves = along_z(k.half_project, k.z_project) + along_z(k.half_pool, k.z_pool)
+        if start:
+            begin()
+            return wait
+        return begin, wait
+
+    def lanes_for(i):
+        return lane_block(odd if i == 0 else 1 - odd, 256)
+
+    early = net.r == net.m // 2
+    is_late = net.r == 1 - net.m // 2
+    pyramid_moves = z_copies(net, k.half_pyramid, k.z_pyramid)
+
+    begin_pyramid, wait_pyramid = to_owners(
+        lambda i: k.pyramid_sum.at[:, :, lanes_for(i)], k.own_pyramid, k.local_sems.at[9], False
+    )
+
+    @pl.when(is_late)
+    def _():
+        for move_ in pyramid_moves:
+            move_.start()
+
+    @pl.when(early)
+    def _():
+        k.pyramid_sum[...] = k.sum_pyramid[...]
+        begin_pyramid()
+
+    wait_project = to_owners(lambda i: k.sum_project, k.own_project, k.local_sems.at[10])
 
     def rows_of(i, size=384):
         return pl.ds(pl.multiple_of(i * size, 128), size)
@@ -1255,6 +1458,7 @@
             k.part[b, at, :] = total[:, b * 128 : b * 128 + 128]
 
     each_rows(1536, 384, expand_rows)
+    swaps, late_moves = [], []
 
     def expand_gradient():
         def body(b, carry):
@@ -1263,6 +1467,7 @@
             return carry
 
         lax.fori_loop(0, 4, body, 0)
+        swaps.append(core_halves(net, k.grad_expand, k.core_expand))
 
     sum_scatter(net, k.part, scatter_refs(k, "sum"), k.grad_2, meanwhile=expand_gradient)
 
@@ -1292,7 +1497,22 @@
     def store_2(at, value):
         k.grad_pad[pl.ds(pl.multiple_of(at.start + 512, 128), 128), :] = value
 
-    norm_back(k.grad_2, k.dilated, k.stats_2, k.affine_2, k.out_2, k.in_2, store_2, k.norm_2)
+    def pass_expand():
+        swaps.pop().wait()
+        add_halves(net, k.grad_expand, k.core_expand, k.half_expand)
+        late_moves.extend(along_z(net, k.half_expand, k.z_expand))
+
+    norm_back(
+        k.grad_2,
+        k.dilated,
+        k.stats_2,
+        k.affine_2,
+        k.out_2,
+        k.in_2,
+        store_2,
+        k.norm_2,
+        meanwhile=pass_expand,
+    )
     halo = send_halo(net, k.grad_pad)
     zero_margins(k.cells, 8, 128)
     halo.wait()
@@ -1320,8 +1540,6 @@
         return carry
 
     lax.fori_loop(0, 4, dilated_rows, 0)
-    swaps = []
-
     def dilated_gradient():
         for i in range(3):
 
@@ -1336,22 +1554,23 @@
 
             lax.fori_loop(0, 4, body, 0)
         swaps.append(core_halves(net, k.grad_dilated, k.core_dilated))
-        swaps.append(core_halves(net, k.grad_expand, k.core_expand))
 
     sum_scatter(net, k.part, scatter_refs(k, "sum2"), k.grad_1, meanwhile=dilated_gradient)
 
     def store_1(at, value):
         k.grad_reduced[at, lane_block(net.m)] = value
 
-    late_moves = []
-
     def pass_halves():
-        for swap in swaps:
-            swap.wait()
+        swaps.pop().wait()
         add_halves(net, k.grad_dilated, k.core_dilated, k.half_dilated)
-        add_halves(net, k.grad_expand, k.core_expand, k.half_expand)
-        late_moves.extend(along_z(k.half_dilated, k.z_dilated))
-        late_moves.extend(along_z(k.half_expand, k.z_expand))
+        late_moves.extend(along_z(net, k.half_dilated, k.z_dilated))
+
+        @pl.when(is_late)
+        def _():
+            for move_ in pyramid_moves:
+                move_.wait()
+            add_z(net, k.half_pyramid, k.z_pyramid, k.pyramid_sum)
+            begin_pyramid()
 
     norm_back(
         k.grad_1,
@@ -1374,67 +1593,21 @@
     lax.fori_loop(0, 4, reduce_gradient, 0)
     swap = core_halves(net, k.grad_reduce, k.core_reduce)
 
-    def finish(half, arrived):
-        return half[net.z].astype(F32) + sum(arrived[d].astype(F32) for d in range(3))
-
-    for move_ in pyramid_moves + small_moves:
-        move_.wait()
-
-    def sum_pyramid(i, carry):
-        total = k.half_pyramid[net.z, i].astype(F32)
-        for d in range(3):
-            total = total + k.z_pyramid[d, i].astype(F32)
-        k.sum_pyramid[i] = total.astype(BF16)
-        return carry
-
-    lax.fori_loop(0, 16, sum_pyramid, 0)
-    k.sum_project[...] = finish(k.half_project, k.z_project)
-    k.sum_pool[...] = finish(k.half_pool, k.z_pool)
-
-    def lanes_for(i):
-        return lane_block(odd if i == 0 else 1 - odd, 256)
-
-    wait_pyramid = to_owners(
-        lambda i: k.sum_pyramid.at[:, :, lanes_for(i)], k.own_pyramid, k.local_sems.at[9]
-    )
-    wait_project = to_owners(lambda i: k.sum_project, k.own_project, k.local_sems.at[10])
     swap.wait()
     add_halves(net, k.grad_reduce, k.core_reduce, k.half_reduce)
-    reduce_moves = along_z(k.half_reduce, k.z_reduce)
-
-    def input_rows(at):
-        total = k.shortcut[at, :]
-        for b in range(4):
-            total = total + mm_t(k.grad_reduced[at, b * 128 : b * 128 + 128], k.w_reduce[b])
-        k.grad_input[at, :] = total
-
-    each_rows(1536, 384, input_rows)
+    reduce_moves = along_z(net, k.half_reduce, k.z_reduce)
+
     for move_ in reduce_moves:
         move_.wait()
-    k.sum_reduce[...] = finish(k.half_reduce, k.z_reduce)
+    k.sum_reduce[...] = finish_z(net, k.half_reduce, k.z_reduce)
     wait_reduce = to_owners(
         lambda i: k.sum_reduce.at[:, lanes_for(i)], k.own_reduce, k.local_sems.at[11]
     )
     for move_ in late_moves:
         move_.wait()
-    k.sum_dilated[...] = finish(k.half_dilated, k.z_dilated)
-    k.sum_expand[...] = finish(k.half_expand, k.z_expand)
+    k.sum_dilated[...] = finish_z(net, k.half_dilated, k.z_dilated)
+    k.sum_expand[...] = finish_z(net, k.half_expand, k.z_expand)
     wait_pyramid()
-
-    def rows_for(i):
-        return pl.ds(pl.multiple_of((odd if i == 0 else 1 - odd) * 32, 32), 32)
-
-    nothing = jnp.zeros((64, 256), F32)
-    for tap in (9, 10, 11, 15, 16, 17, 18, 19, 20, 24, 25, 26):
-        k.grad_rates[tap] = nothing
-    for slot in range(16):
-        for i in range(2):
-            block = k.own_pyramid[i, slot].astype(F32)
-            if slot == 0:
-                k.grad_point[rows_for(i), :] = block
-            else:
-                tap = slot - 1 if slot < 10 else slot + 2 if slot < 13 else slot + 8
-                k.grad_rates[tap, rows_for(i), :] = block
     wait_project()
     wait_reduce()
 
@@ -1446,26 +1619,19 @@
         3,
         args,
         dict(
-            grad_input=((1536, 512), F32),
+            grad_reduced=((1536, 512), BF16),
             norm_2=((8, 128), F32),
             norm_1=((8, 128), F32),
-            grad_rates=((27, 64, 256), F32),
-            grad_point=((64, 256), F32),
+            own_pyramid=((2, 16, 32, 256), BF16),
             own_project=((2, 32, 384), F32),
-            sum_pool=((64, 256), F32),
             sum_dilated=((576, 128), F32),
             sum_expand=((64, 512), F32),
             own_reduce=((2, 64, 256), F32),
         ),
         dict(
             grad_taps=pltpu.VMEM((2560, 384), BF16),
-            grad_reduced=pltpu.VMEM((1536, 512), BF16),
             z_pyramid=pltpu.VMEM((3, 16, 32, 512), BF16),
-            z_project=pltpu.VMEM((3, 32, 384), BF16),
-            z_pool=pltpu.VMEM((3, 64, 256), BF16),
-            sum_pyramid=pltpu.VMEM((16, 32, 512), BF16),
-            own_pyramid=pltpu.VMEM((2, 16, 32, 256), BF16),
-            sum_project=pltpu.VMEM((32, 384), F32),
+            pyramid_sum=pltpu.VMEM((16, 32, 512), BF16),
             sum_reduce=pltpu.VMEM((64, 512), F32),
             grad_expand=pltpu.VMEM((8, 64, 512), BF16),
             core_expand=pltpu.VMEM((4, 64, 512), BF16),
@@ -1487,12 +1653,118 @@
             grad_1=pltpu.VMEM((1536, 128), F32),
             grad_pad=pltpu.VMEM((2560, 128), BF16),
             cells=pltpu.VMEM((20, 144, 128), F32),
-            **exchange_scratch(2, 128),
-            **exchange_scratch(1, 128),
+            **exchange_scratch(2),
+            **exchange_scratch(1),
             local_sems=pltpu.SemaphoreType.DMA((12,)),
         ),
         96,
         hbm=("w_dilated",),
+    )
+
+
+def finish(net, k):
+    counted = pixel_count(k.boxes)
+    odd = lax.rem(lax.axis_index("batch"), 2)
+
+    def rows_for(i):
+        return pl.ds(pl.multiple_of((odd if i == 0 else 1 - odd) * 32, 32), 32)
+
+    nothing = jnp.zeros((64, 256), F32)
+    for tap in (9, 10, 11, 15, 16, 17, 18, 19, 20, 24, 25, 26):
+        k.grad_rates[tap] = nothing
+    for slot in range(16):
+        for i in range(2):
+            block = k.own_pyramid[i, slot].astype(F32)
+            if slot == 0:
+                k.grad_point[rows_for(i), :] = block
+            else:
+                tap = slot - 1 if slot < 10 else slot + 2 if slot < 13 else slot + 8
+                k.grad_rates[tap, rows_for(i), :] = block
+    low = lax.broadcasted_iota(jnp.int32, (768, 128), 1) < 64
+    packed = k.packed[...].astype(F32)
+    k.features[0:768, :] = packed[:, 0:64].astype(BF16)
+    k.features[768:1536, :] = pltpu.roll(packed, 64, 1)[:, 0:64].astype(BF16)
+    for i in range(2):
+        block = k.own_project[i]
+        for slot in range(5):
+            part = block[:, (slot // 2) * 128 : (slot // 2) * 128 + 128]
+            if slot % 2:
+                part = pltpu.roll(part, 64, 1)
+            part = jnp.where(odd == 1, pltpu.roll(part, 96, 1), part)
+            k.grad_project[rows_for(i), slot, :] = part[:, 0:32]
+    rows = jnp.concatenate([k.own_reduce[0], k.own_reduce[1]], axis=0)
+    swapped = jnp.concatenate([k.own_reduce[1], k.own_reduce[0]], axis=0)
+    k.grad_reduce[...] = jnp.where(odd == 0, rows, swapped).T
+    k.grad_dilated[...] = k.from_dilated[...].reshape(9, 64, 128)
+    k.grad_expand[...] = k.from_expand[...]
+    k.grad_pool[...] = k.from_pool[...]
+    k.grad_norm_1[...] = k.norm_1[0:2, :]
+    k.grad_norm_2[...] = k.norm_2[0:2, :]
+    k.grad_norm_3[...] = k.norm_3[0:2, :]
+    for b in range(4):
+        k.grad_norm_b[:, b, :] = k.norm_b[0:2, b * 64 : b * 64 + 64]
+    k.grad_norm_pool[...] = k.norm_pool[0:2, 0:64]
+    k.grad_norm_p[...] = k.norm_p[0:2, 0:64]
+    k.grad_head_weight[...] = k.head_sums[:, 0:256].T[:, 0:22]
+    columns = k.head_sums[:, 256:384].T
+    k.grad_head_bias[...] = columns[0:1, 0:22]
+    loss = columns[1:2, :]
+    task = lax.broadcasted_iota(jnp.int32, (1, 32), 1)
+
+    def total(inside):
+        return jnp.sum(jnp.where(inside, loss, 0.0), axis=1, keepdims=True) / counted
+
+    terms = [total(task == 0), total(task == 19), total((task == 20) | (task == 21))]
+    lane = lax.broadcasted_iota(jnp.int32, (1, 128), 1)
+    losses = jnp.where(lane == 0, terms[0], jnp.where(lane == 1, terms[1], terms[2]))
+    log_vars = jnp.where(
+        lane == 0, k.log_vars[0], jnp.where(lane == 1, k.log_vars[1], k.log_vars[2])
+    )
+    weighted = jnp.exp(-log_vars) * losses
+    k.total_loss[...] = jnp.sum(
+        jnp.where(lane < 3, weighted + log_vars, 0.0), axis=1, keepdims=True
+    )
+    k.grad_log_vars[...] = (1.0 - weighted)[:, 0:3]
+
+    def input_rows(at):
+        total = k.shortcut[at, :]
+        for b in range(4):
+            total = total + mm_t(k.grad_reduced[at, b * 128 : b * 128 + 128], k.w_reduce[b])
+        k.grad_input[at, :] = total
+
+    each_rows(1536, 384, input_rows)
+
+
+def run_finish(args):
+    return call_kernel(
+        finish,
+        "finish",
+        None,
+        args,
+        dict(
+            features=((1536, 64), BF16),
+            total_loss=((1, 1), F32),
+            grad_input=((1536, 512), F32),
+            grad_reduce=((256, 128), F32),
+            grad_dilated=((9, 64, 128), F32),
+            grad_expand=((64, 512), F32),
+            grad_norm_1=((2, 128), F32),
+            grad_norm_2=((2, 128), F32),
+            grad_norm_3=((2, 512), F32),
+            grad_point=((64, 256), F32),
+            grad_rates=((27, 64, 256), F32),
+            grad_pool=((64, 256), F32),
+            grad_norm_b=((2, 4, 64), F32),
+            grad_norm_pool=((2, 64), F32),
+            grad_project=((64, 5, 32), F32),
+            grad_norm_p=((2, 64), F32),
+            grad_head_weight=((256, 22), F32),
+            grad_head_bias=((1, 22), F32),
+            grad_log_vars=((1, 3), F32),
+        ),
+        {},
+        0,
+        smem=("boxes", "log_vars"),
     )
 
 
@@ -1537,34 +1809,25 @@
     )
     w_pyramid = forward.w_pyramid.reshape(13, 256, 512)
 
-    count = jnp.sum((crop_boxes[:, 2] * crop_boxes[:, 3]).astype(F32))
-    task_weights = jnp.exp(-log_vars)
-    by_row = jnp.concatenate(
-        [jnp.full((19,), task_weights[0]), task_weights[1:2], jnp.full((2,), task_weights[2])]
-    )
-    columns = jnp.pad(jnp.stack([head_bias, by_row / count]), ((0, 0), (0, 10)))
-    both = jnp.concatenate([projection_norm_params, pooling_norm_params], axis=0)
     middle = run_pyramid(
         dict(
             trunk=forward.trunk,
             mask=forward.mask,
             w_pyramid=w_pyramid,
-            affine_b=branch_norms.reshape(2, 256),
-            affine_p=jnp.concatenate([both, both], axis=1),
+            branch_norms=branch_norms,
+            norm_project=projection_norm_params,
+            norm_pooling=pooling_norm_params,
             aspp_pool=aspp_pool,
             w_slots=forward.w_project.reshape(256, 1280),
-            head=jnp.pad(head_weight.T, ((0, 10), (0, 0))),
-            head_columns=jnp.broadcast_to(columns[:, :, None], (2, 32, 128)),
+            head_weight=head_weight,
+            head_bias=head_bias,
+            log_vars=log_vars,
             labels=seg_labels,
             depth=depth_target,
             normal=normal_target,
             boxes=crop_boxes,
         )
     )
-    features = jnp.concatenate([middle.features[:, :64], middle.features[:, 64:]], axis=0)
-    sums = middle.head_sums
-    losses = jnp.stack([sums[64, 0], sums[83, 0], sums[84, 0] + sums[85, 0]]) / count
-
     back = run_pyramid_backward(
         dict(
             grad_branches=middle.grad_branches,
@@ -1584,16 +1847,14 @@
     last = run_bottleneck_backward(
         dict(
             grad_expanded=back.grad_expanded,
-            shortcut=back.shortcut,
             half_pyramid=back.half_pyramid,
-            half_project=back.half_project,
-            half_pool=back.half_pool,
+            sum_pyramid=back.sum_pyramid,
+            sum_project=back.sum_project,
             x=x,
             hidden=forward.hidden,
             hidden_two=forward.hidden_two,
             w_expand=conv_expand,
             w_dilated=conv_dilated,
-            w_reduce=forward.w_reduce,
             dilated=forward.dilated,
             stats_2=forward.stats_2,
             affine_2=dilated_norm_params,
@@ -1604,34 +1865,49 @@
             boxes=crop_boxes,
         )
     )
-    odd = lax.rem(lax.axis_index("batch"), 2)
-
-    def in_order(blocks):
-        return jnp.where(odd == 0, blocks, blocks[::-1])
-
-    project_rows = in_order(last.own_project).reshape(64, 6, 64)[:, :5]
-    grad_project = jnp.where(odd == 0, project_rows[:, :, :32], project_rows[:, :, 32:])
-    grad_reduce = in_order(last.own_reduce).reshape(128, 256).T
+    done = run_finish(
+        dict(
+            shortcut=back.shortcut,
+            grad_reduced=last.grad_reduced,
+            w_reduce=forward.w_reduce,
+            own_pyramid=last.own_pyramid,
+            packed=middle.features,
+            own_project=last.own_project,
+            own_reduce=last.own_reduce,
+            from_dilated=last.sum_dilated,
+            from_expand=last.sum_expand,
+            from_pool=back.sum_pool,
+            norm_1=last.norm_1,
+            norm_2=last.norm_2,
+            norm_3=back.norm_3,
+            norm_b=middle.norm_b,
+            norm_pool=middle.norm_pool,
+            norm_p=middle.norm_p,
+            head_sums=middle.head_sums,
+            log_vars=log_vars,
+            boxes=crop_boxes,
+        )
+    )
     return (
-        features.reshape(1, 12, 128, 64),
-        jnp.sum(task_weights * losses + log_vars),
-        last.grad_input.reshape(1, 12, 128, 512),
-        grad_reduce,
-        last.sum_dilated.reshape(3, 3, 64, 128),
-        last.sum_expand,
-        last.norm_1[:2],
-        last.norm_2[:2],
-        back.norm_3[:2],
-        last.grad_point,
-        last.grad_rates.reshape(3, 3, 3, 64, 256),
-        last.sum_pool,
-        middle.norm_b[:2].reshape(2, 4, 64),
-        middle.norm_pool[:2, :64],
-        grad_project,
-        middle.norm_p[:2, :64],
-        sums[:22, :].T,
-        sums[32:54, 0],
-        1.0 - task_weights * losses,
+        done.features.reshape(1, 12, 128, 64),
+        done.total_loss.reshape(()),
+        done.grad_input.reshape(1, 12, 128, 512),
+        done.grad_reduce,
+        done.grad_dilated.reshape(3, 3, 64, 128),
+        done.grad_expand,
+        done.grad_norm_1,
+        done.grad_norm_2,
+        done.grad_norm_3,
+        done.grad_point,
+        done.grad_rates.reshape(3, 3, 3, 64, 256),
+        done.grad_pool,
+        done.grad_norm_b,
+        done.grad_norm_pool,
+        done.grad_project,
+        done.grad_norm_p,
+        done.grad_head_weight,
+        done.grad_head_bias.reshape(22),
+        done.grad_log_vars.reshape(3),
     )
 
 

time: 465 us -> 411 us (0.88)
  Pallas kernels: 424 us -> 396 us
  local copies, waits for them, and re-layouts: 29.1 us -> 12.1 us
  other arithmetic: 8.74 us -> 0 us
    pallas_call x4 -> x5, Pallas kernels: 424 us -> 396 us  [call_kernel(): pl.pallas_call(kernel, out_shape=[jax.ShapeDtypeStruct(s, d) for s, d in...]
    slice x10 -> x0, local copies, waits for them, and re-layouts: 11.3 us -> none  [the longest x1 1.33 us: fast_local(): sums[32:54, 0]]
    unnamed x43 -> x7, local copies, waits for them, and re-layouts: 10 us -> 10.5 us
where the time goes in v3:
time: 411 us; the launch traced here: 408 us
  Pallas kernels  396 us (96%)
  local copies, waits for them, and re-layouts  12.1 us (3%)
    pallas_call x5, Pallas kernels, call_kernel(): pl.pallas_call(kernel, out_shape=[jax.ShapeDtypeStruct(s, d) for s, d in...  396 us
    unnamed x7, local copies, waits for them, and re-layouts  10.5 us

profile of v3, /device:TPU:0, one launch (start us, length us, event | category | flops | bytes accessed | tf_op | source)
XLA Modules:
  0.0 408.5 jit_solution(13087910223719904937)
XLA Ops:
  0.7 1.3 copy.50.refs_11_
  1.9 1.3 copy.51.refs_12_
  3.2 1.3 copy.52.refs_13_
  4.5 1.5 copy.49.refs_8_
  6.0 1.6 copy.56
  7.6 98.5 %bottleneck.1 = (f32[1536,128]{1,0:T(8,128)}, bf16[4,512,128]{2,1,0:T(8,128)(2,1)}, bf16[13,4,64,512]{3,2,1,0:T(8,128)(2,1)}, bf16[4,64,1280]{2,1,0:T(8,128)(2,1...) custom-call(bf16[1536,512]{1,0:T(8,128)(2,1)} %bitcast.12, ...), custom_call_target="tpu_custom_call" | custom-call | tf_op jit(solution)/shard_map/bottleneck/pallas_call | solution.py:443
  106.1 102.4 %pyramid.1 = (bf16[768,128]{1,0:T(8,128)(2,1)}, f32[8,128]{1,0:T(8,128)}, bf16[8,32,384]{2,1,0:T(8,128)(2,1)}, bf16[8,64,256]{2,1,0:T(8,128)(2,1)}, f32[8,256]{1...) custom-call(bf16[1536,512]{1,0:T(8,128)(2,1)} %get-tuple-element.75.refs_0_.re, ...), custom_call_target="tpu_custom_call" | custom-call | tf_op jit(solution)/shard_map/pyramid/pallas_call | solution.py:443
  208.5 72.7 %pyramid_back.1 = (f32[1536,512]{1,0:T(8,128)}, bf16[1536,512]{1,0:T(8,128)(2,1)}, f32[8,512]{1,0:T(8,128)}, bf16[4,16,32,512]{3,2,1,0:T(8,128)(2,1)}, bf16[16,3...) custom-call(bf16[1536,256]{1,0:T(8,128)(2,1)} %get-tuple-element.79.refs_0_, ...), custom_call_target="tpu_custom_call" | custom-call | tf_op jit(solution)/shard_map/pyramid_back/pallas_call | solution.py:443
  281.2 114.0 %bottleneck_back.1 = (bf16[1536,512]{1,0:T(8,128)(2,1)}, f32[8,128]{1,0:T(8,128)}, f32[8,128]{1,0:T(8,128)}, bf16[2,16,32,256]{3,2,1,0:T(8,128)(2,1)}, f32[2,32,...) custom-call(bf16[1536,512]{1,0:T(8,128)(2,1)} %get-tuple-element.86.refs_0_, ...), custom_call_target="tpu_custom_call" | custom-call | tf_op jit(solution)/shard_map/bottleneck_back/pallas_call | solution.py:443
  395.2 8.2 %finish.1 = (bf16[1536,64]{1,0:T(8,128)(2,1)}, f32[1,1]{1,0:T(1,128)}, f32[1536,512]{1,0:T(8,128)}, f32[256,128]{1,0:T(8,128)}, f32[9,64,128]{2,1,0:T(8,128)}, /...) custom-call(f32[1536,512]{1,0:T(8,128)} %get-tuple-element.85.refs_0, ...), custom_call_target="tpu_custom_call" | custom-call | tf_op jit(solution)/shard_map/finish/pallas_call | solution.py:443
  403.4 1.8 copy.53
  405.2 1.6 copy.55
  406.8 1.7 copy.54

commit v4 on v3

--- a/solution.py
+++ b/solution.py
@@ -167,20 +167,19 @@
         return copy
 
 
-def greet(peers, perhaps=None):
+def greet(peers, perhaps=()):
     barrier = pltpu.get_barrier_semaphore()
     for peer in peers:
         pl.semaphore_signal(barrier, inc=1, device_id=peer, device_id_type=MESH)
-    if perhaps is None:
-        pl.semaphore_wait(barrier, len(peers))
-        return
-    peer, there = perhaps
-
-    @pl.when(there)
-    def _():
-        pl.semaphore_signal(barrier, inc=1, device_id=peer, device_id_type=MESH)
-
-    pl.semaphore_wait(barrier, len(peers) + there.astype(jnp.int32))
+    awaited = len(peers)
+    for peer, there in perhaps:
+
+        @pl.when(there)
+        def _(peer=peer):
+            pl.semaphore_signal(barrier, inc=1, device_id=peer, device_id_type=MESH)
+
+        awaited = awaited + there.astype(jnp.int32)
+    pl.semaphore_wait(barrier, awaited)
 
 
 def each_rows(total, step, body):
@@ -299,7 +298,7 @@
         copy.wait()
 
 
-def sum_scatter(net, part, bufs, out, meanwhile=None):
+def sum_scatter(net, part, bufs, out, meanwhile=None, produce=None):
     far, to_side, to_over, far_side, far_over, from_side, from_over = bufs
     rows, width = out.shape
     half, step = rows // 2, 16384 // width
@@ -320,8 +319,12 @@
 
         each_rows(half, step, body)
 
+    if produce is not None:
+        produce(0)
     fill(far, across, 0)
     first = net.send(far.at[head], far_side, net.side)
+    if produce is not None:
+        produce(1)
     fill(far, across, half)
     second = net.send(far.at[tail], far_over, net.over)
     fill(to_side, side, 0)
@@ -430,22 +433,69 @@
     return lax.dot_general(a, b, (((0,), (0,)), ((), ())), preferred_element_type=F32)
 
 
-def call_kernel(body, name, number, args, outs, scratch, sems, hbm=(), smem=("boxes",)):
+class Streams:
+    def __init__(self, ins, outs, sems):
+        self.ins = {n: pltpu.make_async_copy(*pair, sems.at[i]) for i, (n, pair) in enumerate(ins)}
+        self.outs = {
+            n: pltpu.make_async_copy(*pair, sems.at[len(ins) + i])
+            for i, (n, pair) in enumerate(outs)
+        }
+        self.left = []
+        for copy in self.ins.values():
+            copy.start()
+
+    def need(self, *names):
+        for name in names:
+            self.ins.pop(name).wait()
+
+    def done(self, *names):
+        for name in names:
+            copy = self.outs.pop(name)
+            copy.start()
+            self.left.append(copy)
+
+    def finish(self):
+        self.need(*list(self.ins))
+        self.done(*list(self.outs))
+        for copy in self.left:
+            copy.wait()
+
+
+def call_kernel(
+    body, name, number, args, outs, scratch, sems, hbm=(), smem=("boxes",), stream=()
+):
     vmem, anywhere = pl.BlockSpec(memory_space=pltpu.VMEM), pl.BlockSpec(memory_space=pl.ANY)
-    names = [*args, *outs, *scratch]
-    places = {name: anywhere for name in hbm}
+    stream_in = [n for n in args if n in stream]
+    stream_out = [n for n in outs if n in stream]
+    buffers = {n: pltpu.VMEM(args[n].shape, args[n].dtype) for n in stream_in}
+    buffers.update({n: pltpu.VMEM(*outs[n]) for n in stream_out})
+    names = [f"far_{n}" if n in stream else n for n in [*args, *outs]]
+    names = [*names, *scratch, *buffers, "stream_sems"]
+    places = {name: anywhere for name in [*hbm, *stream]}
     places.update({name: pl.BlockSpec(memory_space=pltpu.SMEM) for name in smem})
 
     def kernel(*refs):
         k = types.SimpleNamespace(**dict(zip(names, refs)))
+        held = vars(k)
+        k.stream = Streams(
+            [(n, (held[f"far_{n}"], held[n])) for n in stream_in],
+            [(n, (held[n], held[f"far_{n}"])) for n in stream_out],
+            k.stream_sems,
+        )
         body(Net(refs[-2], refs[-1]) if sems else None, k)
+        k.stream.finish()
 
     results = pl.pallas_call(
         kernel,
         out_shape=[jax.ShapeDtypeStruct(s, d) for s, d in outs.values()],
         in_specs=[places.get(name, vmem) for name in args],
         out_specs=[places.get(name, vmem) for name in outs],
-        scratch_shapes=list(scratch.values()) + [pltpu.SemaphoreType.DMA((sems,))] * (2 if sems else 0),
+        scratch_shapes=[
+            *scratch.values(),
+            *buffers.values(),
+            pltpu.SemaphoreType.DMA((max(len(buffers), 1),)),
+            *([pltpu.SemaphoreType.DMA((sems,))] * (2 if sems else 0)),
+        ],
         name=name,
         compiler_params=pltpu.CompilerParams(
             collective_id=number, has_side_effects=bool(sems), vmem_limit_bytes=VMEM_LIMIT
@@ -538,6 +588,8 @@
         return carry
 
     lax.fori_loop(0, 12, mask_rows, 0)
+    k.stream.done("mask")
+    k.stream.need("x")
 
     def reduce_for(b):
         def reduce_rows(at):
@@ -552,8 +604,17 @@
     arrivals[2].wait()
     reduce_for(net.m ^ 2)
     arrivals[0].wait()
-    reduce_for(net.m ^ 3)
-    sum_scatter(net, k.part, scatter_refs(k, "sum"), k.reduced)
+    k.stream.done("w_reduce")
+
+    def far_half(half):
+        def reduce_rows(at):
+            at = pl.ds(pl.multiple_of(at.start + half * 768, 128), 384)
+            k.part[net.m ^ 3, at, :] = mm(k.x[at, :], k.w_reduce[net.m ^ 3])
+
+        each_rows(768, 384, reduce_rows)
+
+    sum_scatter(net, k.part, scatter_refs(k, "sum"), k.reduced, produce=far_half)
+    k.stream.done("reduced")
 
     half = pl.ds(pl.multiple_of(net.r * 32, 32), 32)
     late = []
@@ -565,7 +626,7 @@
         if kind == "point":
             return k.aspp_point.at[half, lanes], k.w_pyramid.at[0, net.m, half]
         if kind == "project":
-            return k.project.at[half], k.w_project.at[net.m, half]
+            return k.project.at[:, half], k.w_project.at[net.m, :, half]
         return (
             k.aspp_rates.at[kind, 1, :, half, lanes],
             k.w_pyramid.at[pl.ds(1 + 3 * kind, 3), net.m, half],
@@ -600,6 +661,7 @@
     for load in loads:
         load.wait()
     halo.wait()
+    k.stream.done("hidden")
 
     def dilated_rows(i, carry):
         total = 0.0
@@ -619,6 +681,7 @@
         return carry
 
     lax.fori_loop(0, 12, add_columns, 0)
+    k.stream.done("dilated")
     mean_2, inverse_2 = statistics(net, k.dilated, k.mask, counts, k.out_2, k.in_2, counted)
     keep_rows(k.stats_2, mean_2, inverse_2)
 
@@ -629,11 +692,14 @@
     each_rows(1536, 128, activate_2)
     gather_blocks(net, lambda b, at: k.hidden_two.at[at, lane_block(b)], 1536)
     spread_weights(1, 2)
+    k.stream.done("hidden_two")
+    k.stream.need("w_expand")
 
     def expand_rows(at):
         k.expanded[at, :] = mm(k.hidden_two[at, :], k.w_expand[...])
 
     each_rows(1536, 384, expand_rows)
+    k.stream.done("expanded")
     mean_3, inverse_3 = statistics(net, k.expanded, k.mask, counts, k.out_3, k.in_3, counted)
     keep_rows(k.stats_3, mean_3, inverse_3)
     for copy in late:
@@ -663,7 +729,7 @@
             mask=((1536, 128), F32),
             w_reduce=((4, 512, 128), BF16),
             w_pyramid=((13, 4, 64, 512), BF16),
-            w_project=((4, 64, 1280), BF16),
+            w_project=((4, 5, 64, 256), BF16),
             reduced=((1536, 128), F32),
             stats_1=((8, 128), F32),
             hidden=((2560, 512), BF16),
@@ -695,6 +761,17 @@
             "w_pyramid",
             "w_project",
         ),
+        stream=(
+            "x",
+            "w_expand",
+            "mask",
+            "w_reduce",
+            "reduced",
+            "hidden",
+            "dilated",
+            "hidden_two",
+            "expanded",
+        ),
     )
 
 
@@ -715,7 +792,9 @@
         k.affine_p[0:2, i * 64 : i * 64 + 64] = k.norm_project[...]
         k.affine_p[2:4, i * 64 : i * 64 + 64] = k.norm_pooling[...]
     k.head_rows[...] = jnp.zeros((32, 256), F32)
-    k.head_rows[0:22, :] = k.head_weight[...].astype(F32).T
+    k.head_rows[0:22, :] = k.head_weight[...].astype(F32)
+
+    k.stream.need("mask")
 
     (own_sum,) = column_sums(
         lambda at: (k.trunk[at, :].astype(F32) * wide(k.mask[at, :], 512),), 1536, 512, 1
@@ -748,6 +827,7 @@
         k.edge_out[rows_of(i), :] = total.astype(BF16)
         return carry
 
+    k.stream.need("w_pyramid")
     lax.fori_loop(0, 4, edge_rows, 0)
     edge = net.send(k.edge_out, k.edge_in, net.core)
 
@@ -761,9 +841,6 @@
             k.part[b, rows_of(i), 128:256] = block
         return carry
 
-    lax.fori_loop(0, 4, outer_rows, 0)
-    edge.wait()
-
     def inner_rows(i, carry):
         point = mm_t(k.trunk[rows_of(i), :], k.w_pyramid[0])
         first = k.edge_in[rows_of(i), :].astype(F32)
@@ -773,15 +850,20 @@
             k.part[b, rows_of(i), 0:128] = block
         return carry
 
-    lax.fori_loop(0, 4, inner_rows, 0)
-    sum_scatter(net, k.part, scatter_refs(k, "sum"), k.branches)
+    def half_tile(half):
+        lax.fori_loop(2 * half, 2 * half + 2, outer_rows, 0)
+        if half == 0:
+            edge.wait()
+        lax.fori_loop(2 * half, 2 * half + 2, inner_rows, 0)
+
+    sum_scatter(net, k.part, scatter_refs(k, "sum"), k.branches, produce=half_tile)
 
     low_256 = lax.broadcasted_iota(jnp.int32, (256, 128), 1) < 64
     odd = lax.rem(net.m, 2) == 1
 
     def slot(s):
-        lanes = pl.ds(pl.multiple_of(s * 256 + (net.m // 2) * 128, 128), 128)
-        block = k.w_slots[:, lanes].astype(F32)
+        lanes = lane_block(net.m // 2)
+        block = jnp.concatenate([k.w_slots[b, s, :, lanes] for b in range(4)], axis=0).astype(F32)
         return jnp.where(odd, pltpu.roll(block, 64, 1), block)
 
     for s in range(0, 4, 2):
@@ -832,7 +914,9 @@
             k.part_2[b, at, :] = block
         return carry
 
-    lax.fori_loop(0, 2, project_rows, 0)
+    def project_half(half):
+        project_rows(half, 0)
+
     low_128 = lax.broadcasted_iota(jnp.int32, (128, 128), 1) < 64
 
     def pair_mask(at):
@@ -840,7 +924,7 @@
         k.mask_pairs[at, :] = jnp.where(low_128, k.mask[at, :], k.mask[below, :])
 
     each_rows(768, 128, pair_mask)
-    sum_scatter(net, k.part_2, scatter_refs(k, "sum2"), k.projected)
+    sum_scatter(net, k.part_2, scatter_refs(k, "sum2"), k.projected, produce=project_half)
     mean_p, inverse_p = statistics(
         net, k.projected, k.mask_pairs, counts, k.out_2, k.in_2, counted, folded=True
     )
@@ -893,10 +977,10 @@
         inside = inside & (column_id >= left_edge) & (column_id < right_edge)
         inside = jnp.where(inside, 1.0, 0.0)
         span = range(chunk * 4, chunk * 4 + 4)
-        label = four_rows([k.labels[0, y : y + 1, :] for y in span])
-        target = jnp.where(is_depth, four_rows([k.depth[0, y : y + 1, :] for y in span]), 0.0)
+        label = four_rows([k.labels[y] for y in span])
+        target = jnp.where(is_depth, four_rows([k.depth[y] for y in span]), 0.0)
         for n in range(2):
-            normal = four_rows([k.normal[0, n, y : y + 1, :] for y in span])
+            normal = four_rows([k.normal[y, n : n + 1, :] for y in span])
             target = jnp.where(class_row == 20 + n, normal, target)
         top = jnp.max(jnp.where(is_class, logits, -jnp.inf), axis=0, keepdims=True)
         powers = jnp.where(is_class, jnp.exp(jnp.where(is_class, logits - top, 0.0)), 0.0)
@@ -1090,6 +1174,7 @@
         ),
         96,
         smem=("boxes", "head_bias", "log_vars"),
+        stream=("mask", "w_pyramid"),
     )
 
 
@@ -1104,45 +1189,69 @@
         target[z] = total.astype(target.dtype)
 
 
-def z_copies(net, source, target):
+def chunk_of(z):
+    return 2 * lax.rem(z, 2) + z // 2
+
+
+def along_z(net, source, target, chunk=lambda z: z):
     copies = []
     for d in (1, 2, 3):
-        i = net.count
-        net.count += 1
         there = lax.rem(net.z + d, 4)
         copies.append(
-            pltpu.make_async_remote_copy(
-                src_ref=source.at[there],
-                dst_ref=target.at[d - 1],
-                send_sem=net.send_sems.at[i],
-                recv_sem=net.recv_sems.at[i],
-                device_id=(net.m, net.r, there),
-                device_id_type=MESH,
-            )
+            net.send(source.at[chunk(there)], target.at[d - 1], (net.m, net.r, there))
         )
     return copies
 
 
-def along_z(net, source, target):
-    copies = z_copies(net, source, target)
-    for copy in copies:
-        copy.start()
-    return copies
-
-
-def finish_z(net, half, arrived):
-    return half[net.z].astype(F32) + sum(arrived[d].astype(F32) for d in range(3))
-
-
-def add_z(net, half, arrived, target):
-    def body(i, carry):
-        total = half[net.z, i].astype(F32)
-        for d in range(3):
-            total = total + arrived[d, i].astype(F32)
-        target[i] = total.astype(BF16)
-        return carry
-
-    lax.fori_loop(0, 16, body, 0)
+def finish_z(net, half, arrived, chunk=lambda z: z):
+    return half[chunk(net.z)].astype(F32) + sum(arrived[d].astype(F32) for d in range(3))
+
+
+class PairSums:
+    def __init__(self, net, half, other, pair, last):
+        self.net, self.half, self.other, self.pair, self.last = net, half, other, pair, last
+        kept, away = lax.rem(net.z, 2), lax.rem(net.z + 1, 2)
+        self.kept = 2 * kept
+        self.first = self.copy(half.at[pl.ds(2 * away, 2)], other, net.z + 1 - 2 * kept)
+        self.high = net.z // 2
+        self.second = self.copy(pair.at[1 - self.high], last, net.z + 2 - 4 * self.high)
+
+    def copy(self, src, dst, z):
+        net, i = self.net, self.net.count
+        net.count += 1
+        return pltpu.make_async_remote_copy(
+            src_ref=src,
+            dst_ref=dst,
+            send_sem=net.send_sems.at[i],
+            recv_sem=net.recv_sems.at[i],
+            device_id=(net.m, net.r, z),
+            device_id_type=MESH,
+        )
+
+    def begin(self):
+        self.first.start()
+
+    def go_on(self, half):
+        self.first.wait()
+
+        def body(i, carry):
+            for h in range(2):
+                total = half[self.kept + h, i].astype(F32) + self.other[h, i].astype(F32)
+                self.pair[h, i] = total.astype(BF16)
+            return carry
+
+        lax.fori_loop(0, half.shape[1], body, 0)
+        self.second.start()
+
+    def finish(self, target):
+        self.second.wait()
+
+        def body(i, carry):
+            total = self.pair[self.high, i].astype(F32) + self.last[i].astype(F32)
+            target[i] = total.astype(BF16)
+            return carry
+
+        lax.fori_loop(0, target.shape[0], body, 0)
 
 
 def pyramid_backward(net, k):
@@ -1261,6 +1370,7 @@
         build(near)
         copy.wait()
         build_edge(near)
+        k.stream.need("trunk")
         weight_gradients(near)
         first_swap.append(to_core(near))
         pl.when(mine_second)(first_swap[0].start)
@@ -1272,17 +1382,17 @@
         swap.wait()
     add_halves(net, k.grad_project, k.core_project, k.half_project)
     add_halves(net, k.grad_pool, k.core_pool, k.half_pool)
-    small_moves = along_z(net, k.half_project, k.z_project) + along_z(net, k.half_pool, k.z_pool)
+    small_moves = along_z(net, k.half_project, k.z_project, chunk_of)
+    small_moves = small_moves + along_z(net, k.half_pool, k.z_pool)
     copy.wait()
     build_edge(far)
-    z_moves = z_copies(net, k.half_pyramid, k.z_pyramid)
+    pair_sums = PairSums(net, k.half_pyramid, k.z_other, k.z_pair, k.z_last)
 
     @pl.when(mine_first)
     def _():
         first_swap[0].wait_recv()
         add_core(near)
-        for move_ in z_moves:
-            move_.start()
+        pair_sums.begin()
 
     def trunk_rows(i, carry):
         total = 0.0
@@ -1291,6 +1401,7 @@
         k.shortcut[rows_of(i), :] = total
         return carry
 
+    k.stream.need("w_pyramid", "expanded", "x", "mask")
     lax.fori_loop(0, 4, trunk_rows, 0)
     mean, inverse = k.stats_3[0:1, :], k.stats_3[1:2, :]
     gain, bias = k.affine_3[0:1, :], k.affine_3[1:2, :]
@@ -1305,12 +1416,17 @@
         k.shortcut[at, :] = grad * slope(u)
 
     each_rows(1536, 32, back_trunk)
+    k.stream.done("shortcut")
 
     second_swap = to_core(far)
 
     def far_gradients():
         weight_gradients(far)
-        pl.when(mine_first)(second_swap.start)
+
+        @pl.when(mine_first)
+        def _():
+            second_swap.start()
+            pair_sums.go_on(k.half_pyramid)
 
     bias_grad, gain_grad = gradient_sums(
         net, k.shortcut, normed, k.out_1, k.in_1, meanwhile=far_gradients
@@ -1323,9 +1439,10 @@
         k.grad_expanded[at, :] = (inverse * grad).astype(BF16)
 
     each_rows(1536, 32, back_expanded)
+    k.stream.done("grad_expanded")
     for move_ in small_moves:
         move_.wait()
-    k.sum_project[...] = finish_z(net, k.half_project, k.z_project)
+    k.sum_project[...] = finish_z(net, k.half_project, k.z_project, chunk_of)
     k.sum_pool[...] = finish_z(net, k.half_pool, k.z_pool)
 
     @pl.when(mine_second)
@@ -1337,9 +1454,15 @@
     @pl.when(mine_first)
     def _():
         second_swap.wait_send()
-        for move_ in z_moves:
-            move_.wait()
-        add_z(net, k.half_pyramid, k.z_pyramid, k.sum_pyramid)
+        pair_sums.finish(k.sum_pyramid)
+
+
+def pair_scratch():
+    return dict(
+        z_other=pltpu.VMEM((2, 16, 32, 512), BF16),
+        z_pair=pltpu.VMEM((2, 16, 32, 512), BF16),
+        z_last=pltpu.VMEM((16, 32, 512), BF16),
+    )
 
 
 def run_pyramid_backward(args):
@@ -1360,7 +1483,7 @@
         dict(
             half_project=pltpu.VMEM((4, 32, 384), BF16),
             half_pool=pltpu.VMEM((4, 64, 256), BF16),
-            z_pyramid=pltpu.VMEM((3, 16, 32, 512), BF16),
+            **pair_scratch(),
             z_project=pltpu.VMEM((3, 32, 384), BF16),
             z_pool=pltpu.VMEM((3, 64, 256), BF16),
             grad_pyramid=pltpu.VMEM((8, 16, 32, 512), BF16),
@@ -1374,20 +1497,28 @@
             **exchange_scratch(1),
         ),
         48,
+        stream=("w_pyramid", "expanded", "x", "mask", "trunk", "shortcut", "grad_expanded"),
     )
 
 
 def bottleneck_backward(net, k):
     counted = pixel_count(k.boxes)
     loads = load_taps(k)
-    odd = lax.rem(net.slot, 2)
-    owners = []
+    high = net.z // 2
+    owners, givers = [], []
+    for which in (high, 1 - high):
+        part = 2 * net.m + which
+        owners.append((2 * net.r + lax.rem(net.z, 2), part // 4, lax.rem(part, 4)))
+    odd = lax.rem(net.z, 2)
     for which in (odd, 1 - odd):
-        part = 2 * net.m + which
-        owners.append((net.slot // 2, part // 4, lax.rem(part, 4)))
-    stays = net.slot // 2 == net.m
-    moves = jnp.logical_not(stays)
-    greet([net.side, net.over] + net.group + [owners[1]], (owners[0], moves))
+        givers.append((net.slot // 2, net.m // 2, lax.rem(net.m, 2) + 2 * which))
+    here = net.m * 8 + net.slot
+    moves = owners[0][0] * 8 + owners[0][1] * 4 + owners[0][2] != here
+    stays = jnp.logical_not(moves)
+    greet(
+        [net.side, net.over] + net.group + [owners[1], givers[1]],
+        [(owners[0], moves), (givers[0], moves)],
+    )
 
     def to_owners(views, arrived, sem, start=True):
         first = pltpu.make_async_remote_copy(
@@ -1427,11 +1558,11 @@
         return begin, wait
 
     def lanes_for(i):
-        return lane_block(odd if i == 0 else 1 - odd, 256)
+        return lane_block(high if i == 0 else 1 - high, 256)
 
     early = net.r == net.m // 2
     is_late = net.r == 1 - net.m // 2
-    pyramid_moves = z_copies(net, k.half_pyramid, k.z_pyramid)
+    pair_sums = PairSums(net, k.far_half_pyramid, k.z_other, k.z_pair, k.z_last)
 
     begin_pyramid, wait_pyramid = to_owners(
         lambda i: k.pyramid_sum.at[:, :, lanes_for(i)], k.own_pyramid, k.local_sems.at[9], False
@@ -1439,8 +1570,7 @@
 
     @pl.when(is_late)
     def _():
-        for move_ in pyramid_moves:
-            move_.start()
+        pair_sums.begin()
 
     @pl.when(early)
     def _():
@@ -1452,15 +1582,20 @@
     def rows_of(i, size=384):
         return pl.ds(pl.multiple_of(i * size, 128), size)
 
-    def expand_rows(at):
-        total = mm_t(k.grad_expanded[at, :], k.w_expand[...])
-        for b in range(4):
-            k.part[b, at, :] = total[:, b * 128 : b * 128 + 128]
-
-    each_rows(1536, 384, expand_rows)
+    def expand_half(half):
+        def expand_rows(at):
+            at = pl.ds(pl.multiple_of(at.start + half * 768, 128), 384)
+            total = mm_t(k.grad_expanded[at, :], k.w_expand[...])
+            for b in range(4):
+                k.part[b, at, :] = total[:, b * 128 : b * 128 + 128]
+
+        each_rows(768, 384, expand_rows)
+
     swaps, late_moves = [], []
 
     def expand_gradient():
+        k.stream.need("hidden_two")
+
         def body(b, carry):
             grad = tm_m(k.hidden_two[:, lane_block(b)], k.grad_expanded[...])
             k.grad_expand[pl.ds(2 * b, 2)] = grad.reshape(2, 64, 512).astype(BF16)
@@ -1469,7 +1604,8 @@
         lax.fori_loop(0, 4, body, 0)
         swaps.append(core_halves(net, k.grad_expand, k.core_expand))
 
-    sum_scatter(net, k.part, scatter_refs(k, "sum"), k.grad_2, meanwhile=expand_gradient)
+    sum_scatter(net, k.part, scatter_refs(k, "sum"), k.grad_2, meanwhile=expand_gradient, produce=expand_half)
+    k.stream.need("dilated", "mask")
 
     def norm_back(grad, value, stats, affine, outgoing, incoming, store, kept, meanwhile=None):
         mean, inverse = stats[0:1, :], stats[1:2, :]
@@ -1498,6 +1634,12 @@
         k.grad_pad[pl.ds(pl.multiple_of(at.start + 512, 128), 128), :] = value
 
     def pass_expand():
+        k.stream.need("half_pyramid")
+
+        @pl.when(is_late)
+        def _():
+            pair_sums.go_on(k.half_pyramid)
+
         swaps.pop().wait()
         add_halves(net, k.grad_expand, k.core_expand, k.half_expand)
         late_moves.extend(along_z(net, k.half_expand, k.z_expand))
@@ -1539,8 +1681,12 @@
             k.part[b, rows_of(i), :] = total[:, b * 128 : b * 128 + 128]
         return carry
 
-    lax.fori_loop(0, 4, dilated_rows, 0)
+    def dilated_half(half):
+        lax.fori_loop(2 * half, 2 * half + 2, dilated_rows, 0)
+
     def dilated_gradient():
+        k.stream.need("hidden")
+
         for i in range(3):
 
             def body(b, carry):
@@ -1555,22 +1701,21 @@
             lax.fori_loop(0, 4, body, 0)
         swaps.append(core_halves(net, k.grad_dilated, k.core_dilated))
 
-    sum_scatter(net, k.part, scatter_refs(k, "sum2"), k.grad_1, meanwhile=dilated_gradient)
+    sum_scatter(net, k.part, scatter_refs(k, "sum2"), k.grad_1, meanwhile=dilated_gradient, produce=dilated_half)
+    k.stream.need("reduced")
 
     def store_1(at, value):
         k.grad_reduced[at, lane_block(net.m)] = value
 
     def pass_halves():
+        @pl.when(is_late)
+        def _():
+            pair_sums.finish(k.pyramid_sum)
+            begin_pyramid()
+
         swaps.pop().wait()
         add_halves(net, k.grad_dilated, k.core_dilated, k.half_dilated)
         late_moves.extend(along_z(net, k.half_dilated, k.z_dilated))
-
-        @pl.when(is_late)
-        def _():
-            for move_ in pyramid_moves:
-                move_.wait()
-            add_z(net, k.half_pyramid, k.z_pyramid, k.pyramid_sum)
-            begin_pyramid()
 
     norm_back(
         k.grad_1,
@@ -1585,6 +1730,8 @@
     )
     gather_blocks(net, lambda b, at: k.grad_reduced.at[at, lane_block(b)], 1536)
 
+    k.stream.need("x")
+
     def reduce_gradient(b, carry):
         grad = tm_m(k.grad_reduced[:, lane_block(b)], k.x[...])
         k.grad_reduce[pl.ds(2 * b, 2)] = grad.reshape(2, 64, 512).astype(BF16)
@@ -1595,11 +1742,21 @@
 
     swap.wait()
     add_halves(net, k.grad_reduce, k.core_reduce, k.half_reduce)
-    reduce_moves = along_z(net, k.half_reduce, k.z_reduce)
-
+    reduce_moves = along_z(net, k.half_reduce, k.z_reduce, chunk_of)
+
+    k.stream.need("shortcut", "w_reduce")
+
+    def input_rows(at):
+        total = k.shortcut[at, :]
+        for b in range(4):
+            total = total + mm_t(k.grad_reduced[at, b * 128 : b * 128 + 128], k.w_reduce[b])
+        k.grad_input[at, :] = total
+
+    each_rows(1536, 384, input_rows)
+    k.stream.done("grad_input")
     for move_ in reduce_moves:
         move_.wait()
-    k.sum_reduce[...] = finish_z(net, k.half_reduce, k.z_reduce)
+    k.sum_reduce[...] = finish_z(net, k.half_reduce, k.z_reduce, chunk_of)
     wait_reduce = to_owners(
         lambda i: k.sum_reduce.at[:, lanes_for(i)], k.own_reduce, k.local_sems.at[11]
     )
@@ -1619,7 +1776,7 @@
         3,
         args,
         dict(
-            grad_reduced=((1536, 512), BF16),
+            grad_input=((1536, 512), F32),
             norm_2=((8, 128), F32),
             norm_1=((8, 128), F32),
             own_pyramid=((2, 16, 32, 256), BF16),
@@ -1630,7 +1787,8 @@
         ),
         dict(
             grad_taps=pltpu.VMEM((2560, 384), BF16),
-            z_pyramid=pltpu.VMEM((3, 16, 32, 512), BF16),
+            grad_reduced=pltpu.VMEM((1536, 512), BF16),
+            **pair_scratch(),
             pyramid_sum=pltpu.VMEM((16, 32, 512), BF16),
             sum_reduce=pltpu.VMEM((64, 512), F32),
             grad_expand=pltpu.VMEM((8, 64, 512), BF16),
@@ -1659,6 +1817,18 @@
         ),
         96,
         hbm=("w_dilated",),
+        stream=(
+            "half_pyramid",
+            "hidden_two",
+            "dilated",
+            "mask",
+            "hidden",
+            "reduced",
+            "x",
+            "shortcut",
+            "w_reduce",
+            "grad_input",
+        ),
     )
 
 
@@ -1680,18 +1850,20 @@
             else:
                 tap = slot - 1 if slot < 10 else slot + 2 if slot < 13 else slot + 8
                 k.grad_rates[tap, rows_for(i), :] = block
-    low = lax.broadcasted_iota(jnp.int32, (768, 128), 1) < 64
-    packed = k.packed[...].astype(F32)
-    k.features[0:768, :] = packed[:, 0:64].astype(BF16)
-    k.features[768:1536, :] = pltpu.roll(packed, 64, 1)[:, 0:64].astype(BF16)
-    for i in range(2):
-        block = k.own_project[i]
-        for slot in range(5):
-            part = block[:, (slot // 2) * 128 : (slot // 2) * 128 + 128]
-            if slot % 2:
-                part = pltpu.roll(part, 64, 1)
-            part = jnp.where(odd == 1, pltpu.roll(part, 96, 1), part)
-            k.grad_project[rows_for(i), slot, :] = part[:, 0:32]
+    k.stream.done("grad_rates")
+    k.stream.need("from_input")
+    leave = pltpu.make_async_copy(k.from_input, k.grad_input, k.sem.at[0])
+    leave.start()
+    for y in range(6):
+        turned = k.packed[y * 128 : y * 128 + 128, :].astype(F32).T.astype(BF16)
+        k.features[y] = turned[0:64, :]
+        k.features[y + 6] = turned[64:128, :]
+    rows = jnp.concatenate([k.own_project[0], k.own_project[1]], axis=0)
+    swapped = jnp.concatenate([k.own_project[1], k.own_project[0]], axis=0)
+    k.turned[...] = jnp.where(odd == 0, rows, swapped).T
+    for slot in range(5):
+        start = pl.multiple_of(slot * 64 + odd * 32, 32)
+        k.grad_project[slot] = k.turned[pl.ds(start, 32), :]
     rows = jnp.concatenate([k.own_reduce[0], k.own_reduce[1]], axis=0)
     swapped = jnp.concatenate([k.own_reduce[1], k.own_reduce[0]], axis=0)
     k.grad_reduce[...] = jnp.where(odd == 0, rows, swapped).T
@@ -1705,7 +1877,7 @@
         k.grad_norm_b[:, b, :] = k.norm_b[0:2, b * 64 : b * 64 + 64]
     k.grad_norm_pool[...] = k.norm_pool[0:2, 0:64]
     k.grad_norm_p[...] = k.norm_p[0:2, 0:64]
-    k.grad_head_weight[...] = k.head_sums[:, 0:256].T[:, 0:22]
+    k.grad_head_weight[...] = k.head_sums[0:22, 0:256]
     columns = k.head_sums[:, 256:384].T
     k.grad_head_bias[...] = columns[0:1, 0:22]
     loss = columns[1:2, :]
@@ -1726,13 +1898,7 @@
     )
     k.grad_log_vars[...] = (1.0 - weighted)[:, 0:3]
 
-    def input_rows(at):
-        total = k.shortcut[at, :]
-        for b in range(4):
-            total = total + mm_t(k.grad_reduced[at, b * 128 : b * 128 + 128], k.w_reduce[b])
-        k.grad_input[at, :] = total
-
-    each_rows(1536, 384, input_rows)
+    leave.wait()
 
 
 def run_finish(args):
@@ -1742,7 +1908,7 @@
         None,
         args,
         dict(
-            features=((1536, 64), BF16),
+            features=((12, 64, 128), BF16),
             total_loss=((1, 1), F32),
             grad_input=((1536, 512), F32),
             grad_reduce=((256, 128), F32),
@@ -1756,14 +1922,16 @@
             grad_pool=((64, 256), F32),
             grad_norm_b=((2, 4, 64), F32),
             grad_norm_pool=((2, 64), F32),
-            grad_project=((64, 5, 32), F32),
+            grad_project=((5, 32, 64), F32),
             grad_norm_p=((2, 64), F32),
-            grad_head_weight=((256, 22), F32),
+            grad_head_weight=((22, 256), F32),
             grad_head_bias=((1, 22), F32),
             grad_log_vars=((1, 3), F32),
         ),
-        {},
+        dict(turned=pltpu.VMEM((384, 64), F32), sem=pltpu.SemaphoreType.DMA((1,))),
         0,
+        hbm=("grad_input",),
+        stream=("from_input", "grad_rates"),
         smem=("boxes", "log_vars"),
     )
 
@@ -1800,7 +1968,7 @@
             w_expand=conv_expand,
             aspp_point=aspp_point,
             aspp_rates=aspp_rates,
-            project=aspp_project.reshape(64, 1280),
+            project=aspp_project.transpose(1, 0, 2),
             affine_1=reduction_norm_params,
             affine_2=dilated_norm_params,
             affine_3=expansion_norm_params,
@@ -1818,13 +1986,13 @@
             norm_project=projection_norm_params,
             norm_pooling=pooling_norm_params,
             aspp_pool=aspp_pool,
-            w_slots=forward.w_project.reshape(256, 1280),
-            head_weight=head_weight,
+            w_slots=forward.w_project,
+            head_weight=head_weight.T,
             head_bias=head_bias,
             log_vars=log_vars,
-            labels=seg_labels,
-            depth=depth_target,
-            normal=normal_target,
+            labels=seg_labels.transpose(1, 0, 2),
+            depth=depth_target.transpose(1, 0, 2),
+            normal=normal_target.transpose(0, 2, 1, 3).reshape(12, 2, 128),
             boxes=crop_boxes,
         )
     )
@@ -1847,6 +2015,8 @@
     last = run_bottleneck_backward(
         dict(
             grad_expanded=back.grad_expanded,
+            shortcut=back.shortcut,
+            w_reduce=forward.w_reduce,
             half_pyramid=back.half_pyramid,
             sum_pyramid=back.sum_pyramid,
             sum_project=back.sum_project,
@@ -1867,9 +2037,7 @@
     )
     done = run_finish(
         dict(
-            shortcut=back.shortcut,
-            grad_reduced=last.grad_reduced,
-            w_reduce=forward.w_reduce,
+            from_input=last.grad_input,
             own_pyramid=last.own_pyramid,
             packed=middle.features,
             own_project=last.own_project,
@@ -1889,7 +2057,7 @@
         )
     )
     return (
-        done.features.reshape(1, 12, 128, 64),
+        done.features.transpose(0, 2, 1).reshape(1, 12, 128, 64),
         done.total_loss.reshape(()),
         done.grad_input.reshape(1, 12, 128, 512),
         done.grad_reduce,
@@ -1903,9 +2071,9 @@
         done.grad_pool,
         done.grad_norm_b,
         done.grad_norm_pool,
-        done.grad_project,
+        done.grad_project.transpose(2, 0, 1),
         done.grad_norm_p,
-        done.grad_head_weight,
+        done.grad_head_weight.T,
         done.grad_head_bias.reshape(22),
         done.grad_log_vars.reshape(3),
     )

time: 411 us -> 375 us (0.912)
  Pallas kernels: 396 us -> 373 us
  local copies, waits for them, and re-layouts: 12.1 us -> 0 us
    pallas_call x5, Pallas kernels: 396 us -> 373 us  [call_kernel(): pl.pallas_call(kernel, out_shape=[jax.ShapeDtypeStruct(s, d) for s, d in...]
    unnamed x7 -> x0, local copies, waits for them, and re-layouts: 10.5 us -> none
where the time goes in v4:
time: 375 us; the launch traced here: 374 us
  Pallas kernels  373 us (99%)
    pallas_call x5, Pallas kernels, call_kernel(): pl.pallas_call(kernel, out_shape=[jax.ShapeDtypeStruct(s, d) for s, d in...  373 us

profile of v4, /device:TPU:0, one launch (start us, length us, event | category | flops | bytes accessed | tf_op | source)
XLA Modules:
  0.0 373.7 jit_solution(736539513808542651)
XLA Ops:
  0.7 94.7 %bottleneck.1 = (f32[1536,128]{1,0:T(8,128)}, bf16[4,512,128]{2,1,0:T(8,128)(2,1)}, bf16[13,4,64,512]{3,2,1,0:T(8,128)(2,1)}, bf16[4,5,64,256]{3,2,1,0:T(8,128)(...) custom-call(bf16[1536,512]{1,0:T(8,128)(2,1)} %bitcast.20, ...), custom_call_target="tpu_custom_call" | custom-call | tf_op jit(solution)/shard_map/bottleneck/pallas_call | solution.py:488
  95.4 101.4 %pyramid.1 = (bf16[768,128]{1,0:T(8,128)(2,1)}, f32[8,128]{1,0:T(8,128)}, bf16[8,32,384]{2,1,0:T(8,128)(2,1)}, bf16[8,64,256]{2,1,0:T(8,128)(2,1)}, f32[8,256]{1...) custom-call(bf16[1536,512]{1,0:T(8,128)(2,1)} %get-tuple-element.75.refs_0_.re, ...), custom_call_target="tpu_custom_call" | custom-call | tf_op jit(solution)/shard_map/pyramid/pallas_call | solution.py:488
  196.8 69.8 %pyramid_back.1 = (f32[1536,512]{1,0:T(8,128)}, bf16[1536,512]{1,0:T(8,128)(2,1)}, f32[8,512]{1,0:T(8,128)}, bf16[4,16,32,512]{3,2,1,0:T(8,128)(2,1)}, bf16[16,3...) custom-call(bf16[1536,256]{1,0:T(8,128)(2,1)} %get-tuple-element.79.refs_0_, ...), custom_call_target="tpu_custom_call" | custom-call | tf_op jit(solution)/shard_map/pyramid_back/pallas_call | solution.py:488
  266.6 100.3 %bottleneck_back.1 = (f32[1536,512]{1,0:T(8,128)}, f32[8,128]{1,0:T(8,128)}, f32[8,128]{1,0:T(8,128)}, bf16[2,16,32,256]{3,2,1,0:T(8,128)(2,1)}, f32[2,32,384]{2...) custom-call(bf16[1536,512]{1,0:T(8,128)(2,1)} %get-tuple-element.85.refs_0_, ...), custom_call_target="tpu_custom_call" | custom-call | tf_op jit(solution)/shard_map/bottleneck_back/pallas_call | solution.py:488
  366.9 6.7 %finish.1 = (bf16[12,64,128]{2,1,0:T(8,128)(2,1)}, f32[1,1]{1,0:T(1,128)}, f32[1536,512]{1,0:T(8,128)}, f32[256,128]{1,0:T(8,128)}, f32[9,64,128]{2,1,0:T(8,128)...) custom-call(f32[1536,512]{1,0:T(8,128)} %get-tuple-element.97.refs_0, ...), custom_call_target="tpu_custom_call" | custom-call | tf_op jit(solution)/shard_map/finish/pallas_call | solution.py:488

commit v5 on v4

--- a/solution.py
+++ b/solution.py
@@ -444,25 +444,25 @@
         for copy in self.ins.values():
             copy.start()
 
-    def need(self, *names):
+    def need(self, **names):
         for name in names:
             self.ins.pop(name).wait()
 
-    def done(self, *names):
+    def done(self, **names):
         for name in names:
             copy = self.outs.pop(name)
             copy.start()
             self.left.append(copy)
 
     def finish(self):
-        self.need(*list(self.ins))
-        self.done(*list(self.outs))
+        self.need(**dict.fromkeys(self.ins))
+        self.done(**dict.fromkeys(self.outs))
         for copy in self.left:
             copy.wait()
 
 
 def call_kernel(
-    body, name, number, args, outs, scratch, sems, hbm=(), smem=("boxes",), stream=()
+    body, name, number, args, outs, scratch, sems, hbm={}, smem=dict(boxes=1), stream={}
 ):
     vmem, anywhere = pl.BlockSpec(memory_space=pltpu.VMEM), pl.BlockSpec(memory_space=pl.ANY)
     stream_in = [n for n in args if n in stream]
@@ -588,8 +588,8 @@
         return carry
 
     lax.fori_loop(0, 12, mask_rows, 0)
-    k.stream.done("mask")
-    k.stream.need("x")
+    k.stream.done(mask=1)
+    k.stream.need(x=1)
 
     def reduce_for(b):
         def reduce_rows(at):
@@ -604,7 +604,7 @@
     arrivals[2].wait()
     reduce_for(net.m ^ 2)
     arrivals[0].wait()
-    k.stream.done("w_reduce")
+    k.stream.done(w_reduce=1)
 
     def far_half(half):
         def reduce_rows(at):
@@ -614,7 +614,7 @@
         each_rows(768, 384, reduce_rows)
 
     sum_scatter(net, k.part, scatter_refs(k, "sum"), k.reduced, produce=far_half)
-    k.stream.done("reduced")
+    k.stream.done(reduced=1)
 
     half = pl.ds(pl.multiple_of(net.r * 32, 32), 32)
     late = []
@@ -661,7 +661,7 @@
     for load in loads:
         load.wait()
     halo.wait()
-    k.stream.done("hidden")
+    k.stream.done(hidden=1)
 
     def dilated_rows(i, carry):
         total = 0.0
@@ -681,7 +681,7 @@
         return carry
 
     lax.fori_loop(0, 12, add_columns, 0)
-    k.stream.done("dilated")
+    k.stream.done(dilated=1)
     mean_2, inverse_2 = statistics(net, k.dilated, k.mask, counts, k.out_2, k.in_2, counted)
     keep_rows(k.stats_2, mean_2, inverse_2)
 
@@ -692,14 +692,14 @@
     each_rows(1536, 128, activate_2)
     gather_blocks(net, lambda b, at: k.hidden_two.at[at, lane_block(b)], 1536)
     spread_weights(1, 2)
-    k.stream.done("hidden_two")
-    k.stream.need("w_expand")
+    k.stream.done(hidden_two=1)
+    k.stream.need(w_expand=1)
 
     def expand_rows(at):
         k.expanded[at, :] = mm(k.hidden_two[at, :], k.w_expand[...])
 
     each_rows(1536, 384, expand_rows)
-    k.stream.done("expanded")
+    k.stream.done(expanded=1)
     mean_3, inverse_3 = statistics(net, k.expanded, k.mask, counts, k.out_3, k.in_3, counted)
     keep_rows(k.stats_3, mean_3, inverse_3)
     for copy in late:
@@ -752,26 +752,8 @@
             local_sems=pltpu.SemaphoreType.DMA((16,)),
         ),
         96,
-        hbm=(
-            "conv_reduce",
-            "w_dilated",
-            "aspp_point",
-            "aspp_rates",
-            "project",
-            "w_pyramid",
-            "w_project",
-        ),
-        stream=(
-            "x",
-            "w_expand",
-            "mask",
-            "w_reduce",
-            "reduced",
-            "hidden",
-            "dilated",
-            "hidden_two",
-            "expanded",
-        ),
+        hbm=dict(conv_reduce=1, w_dilated=1, aspp_point=1, aspp_rates=1, project=1, w_pyramid=1, w_project=1),
+        stream=dict(x=1, w_expand=1, mask=1, w_reduce=1, reduced=1, hidden=1, dilated=1, hidden_two=1, expanded=1),
     )
 
 
@@ -794,7 +776,7 @@
     k.head_rows[...] = jnp.zeros((32, 256), F32)
     k.head_rows[0:22, :] = k.head_weight[...].astype(F32)
 
-    k.stream.need("mask")
+    k.stream.need(mask=1)
 
     (own_sum,) = column_sums(
         lambda at: (k.trunk[at, :].astype(F32) * wide(k.mask[at, :], 512),), 1536, 512, 1
@@ -827,7 +809,7 @@
         k.edge_out[rows_of(i), :] = total.astype(BF16)
         return carry
 
-    k.stream.need("w_pyramid")
+    k.stream.need(w_pyramid=1)
     lax.fori_loop(0, 4, edge_rows, 0)
     edge = net.send(k.edge_out, k.edge_in, net.core)
 
@@ -1173,8 +1155,8 @@
             **exchange_scratch(4),
         ),
         96,
-        smem=("boxes", "head_bias", "log_vars"),
-        stream=("mask", "w_pyramid"),
+        smem=dict(boxes=1, head_bias=1, log_vars=1),
+        stream=dict(mask=1, w_pyramid=1),
     )
 
 
@@ -1189,8 +1171,8 @@
         target[z] = total.astype(target.dtype)
 
 
-def chunk_of(z):
-    return 2 * lax.rem(z, 2) + z // 2
+def chunk_of(net):
+    return lambda z: 2 * lax.rem(z + net.m, 2) + z // 2
 
 
 def along_z(net, source, target, chunk=lambda z: z):
@@ -1210,9 +1192,10 @@
 class PairSums:
     def __init__(self, net, half, other, pair, last):
         self.net, self.half, self.other, self.pair, self.last = net, half, other, pair, last
-        kept, away = lax.rem(net.z, 2), lax.rem(net.z + 1, 2)
+        kept, away = lax.rem(net.z + net.m, 2), lax.rem(net.z + net.m + 1, 2)
         self.kept = 2 * kept
-        self.first = self.copy(half.at[pl.ds(2 * away, 2)], other, net.z + 1 - 2 * kept)
+        beside = net.z + 1 - 2 * lax.rem(net.z, 2)
+        self.first = self.copy(half.at[pl.ds(2 * away, 2)], other, beside)
         self.high = net.z // 2
         self.second = self.copy(pair.at[1 - self.high], last, net.z + 2 - 4 * self.high)
 
@@ -1248,10 +1231,11 @@
 
         def body(i, carry):
             total = self.pair[self.high, i].astype(F32) + self.last[i].astype(F32)
-            target[i] = total.astype(BF16)
+            target[0, i] = total[:, 0:256].astype(BF16)
+            target[1, i] = total[:, 256:512].astype(BF16)
             return carry
 
-        lax.fori_loop(0, target.shape[0], body, 0)
+        lax.fori_loop(0, target.shape[1], body, 0)
 
 
 def pyramid_backward(net, k):
@@ -1370,7 +1354,7 @@
         build(near)
         copy.wait()
         build_edge(near)
-        k.stream.need("trunk")
+        k.stream.need(trunk=1)
         weight_gradients(near)
         first_swap.append(to_core(near))
         pl.when(mine_second)(first_swap[0].start)
@@ -1382,7 +1366,7 @@
         swap.wait()
     add_halves(net, k.grad_project, k.core_project, k.half_project)
     add_halves(net, k.grad_pool, k.core_pool, k.half_pool)
-    small_moves = along_z(net, k.half_project, k.z_project, chunk_of)
+    small_moves = along_z(net, k.half_project, k.z_project, chunk_of(net))
     small_moves = small_moves + along_z(net, k.half_pool, k.z_pool)
     copy.wait()
     build_edge(far)
@@ -1401,7 +1385,7 @@
         k.shortcut[rows_of(i), :] = total
         return carry
 
-    k.stream.need("w_pyramid", "expanded", "x", "mask")
+    k.stream.need(w_pyramid=1, expanded=1, x=1, mask=1)
     lax.fori_loop(0, 4, trunk_rows, 0)
     mean, inverse = k.stats_3[0:1, :], k.stats_3[1:2, :]
     gain, bias = k.affine_3[0:1, :], k.affine_3[1:2, :]
@@ -1416,7 +1400,7 @@
         k.shortcut[at, :] = grad * slope(u)
 
     each_rows(1536, 32, back_trunk)
-    k.stream.done("shortcut")
+    k.stream.done(shortcut=1)
 
     second_swap = to_core(far)
 
@@ -1439,10 +1423,10 @@
         k.grad_expanded[at, :] = (inverse * grad).astype(BF16)
 
     each_rows(1536, 32, back_expanded)
-    k.stream.done("grad_expanded")
+    k.stream.done(grad_expanded=1)
     for move_ in small_moves:
         move_.wait()
-    k.sum_project[...] = finish_z(net, k.half_project, k.z_project, chunk_of)
+    k.sum_project[...] = finish_z(net, k.half_project, k.z_project, chunk_of(net)).astype(BF16)
     k.sum_pool[...] = finish_z(net, k.half_pool, k.z_pool)
 
     @pl.when(mine_second)
@@ -1476,8 +1460,8 @@
             grad_expanded=((1536, 512), BF16),
             norm_3=((8, 512), F32),
             half_pyramid=((4, 16, 32, 512), BF16),
-            sum_pyramid=((16, 32, 512), BF16),
-            sum_project=((32, 384), F32),
+            sum_pyramid=((2, 16, 32, 256), BF16),
+            sum_project=((32, 384), BF16),
             sum_pool=((64, 256), F32),
         ),
         dict(
@@ -1497,50 +1481,48 @@
             **exchange_scratch(1),
         ),
         48,
-        stream=("w_pyramid", "expanded", "x", "mask", "trunk", "shortcut", "grad_expanded"),
+        stream=dict(w_pyramid=1, expanded=1, x=1, mask=1, trunk=1, shortcut=1, grad_expanded=1),
     )
 
 
 def bottleneck_backward(net, k):
     counted = pixel_count(k.boxes)
     loads = load_taps(k)
-    high = net.z // 2
+    high, source = net.z // 2, net.slot // 2
+    here = net.m * 8 + net.slot
     owners, givers = [], []
-    for which in (high, 1 - high):
-        part = 2 * net.m + which
-        owners.append((2 * net.r + lax.rem(net.z, 2), part // 4, lax.rem(part, 4)))
-    odd = lax.rem(net.z, 2)
-    for which in (odd, 1 - odd):
-        givers.append((net.slot // 2, net.m // 2, lax.rem(net.m, 2) + 2 * which))
-    here = net.m * 8 + net.slot
-    moves = owners[0][0] * 8 + owners[0][1] * 4 + owners[0][2] != here
+    for i in range(2):
+        part = 2 * net.m + i
+        column = 2 * net.r + lax.rem(net.z + net.m, 2)
+        owners.append((column, part // 4, lax.rem(part, 4)))
+        givers.append((source, net.m // 2, lax.rem(net.m + source, 2) + 2 * i))
+
+    def elsewhere(device):
+        return device[0] * 8 + device[1] * 4 + device[2] != here
+
+    moves = elsewhere(owners[0])
     stays = jnp.logical_not(moves)
     greet(
-        [net.side, net.over] + net.group + [owners[1], givers[1]],
-        [(owners[0], moves), (givers[0], moves)],
-    )
-
-    def to_owners(views, arrived, sem, start=True):
-        first = pltpu.make_async_remote_copy(
-            src_ref=views(0),
-            dst_ref=arrived.at[0],
-            send_sem=net.send_sems.at[net.count],
-            recv_sem=net.recv_sems.at[net.count],
-            device_id=owners[0],
-            device_id_type=MESH,
-        )
-        net.count += 1
-        kept = pltpu.make_async_copy(views(0), arrived.at[0], sem)
-        i = net.count
-        net.count += 1
-        second = pltpu.make_async_remote_copy(
-            src_ref=views(1),
-            dst_ref=arrived.at[1],
-            send_sem=net.send_sems.at[i],
-            recv_sem=net.recv_sems.at[i],
-            device_id=owners[1],
-            device_id_type=MESH,
-        )
+        [net.side, net.over, net.diagonal] + net.group + [owners[1]],
+        [(owners[0], moves), (givers[0], elsewhere(givers[0])), (givers[1], elsewhere(givers[1]))],
+    )
+
+    def to_owners(views, arrived, sem):
+        base = net.count
+        net.count += 2
+
+        def copy(i, g, device):
+            return pltpu.make_async_remote_copy(
+                src_ref=views(i),
+                dst_ref=arrived.at[g],
+                send_sem=net.send_sems.at[base + i],
+                recv_sem=net.recv_sems.at[base + g],
+                device_id=device,
+                device_id_type=MESH,
+            )
+
+        first, second = copy(0, high, owners[0]), copy(1, high, owners[1])
+        kept = pltpu.make_async_copy(views(0), arrived.at[high], sem)
 
         def begin():
             pl.when(moves)(first.start)
@@ -1548,25 +1530,84 @@
             second.start()
 
         def wait():
-            pl.when(moves)(first.wait)
+            pl.when(moves)(first.wait_send)
             pl.when(stays)(kept.wait)
-            second.wait()
-
-        if start:
-            begin()
-            return wait
-        return begin, wait
+            second.wait_send()
+            for g in range(2):
+                pl.when(elsewhere(givers[g]))(copy(0, g, owners[1]).wait_recv)
+
+        begin()
+        return wait
 
     def lanes_for(i):
-        return lane_block(high if i == 0 else 1 - high, 256)
+        return pl.ds(i * 256, 256)
 
     early = net.r == net.m // 2
     is_late = net.r == 1 - net.m // 2
     pair_sums = PairSums(net, k.far_half_pyramid, k.z_other, k.z_pair, k.z_last)
 
-    begin_pyramid, wait_pyramid = to_owners(
-        lambda i: k.pyramid_sum.at[:, :, lanes_for(i)], k.own_pyramid, k.local_sems.at[9], False
-    )
+    odd_z = lax.rem(net.z, 2)
+    lone = early & (odd_z == 0)
+    beside = early & (odd_z == 1)
+    stay = pltpu.make_async_copy(k.pyramid_sum, k.relay.at[0], k.local_sems.at[9])
+
+    def remote(src, dst, send, arrive, device):
+        return pltpu.make_async_remote_copy(
+            src_ref=src,
+            dst_ref=dst,
+            send_sem=net.send_sems.at[send],
+            recv_sem=net.recv_sems.at[arrive],
+            device_id=device,
+            device_id_type=MESH,
+        )
+
+    base = net.count
+    net.count += 6
+    to_side = remote(k.pyramid_sum, k.relay.at[0], base, base, net.side)
+    across = (net.m ^ (2 + odd_z), net.r, net.z)
+    to_across = remote(k.pyramid_sum, k.relay.at[1], base + 1, base + 1, across)
+    plane = lax.rem(net.m + net.z, 2)
+
+    def forward(e, i):
+        device = (net.m, net.r if e == 0 else 1 - net.r, 2 * plane + i)
+        return remote(
+            k.relay.at[e, i], k.own_pyramid.at[high], base + 2 + 2 * e + i, base + 2 + high, device
+        )
+
+    forwards = [[forward(e, i) for i in range(2)] for e in range(2)]
+    keep = pltpu.make_async_copy(k.relay.at[0, odd_z], k.own_pyramid.at[high], k.local_sems.at[12])
+    keeps = early & (plane == high)
+
+    def kept_here(i):
+        return keeps & (odd_z == i)
+
+    def begin_early():
+        pl.when(lone)(stay.start)
+        pl.when(beside)(to_side.start)
+
+    def relay_early():
+        pl.when(lone)(stay.wait)
+        pl.when(beside)(to_side.wait)
+        for i in range(2):
+            pl.when(early & jnp.logical_not(kept_here(i)))(forwards[0][i].start)
+        pl.when(keeps)(keep.start)
+
+    def relay_late():
+        pl.when(early)(to_across.wait_recv)
+        for i in range(2):
+            pl.when(early)(forwards[1][i].start)
+
+    def wait_pyramid():
+        pl.when(is_late)(to_across.wait_send)
+        for i in range(2):
+            pl.when(early & jnp.logical_not(kept_here(i)))(forwards[0][i].wait_send)
+            pl.when(early)(forwards[1][i].wait_send)
+        pl.when(keeps)(keep.wait)
+        for g in range(2):
+            local = early & (lax.rem(net.z // 2 + net.m, 2) + 2 * g == net.z)
+            arrival = remote(k.relay.at[0, 0], k.own_pyramid.at[g], base, base + 2 + g, net.core)
+            pl.when(jnp.logical_not(local))(arrival.wait_recv)
+
 
     @pl.when(is_late)
     def _():
@@ -1575,7 +1616,6 @@
     @pl.when(early)
     def _():
         k.pyramid_sum[...] = k.sum_pyramid[...]
-        begin_pyramid()
 
     wait_project = to_owners(lambda i: k.sum_project, k.own_project, k.local_sems.at[10])
 
@@ -1594,7 +1634,7 @@
     swaps, late_moves = [], []
 
     def expand_gradient():
-        k.stream.need("hidden_two")
+        k.stream.need(hidden_two=1)
 
         def body(b, carry):
             grad = tm_m(k.hidden_two[:, lane_block(b)], k.grad_expanded[...])
@@ -1605,7 +1645,7 @@
         swaps.append(core_halves(net, k.grad_expand, k.core_expand))
 
     sum_scatter(net, k.part, scatter_refs(k, "sum"), k.grad_2, meanwhile=expand_gradient, produce=expand_half)
-    k.stream.need("dilated", "mask")
+    k.stream.need(dilated=1, mask=1)
 
     def norm_back(grad, value, stats, affine, outgoing, incoming, store, kept, meanwhile=None):
         mean, inverse = stats[0:1, :], stats[1:2, :]
@@ -1634,7 +1674,8 @@
         k.grad_pad[pl.ds(pl.multiple_of(at.start + 512, 128), 128), :] = value
 
     def pass_expand():
-        k.stream.need("half_pyramid")
+        k.stream.need(half_pyramid=1)
+        begin_early()
 
         @pl.when(is_late)
         def _():
@@ -1685,7 +1726,7 @@
         lax.fori_loop(2 * half, 2 * half + 2, dilated_rows, 0)
 
     def dilated_gradient():
-        k.stream.need("hidden")
+        k.stream.need(hidden=1)
 
         for i in range(3):
 
@@ -1702,7 +1743,7 @@
         swaps.append(core_halves(net, k.grad_dilated, k.core_dilated))
 
     sum_scatter(net, k.part, scatter_refs(k, "sum2"), k.grad_1, meanwhile=dilated_gradient, produce=dilated_half)
-    k.stream.need("reduced")
+    k.stream.need(reduced=1)
 
     def store_1(at, value):
         k.grad_reduced[at, lane_block(net.m)] = value
@@ -1711,8 +1752,9 @@
         @pl.when(is_late)
         def _():
             pair_sums.finish(k.pyramid_sum)
-            begin_pyramid()
-
+            to_across.start()
+
+        relay_early()
         swaps.pop().wait()
         add_halves(net, k.grad_dilated, k.core_dilated, k.half_dilated)
         late_moves.extend(along_z(net, k.half_dilated, k.z_dilated))
@@ -1730,7 +1772,8 @@
     )
     gather_blocks(net, lambda b, at: k.grad_reduced.at[at, lane_block(b)], 1536)
 
-    k.stream.need("x")
+    relay_late()
+    k.stream.need(x=1)
 
     def reduce_gradient(b, carry):
         grad = tm_m(k.grad_reduced[:, lane_block(b)], k.x[...])
@@ -1742,9 +1785,9 @@
 
     swap.wait()
     add_halves(net, k.grad_reduce, k.core_reduce, k.half_reduce)
-    reduce_moves = along_z(net, k.half_reduce, k.z_reduce, chunk_of)
-
-    k.stream.need("shortcut", "w_reduce")
+    reduce_moves = along_z(net, k.half_reduce, k.z_reduce, chunk_of(net))
+
+    k.stream.need(shortcut=1, w_reduce=1)
 
     def input_rows(at):
         total = k.shortcut[at, :]
@@ -1753,10 +1796,10 @@
         k.grad_input[at, :] = total
 
     each_rows(1536, 384, input_rows)
-    k.stream.done("grad_input")
+    k.stream.done(grad_input=1)
     for move_ in reduce_moves:
         move_.wait()
-    k.sum_reduce[...] = finish_z(net, k.half_reduce, k.z_reduce, chunk_of)
+    k.sum_reduce[...] = finish_z(net, k.half_reduce, k.z_reduce, chunk_of(net)).astype(BF16)
     wait_reduce = to_owners(
         lambda i: k.sum_reduce.at[:, lanes_for(i)], k.own_reduce, k.local_sems.at[11]
     )
@@ -1780,17 +1823,18 @@
             norm_2=((8, 128), F32),
             norm_1=((8, 128), F32),
             own_pyramid=((2, 16, 32, 256), BF16),
-            own_project=((2, 32, 384), F32),
+            own_project=((2, 32, 384), BF16),
             sum_dilated=((576, 128), F32),
             sum_expand=((64, 512), F32),
-            own_reduce=((2, 64, 256), F32),
+            own_reduce=((2, 64, 256), BF16),
         ),
         dict(
             grad_taps=pltpu.VMEM((2560, 384), BF16),
             grad_reduced=pltpu.VMEM((1536, 512), BF16),
             **pair_scratch(),
-            pyramid_sum=pltpu.VMEM((16, 32, 512), BF16),
-            sum_reduce=pltpu.VMEM((64, 512), F32),
+            relay=pltpu.VMEM((2, 2, 16, 32, 256), BF16),
+            pyramid_sum=pltpu.VMEM((2, 16, 32, 256), BF16),
+            sum_reduce=pltpu.VMEM((64, 512), BF16),
             grad_expand=pltpu.VMEM((8, 64, 512), BF16),
             core_expand=pltpu.VMEM((4, 64, 512), BF16),
             half_expand=pltpu.VMEM((4, 64, 512), BF16),
@@ -1813,22 +1857,11 @@
             cells=pltpu.VMEM((20, 144, 128), F32),
             **exchange_scratch(2),
             **exchange_scratch(1),
-            local_sems=pltpu.SemaphoreType.DMA((12,)),
+            local_sems=pltpu.SemaphoreType.DMA((13,)),
         ),
         96,
-        hbm=("w_dilated",),
-        stream=(
-            "half_pyramid",
-            "hidden_two",
-            "dilated",
-            "mask",
-            "hidden",
-            "reduced",
-            "x",
-            "shortcut",
-            "w_reduce",
-            "grad_input",
-        ),
+        hbm=dict(w_dilated=1),
+        stream=dict(half_pyramid=1, hidden_two=1, dilated=1, mask=1, hidden=1, reduced=1, x=1, shortcut=1, w_reduce=1, grad_input=1),
     )
 
 
@@ -1837,7 +1870,7 @@
     odd = lax.rem(lax.axis_index("batch"), 2)
 
     def rows_for(i):
-        return pl.ds(pl.multiple_of((odd if i == 0 else 1 - odd) * 32, 32), 32)
+        return slice(i * 32, i * 32 + 32)
 
     nothing = jnp.zeros((64, 256), F32)
     for tap in (9, 10, 11, 15, 16, 17, 18, 19, 20, 24, 25, 26):
@@ -1850,23 +1883,21 @@
             else:
                 tap = slot - 1 if slot < 10 else slot + 2 if slot < 13 else slot + 8
                 k.grad_rates[tap, rows_for(i), :] = block
-    k.stream.done("grad_rates")
-    k.stream.need("from_input")
+    k.stream.done(grad_rates=1)
+    k.stream.need(from_input=1)
     leave = pltpu.make_async_copy(k.from_input, k.grad_input, k.sem.at[0])
     leave.start()
     for y in range(6):
         turned = k.packed[y * 128 : y * 128 + 128, :].astype(F32).T.astype(BF16)
         k.features[y] = turned[0:64, :]
         k.features[y + 6] = turned[64:128, :]
-    rows = jnp.concatenate([k.own_project[0], k.own_project[1]], axis=0)
-    swapped = jnp.concatenate([k.own_project[1], k.own_project[0]], axis=0)
-    k.turned[...] = jnp.where(odd == 0, rows, swapped).T
+    k.turned[...] = jnp.concatenate([k.own_project[i].astype(F32) for i in range(2)], axis=0).T
     for slot in range(5):
         start = pl.multiple_of(slot * 64 + odd * 32, 32)
         k.grad_project[slot] = k.turned[pl.ds(start, 32), :]
-    rows = jnp.concatenate([k.own_reduce[0], k.own_reduce[1]], axis=0)
-    swapped = jnp.concatenate([k.own_reduce[1], k.own_reduce[0]], axis=0)
-    k.grad_reduce[...] = jnp.where(odd == 0, rows, swapped).T
+    k.grad_reduce[...] = jnp.concatenate(
+        [k.own_reduce[i].astype(F32) for i in range(2)], axis=0
+    ).T
     k.grad_dilated[...] = k.from_dilated[...].reshape(9, 64, 128)
     k.grad_expand[...] = k.from_expand[...]
     k.grad_pool[...] = k.from_pool[...]
@@ -1930,9 +1961,9 @@
         ),
         dict(turned=pltpu.VMEM((384, 64), F32), sem=pltpu.SemaphoreType.DMA((1,))),
         0,
-        hbm=("grad_input",),
-        stream=("from_input", "grad_rates"),
-        smem=("boxes", "log_vars"),
+        hbm=dict(grad_input=1),
+        stream=dict(from_input=1, grad_rates=1),
+        smem=dict(boxes=1, log_vars=1),
     )
 
 

time: 375 us -> 363 us (0.968)
  Pallas kernels: 373 us -> 362 us
    pallas_call x5, Pallas kernels: 373 us -> 362 us  [call_kernel(): pl.pallas_call(kernel, out_shape=[jax.ShapeDtypeStruct(s, d) for s, d in...]
where the time goes in v5:
time: 363 us; the launch traced here: 362 us
  Pallas kernels  362 us (100%)
    pallas_call x5, Pallas kernels, call_kernel(): pl.pallas_call(kernel, out_shape=[jax.ShapeDtypeStruct(s, d) for s, d in...  362 us

profile of v5, /device:TPU:0, one launch (start us, length us, event | category | flops | bytes accessed | tf_op | source)
XLA Modules:
  0.0 362.4 jit_solution(17389077500989412660)
XLA Ops:
  0.7 94.7 %bottleneck.1 = (f32[1536,128]{1,0:T(8,128)}, bf16[4,512,128]{2,1,0:T(8,128)(2,1)}, bf16[13,4,64,512]{3,2,1,0:T(8,128)(2,1)}, bf16[4,5,64,256]{3,2,1,0:T(8,128)(...) custom-call(bf16[1536,512]{1,0:T(8,128)(2,1)} %bitcast.20, ...), custom_call_target="tpu_custom_call" | custom-call | tf_op jit(solution)/shard_map/bottleneck/pallas_call | solution.py:488
  95.4 101.4 %pyramid.1 = (bf16[768,128]{1,0:T(8,128)(2,1)}, f32[8,128]{1,0:T(8,128)}, bf16[8,32,384]{2,1,0:T(8,128)(2,1)}, bf16[8,64,256]{2,1,0:T(8,128)(2,1)}, f32[8,256]{1...) custom-call(bf16[1536,512]{1,0:T(8,128)(2,1)} %get-tuple-element.75.refs_0_.re, ...), custom_call_target="tpu_custom_call" | custom-call | tf_op jit(solution)/shard_map/pyramid/pallas_call | solution.py:488
  196.8 69.8 %pyramid_back.1 = (f32[1536,512]{1,0:T(8,128)}, bf16[1536,512]{1,0:T(8,128)(2,1)}, f32[8,512]{1,0:T(8,128)}, bf16[4,16,32,512]{3,2,1,0:T(8,128)(2,1)}, bf16[2,16...) custom-call(bf16[1536,256]{1,0:T(8,128)(2,1)} %get-tuple-element.79.refs_0_, ...), custom_call_target="tpu_custom_call" | custom-call | tf_op jit(solution)/shard_map/pyramid_back/pallas_call | solution.py:488
  266.6 88.9 %bottleneck_back.1 = (f32[1536,512]{1,0:T(8,128)}, f32[8,128]{1,0:T(8,128)}, f32[8,128]{1,0:T(8,128)}, bf16[2,16,32,256]{3,2,1,0:T(8,128)(2,1)}, bf16[2,32,384]{...) custom-call(bf16[1536,512]{1,0:T(8,128)(2,1)} %get-tuple-element.85.refs_0_, ...), custom_call_target="tpu_custom_call" | custom-call | tf_op jit(solution)/shard_map/bottleneck_back/pallas_call | solution.py:488
  355.6 6.6 %finish.1 = (bf16[12,64,128]{2,1,0:T(8,128)(2,1)}, f32[1,1]{1,0:T(1,128)}, f32[1536,512]{1,0:T(8,128)}, f32[256,128]{1,0:T(8,128)}, f32[9,64,128]{2,1,0:T(8,128)...) custom-call(f32[1536,512]{1,0:T(8,128)} %get-tuple-element.97.refs_0, ...), custom_call_target="tpu_custom_call" | custom-call | tf_op jit(solution)/shard_map/finish/pallas_call | solution.py:488

commit v6 on v5

--- a/solution.py
+++ b/solution.py
@@ -305,12 +305,14 @@
     head, tail = pl.ds(0, half), pl.ds(half, half)
     across, side, over = net.m ^ 3, net.m ^ 1, net.m ^ 2
 
-    def fill(target, index, base):
+    def fill(target, index, base, count=half):
+        size = min(step, count) if count % step == 0 else 64
+
         def body(at):
-            rows_at = pl.ds(pl.multiple_of(at.start + base, step), step)
+            rows_at = pl.ds(pl.multiple_of(at.start + base, size), size)
             target[rows_at, :] = part[index, rows_at, :].astype(BF16)
 
-        each_rows(half, step, body)
+        each_rows(count, size, body)
 
     def combine(target, index, base, arrived):
         def body(at):
@@ -319,22 +321,26 @@
 
         each_rows(half, step, body)
 
-    if produce is not None:
-        produce(0)
-    fill(far, across, 0)
-    first = net.send(far.at[head], far_side, net.side)
-    if produce is not None:
-        produce(1)
-    fill(far, across, half)
-    second = net.send(far.at[tail], far_over, net.over)
+    quarter, first, second = half // 2, [], []
+    for i in range(2):
+        if produce is not None:
+            produce(i)
+        at = pl.ds(i * quarter, quarter)
+        fill(far, across, i * quarter, quarter)
+        first.append(net.send(far.at[at], far_side.at[at], net.side))
+        fill(far, across, half + i * quarter, quarter)
+        below = pl.ds(half + i * quarter, quarter)
+        second.append(net.send(far.at[below], far_over.at[at], net.over))
     fill(to_side, side, 0)
     third = net.send(to_side.at[head], from_side.at[head], net.side)
     fill(to_over, over, half)
     fourth = net.send(to_over.at[tail], from_over.at[tail], net.over)
-    second.wait_recv()
+    for copy in second:
+        copy.wait_recv()
     combine(to_side, side, half, far_over)
     fifth = net.send(to_side.at[tail], from_side.at[tail], net.side)
-    first.wait_recv()
+    for copy in first:
+        copy.wait_recv()
     combine(to_over, over, 0, far_side)
     sixth = net.send(to_over.at[head], from_over.at[head], net.over)
     if meanwhile is not None:
@@ -348,7 +354,7 @@
         )
 
     each_rows(rows, step, body)
-    for copy in (first, second, third, fourth, fifth, sixth):
+    for copy in (*first, *second, third, fourth, fifth, sixth):
         copy.wait_send()
 
 
@@ -607,11 +613,9 @@
     k.stream.done(w_reduce=1)
 
     def far_half(half):
-        def reduce_rows(at):
-            at = pl.ds(pl.multiple_of(at.start + half * 768, 128), 384)
+        for i in (half, half + 2):
+            at = pl.ds(i * 384, 384)
             k.part[net.m ^ 3, at, :] = mm(k.x[at, :], k.w_reduce[net.m ^ 3])
-
-        each_rows(768, 384, reduce_rows)
 
     sum_scatter(net, k.part, scatter_refs(k, "sum"), k.reduced, produce=far_half)
     k.stream.done(reduced=1)
@@ -702,20 +706,13 @@
     k.stream.done(expanded=1)
     mean_3, inverse_3 = statistics(net, k.expanded, k.mask, counts, k.out_3, k.in_3, counted)
     keep_rows(k.stats_3, mean_3, inverse_3)
-    for copy in late:
-        copy.wait()
-    swaps = [
-        net.send(ref.at[..., half, :], ref.at[..., half, :], net.core)
-        for ref in (k.w_pyramid.at[pl.ds(0, 10)], k.w_project)
-    ]
-
     def activate_3(at):
         u = k.affine_3[0:1, :] * ((k.expanded[at, :] - mean_3) * inverse_3) + k.affine_3[1:2, :]
         u = u + k.x[at, :].astype(F32)
         k.trunk[at, :] = (u * sigmoid(u)).astype(BF16)
 
     each_rows(1536, 32, activate_3)
-    for copy in swaps:
+    for copy in late:
         copy.wait()
 
 
@@ -766,7 +763,24 @@
         for b in range(2)
         if a or b
     ]
+    own_rows = pl.ds(pl.multiple_of(net.r * 32, 32), 32)
+    common = (pl.ds(0, 10), slice(None), own_rows)
+    every = (slice(None), slice(None), own_rows)
+    weight_copies = [
+        pltpu.make_async_copy(source.at[view], target.at[view], k.local_sems.at[i])
+        for i, (source, target, view) in enumerate(
+            (
+                (k.far_pyramid, k.w_pyramid, common),
+                (k.far_pyramid, k.w_pyramid, pl.ds(10, 3)),
+                (k.far_slots, k.w_slots, every),
+            )
+        )
+    ]
+    for copy in weight_copies:
+        copy.start()
     greet(net.group + [peer for i, peer in enumerate(near) if i])
+    weight_copies.append(net.send(k.far_pyramid.at[common], k.w_pyramid.at[common], net.core))
+    weight_copies.append(net.send(k.far_slots.at[every], k.w_slots.at[every], net.core))
 
     for b in range(4):
         k.affine_b[0:2, b * 64 : b * 64 + 64] = k.branch_norms[:, b, :]
@@ -805,38 +819,48 @@
     def edge_rows(i, carry):
         total = 0.0
         for j in range(3):
-            total = total + mm_t(shifted(i, 12 * (j - 1)), k.w_pyramid[10 + j])
+            total = total + mm_t(shifted(i, 12 * (j - 1)), k.w_pyramid[10 + j].reshape(256, 512))
         k.edge_out[rows_of(i), :] = total.astype(BF16)
         return carry
 
-    k.stream.need(w_pyramid=1)
+    weight_copies.pop(1).wait()
     lax.fori_loop(0, 4, edge_rows, 0)
     edge = net.send(k.edge_out, k.edge_in, net.core)
 
     def outer_rows(i, carry):
         second, third = 0.0, 0.0
         for j in range(3):
-            second = second + mm_t(shifted(i, 24 * (j - 1)), k.w_pyramid[4 + j])
+            second = second + mm_t(shifted(i, 24 * (j - 1)), k.w_pyramid[4 + j].reshape(256, 512))
         for j in range(3):
-            third = third + mm_t(shifted(i, 36 * (j - 1)), k.w_pyramid[7 + j])
+            third = third + mm_t(shifted(i, 36 * (j - 1)), k.w_pyramid[7 + j].reshape(256, 512))
         for b, block in enumerate(pair(second, third)):
             k.part[b, rows_of(i), 128:256] = block
         return carry
 
     def inner_rows(i, carry):
-        point = mm_t(k.trunk[rows_of(i), :], k.w_pyramid[0])
+        point = mm_t(k.trunk[rows_of(i), :], k.w_pyramid[0].reshape(256, 512))
         first = k.edge_in[rows_of(i), :].astype(F32)
         for j in range(3):
-            first = first + mm_t(shifted(i, 12 * (j - 1)), k.w_pyramid[1 + j])
+            first = first + mm_t(shifted(i, 12 * (j - 1)), k.w_pyramid[1 + j].reshape(256, 512))
         for b, block in enumerate(pair(point, first)):
             k.part[b, rows_of(i), 0:128] = block
         return carry
 
+    def alternate(body, half):
+        def run(i, carry):
+            return body(half + 2 * i, carry)
+
+        lax.fori_loop(0, 2, run, 0)
+
     def half_tile(half):
-        lax.fori_loop(2 * half, 2 * half + 2, outer_rows, 0)
+        alternate(outer_rows, half)
         if half == 0:
             edge.wait()
-        lax.fori_loop(2 * half, 2 * half + 2, inner_rows, 0)
+        alternate(inner_rows, half)
+
+    for copy in weight_copies:
+        copy.wait()
+    k.stream.done(w_pyramid=1)
 
     sum_scatter(net, k.part, scatter_refs(k, "sum"), k.branches, produce=half_tile)
 
@@ -888,8 +912,8 @@
     pool_row = mm_t(pool_act, k.w_slot[...])[0:1, :]
 
     def project_rows(i, carry):
-        at = pl.ds(pl.multiple_of(i * 384, 128), 384)
-        below = pl.ds(pl.multiple_of(i * 384 + 768, 128), 384)
+        at = pl.ds(pl.multiple_of(i * 192, 64), 192)
+        below = pl.ds(pl.multiple_of(i * 192 + 768, 64), 192)
         first = mm_t(k.spatial[at, :], k.w_project[...]) + pool_row
         second = mm_t(k.spatial[below, :], k.w_project[...]) + pool_row
         for b, block in enumerate(pair(first, second)):
@@ -897,7 +921,7 @@
         return carry
 
     def project_half(half):
-        project_rows(half, 0)
+        alternate(project_rows, half)
 
     low_128 = lax.broadcasted_iota(jnp.int32, (128, 128), 1) < 64
 
@@ -1105,6 +1129,7 @@
         1,
         args,
         dict(
+            w_pyramid=((13, 4, 64, 512), BF16),
             features=((768, 128), BF16),
             norm_p=((8, 128), F32),
             grad_project=((8, 32, 384), BF16),
@@ -1116,6 +1141,8 @@
             head_sums=((32, 384), F32),
         ),
         dict(
+            w_slots=pltpu.VMEM((4, 5, 64, 256), BF16),
+            local_sems=pltpu.SemaphoreType.DMA((3,)),
             affine_b=pltpu.VMEM((8, 256), F32),
             affine_p=pltpu.VMEM((8, 128), F32),
             head_rows=pltpu.VMEM((32, 256), F32),
@@ -1156,6 +1183,7 @@
         ),
         96,
         smem=dict(boxes=1, head_bias=1, log_vars=1),
+        hbm=dict(far_pyramid=1, far_slots=1),
         stream=dict(mask=1, w_pyramid=1),
     )
 
@@ -1623,13 +1651,11 @@
         return pl.ds(pl.multiple_of(i * size, 128), size)
 
     def expand_half(half):
-        def expand_rows(at):
-            at = pl.ds(pl.multiple_of(at.start + half * 768, 128), 384)
+        for i in (half, half + 2):
+            at = pl.ds(i * 384, 384)
             total = mm_t(k.grad_expanded[at, :], k.w_expand[...])
             for b in range(4):
                 k.part[b, at, :] = total[:, b * 128 : b * 128 + 128]
-
-        each_rows(768, 384, expand_rows)
 
     swaps, late_moves = [], []
 
@@ -1723,7 +1749,10 @@
         return carry
 
     def dilated_half(half):
-        lax.fori_loop(2 * half, 2 * half + 2, dilated_rows, 0)
+        def run(i, carry):
+            return dilated_rows(half + 2 * i, carry)
+
+        lax.fori_loop(0, 2, run, 0)
 
     def dilated_gradient():
         k.stream.need(hidden=1)
@@ -2006,18 +2035,16 @@
             boxes=crop_boxes,
         )
     )
-    w_pyramid = forward.w_pyramid.reshape(13, 256, 512)
-
     middle = run_pyramid(
         dict(
             trunk=forward.trunk,
             mask=forward.mask,
-            w_pyramid=w_pyramid,
+            far_pyramid=forward.w_pyramid,
             branch_norms=branch_norms,
             norm_project=projection_norm_params,
             norm_pooling=pooling_norm_params,
             aspp_pool=aspp_pool,
-            w_slots=forward.w_project,
+            far_slots=forward.w_project,
             head_weight=head_weight.T,
             head_bias=head_bias,
             log_vars=log_vars,
@@ -2030,7 +2057,7 @@
     back = run_pyramid_backward(
         dict(
             grad_branches=middle.grad_branches,
-            w_pyramid=w_pyramid,
+            w_pyramid=middle.w_pyramid.reshape(13, 256, 512),
             x=x,
             trunk=forward.trunk,
             expanded=forward.expanded,

time: 363 us -> 356 us (0.981)
  Pallas kernels: 362 us -> 355 us
    pallas_call x5, Pallas kernels: 362 us -> 355 us  [call_kernel(): pl.pallas_call(kernel, out_shape=[jax.ShapeDtypeStruct(s, d) for s, d in...]
where the time goes in v6:
time: 356 us
  Pallas kernels  355 us (100%)
    pallas_call x5, Pallas kernels, call_kernel(): pl.pallas_call(kernel, out_shape=[jax.ShapeDtypeStruct(s, d) for s, d in...  355 us

profile of v6, /device:TPU:0, one launch (start us, length us, event | category | flops | bytes accessed | tf_op | source)
XLA Modules:
  0.0 356.1 jit_solution(8071217624673736949)
XLA Ops:
  0.7 90.5 %bottleneck.1 = (f32[1536,128]{1,0:T(8,128)}, bf16[4,512,128]{2,1,0:T(8,128)(2,1)}, bf16[13,4,64,512]{3,2,1,0:T(8,128)(2,1)}, bf16[4,5,64,256]{3,2,1,0:T(8,128)(...) custom-call(bf16[1536,512]{1,0:T(8,128)(2,1)} %bitcast.20, ...), custom_call_target="tpu_custom_call" | custom-call | tf_op jit(solution)/shard_map/bottleneck/pallas_call | solution.py:494
  91.2 97.5 %pyramid.1 = (bf16[13,4,64,512]{3,2,1,0:T(8,128)(2,1)}, bf16[768,128]{1,0:T(8,128)(2,1)}, f32[8,128]{1,0:T(8,128)}, bf16[8,32,384]{2,1,0:T(8,128)(2,1)}, bf16[8,...) custom-call(bf16[1536,512]{1,0:T(8,128)(2,1)} %get-tuple-element.76., ...), custom_call_target="tpu_custom_call" | custom-call | tf_op jit(solution)/shard_map/pyramid/pallas_call | solution.py:494
  188.7 70.1 %pyramid_back.1 = (f32[1536,512]{1,0:T(8,128)}, bf16[1536,512]{1,0:T(8,128)(2,1)}, f32[8,512]{1,0:T(8,128)}, bf16[4,16,32,512]{3,2,1,0:T(8,128)(2,1)}, bf16[2,16...) custom-call(bf16[1536,256]{1,0:T(8,128)(2,1)} %get-tuple-element.80.refs_0_, ...), custom_call_target="tpu_custom_call" | custom-call | tf_op jit(solution)/shard_map/pyramid_back/pallas_call | solution.py:494
  258.9 90.4 %bottleneck_back.1 = (f32[1536,512]{1,0:T(8,128)}, f32[8,128]{1,0:T(8,128)}, f32[8,128]{1,0:T(8,128)}, bf16[2,16,32,256]{3,2,1,0:T(8,128)(2,1)}, bf16[2,32,384]{...) custom-call(bf16[1536,512]{1,0:T(8,128)(2,1)} %get-tuple-element.87.refs_0_, ...), custom_call_target="tpu_custom_call" | custom-call | tf_op jit(solution)/shard_map/bottleneck_back/pallas_call | solution.py:494
  349.3 6.6 %finish.1 = (bf16[12,64,128]{2,1,0:T(8,128)(2,1)}, f32[1,1]{1,0:T(1,128)}, f32[1536,512]{1,0:T(8,128)}, f32[256,128]{1,0:T(8,128)}, f32[9,64,128]{2,1,0:T(8,128)...) custom-call(f32[1536,512]{1,0:T(8,128)} %get-tuple-element.99.refs_0, ...), custom_call_target="tpu_custom_call" | custom-call | tf_op jit(solution)/shard_map/finish/pallas_call | solution.py:494

commit v7 on v6

--- a/solution.py
+++ b/solution.py
@@ -1225,7 +1225,8 @@
         beside = net.z + 1 - 2 * lax.rem(net.z, 2)
         self.first = self.copy(half.at[pl.ds(2 * away, 2)], other, beside)
         self.high = net.z // 2
-        self.second = self.copy(pair.at[1 - self.high], last, net.z + 2 - 4 * self.high)
+        if last is not None:
+            self.second = self.copy(pair.at[1 - self.high], last, net.z + 2 - 4 * self.high)
 
     def copy(self, src, dst, z):
         net, i = self.net, self.net.count
@@ -1239,9 +1240,6 @@
             device_id_type=MESH,
         )
 
-    def begin(self):
-        self.first.start()
-
     def go_on(self, half):
         self.first.wait()
 
@@ -1252,7 +1250,6 @@
             return carry
 
         lax.fori_loop(0, half.shape[1], body, 0)
-        self.second.start()
 
     def finish(self, target):
         self.second.wait()
@@ -1331,7 +1328,7 @@
 
         lax.fori_loop(0, 12, spread, 0)
 
-    def weight_gradients(pair_of):
+    def weight_gradients(pair_of, between=None):
         owners = pl.ds(4 * pair_of, 4)
 
         def run(start, stop, shift):
@@ -1344,28 +1341,31 @@
 
         run(0, 1, 0)
         run(1, 4, 3)
-        run(4, 10, 6)
         run(10, 13, net.r * 6 - 9)
         for j in range(3):
             k.grad_pyramid[owners, 7 - net.r * 6 + j] = jnp.zeros((4, 32, 512), BF16)
+        if between is not None:
+            between()
+        run(4, 10, 6)
 
     def beside(pair_of):
         view = (pl.ds(2 * pair_of, 2), slice(None), pl.ds(0, 128))
         return net.send(k.blocks.at[view], k.other.at[pl.ds(2 * pair_of, 2)], net.core)
 
-    def to_core(pair_of):
+    def to_core(pair_of, low, high):
         i = net.count
         net.count += 1
+        taps = pl.ds(low, high - low)
         return pltpu.make_async_remote_copy(
-            src_ref=k.grad_pyramid.at[pl.ds(4 * pair_of, 4)],
-            dst_ref=k.core_pyramid,
+            src_ref=k.grad_pyramid.at[pl.ds(4 * pair_of, 4), taps],
+            dst_ref=k.core_pyramid.at[:, taps],
             send_sem=net.send_sems.at[i],
             recv_sem=net.recv_sems.at[i],
             device_id=net.core,
             device_id_type=MESH,
         )
 
-    def add_core(pair_of):
+    def add_core(pair_of, low, high):
         def body(i, carry):
             for z in range(4):
                 total = k.grad_pyramid[4 * pair_of + z, i].astype(F32)
@@ -1373,7 +1373,7 @@
                 k.half_pyramid[z, i] = total.astype(BF16)
             return carry
 
-        lax.fori_loop(0, 16, body, 0)
+        lax.fori_loop(low, high, body, 0)
 
     first_swap = []
 
@@ -1384,7 +1384,7 @@
         build_edge(near)
         k.stream.need(trunk=1)
         weight_gradients(near)
-        first_swap.append(to_core(near))
+        first_swap.append(to_core(near, 0, 16))
         pl.when(mine_second)(first_swap[0].start)
 
     gather_blocks(net, lambda b, at: k.blocks.at[b, at], 1536, meanwhile=near_pair)
@@ -1398,13 +1398,13 @@
     small_moves = small_moves + along_z(net, k.half_pool, k.z_pool)
     copy.wait()
     build_edge(far)
-    pair_sums = PairSums(net, k.half_pyramid, k.z_other, k.z_pair, k.z_last)
+    pair_sums = PairSums(net, k.half_pyramid, k.z_other, k.z_pair, None)
 
     @pl.when(mine_first)
     def _():
         first_swap[0].wait_recv()
-        add_core(near)
-        pair_sums.begin()
+        add_core(near, 0, 16)
+        pair_sums.first.start()
 
     def trunk_rows(i, carry):
         total = 0.0
@@ -1430,14 +1430,14 @@
     each_rows(1536, 32, back_trunk)
     k.stream.done(shortcut=1)
 
-    second_swap = to_core(far)
+    second_swap = [to_core(far, 0, 10), to_core(far, 10, 16)]
 
     def far_gradients():
-        weight_gradients(far)
+        weight_gradients(far, lambda: pl.when(mine_first)(second_swap[0].start))
 
         @pl.when(mine_first)
         def _():
-            second_swap.start()
+            second_swap[1].start()
             pair_sums.go_on(k.half_pyramid)
 
     bias_grad, gain_grad = gradient_sums(
@@ -1460,21 +1460,15 @@
     @pl.when(mine_second)
     def _():
         first_swap[0].wait_send()
-        second_swap.wait_recv()
-        add_core(far)
+        second_swap[0].wait_recv()
+        add_core(far, 0, 10)
+        second_swap[1].wait_recv()
+        add_core(far, 10, 16)
 
     @pl.when(mine_first)
     def _():
-        second_swap.wait_send()
-        pair_sums.finish(k.sum_pyramid)
-
-
-def pair_scratch():
-    return dict(
-        z_other=pltpu.VMEM((2, 16, 32, 512), BF16),
-        z_pair=pltpu.VMEM((2, 16, 32, 512), BF16),
-        z_last=pltpu.VMEM((16, 32, 512), BF16),
-    )
+        for swap in second_swap:
+            swap.wait_send()
 
 
 def run_pyramid_backward(args):
@@ -1488,14 +1482,14 @@
             grad_expanded=((1536, 512), BF16),
             norm_3=((8, 512), F32),
             half_pyramid=((4, 16, 32, 512), BF16),
-            sum_pyramid=((2, 16, 32, 256), BF16),
+            z_pair=((2, 16, 32, 512), BF16),
             sum_project=((32, 384), BF16),
             sum_pool=((64, 256), F32),
         ),
         dict(
             half_project=pltpu.VMEM((4, 32, 384), BF16),
             half_pool=pltpu.VMEM((4, 64, 256), BF16),
-            **pair_scratch(),
+            z_other=pltpu.VMEM((2, 16, 32, 512), BF16),
             z_project=pltpu.VMEM((3, 32, 384), BF16),
             z_pool=pltpu.VMEM((3, 64, 256), BF16),
             grad_pyramid=pltpu.VMEM((8, 16, 32, 512), BF16),
@@ -1637,14 +1631,9 @@
             pl.when(jnp.logical_not(local))(arrival.wait_recv)
 
 
-    @pl.when(is_late)
-    def _():
-        pair_sums.begin()
-
-    @pl.when(early)
-    def _():
-        k.pyramid_sum[...] = k.sum_pyramid[...]
-
+    k.stream.need(z_pair=1)
+    pl.when(is_late)(pair_sums.first.start)
+    pl.when(early)(pair_sums.second.start)
     wait_project = to_owners(lambda i: k.sum_project, k.own_project, k.local_sems.at[10])
 
     def rows_of(i, size=384):
@@ -1701,12 +1690,16 @@
 
     def pass_expand():
         k.stream.need(half_pyramid=1)
-        begin_early()
-
         @pl.when(is_late)
         def _():
             pair_sums.go_on(k.half_pyramid)
-
+            pair_sums.second.start()
+
+        @pl.when(early)
+        def _():
+            pair_sums.finish(k.pyramid_sum)
+
+        begin_early()
         swaps.pop().wait()
         add_halves(net, k.grad_expand, k.core_expand, k.half_expand)
         late_moves.extend(along_z(net, k.half_expand, k.z_expand))
@@ -1799,17 +1792,29 @@
         k.norm_1,
         meanwhile=pass_halves,
     )
-    gather_blocks(net, lambda b, at: k.grad_reduced.at[at, lane_block(b)], 1536)
-
-    relay_late()
-    k.stream.need(x=1)
-
-    def reduce_gradient(b, carry):
-        grad = tm_m(k.grad_reduced[:, lane_block(b)], k.x[...])
-        k.grad_reduce[pl.ds(2 * b, 2)] = grad.reshape(2, 64, 512).astype(BF16)
-        return carry
-
-    lax.fori_loop(0, 4, reduce_gradient, 0)
+
+    def reduce_gradients(pair_of):
+        def body(i, carry):
+            b = 2 * pair_of + i
+            grad = tm_m(k.grad_reduced[:, lane_block(b)], k.x[...])
+            k.grad_reduce[pl.ds(2 * b, 2)] = grad.reshape(2, 64, 512).astype(BF16)
+            return carry
+
+        lax.fori_loop(0, 2, body, 0)
+
+    def near_gradients():
+        relay_late()
+        k.stream.need(x=1)
+        reduce_gradients(net.m // 2)
+
+    gather_blocks(
+        net,
+        lambda b, at: k.grad_reduced.at[at, lane_block(b)],
+        1536,
+        meanwhile=near_gradients,
+    )
+
+    reduce_gradients(1 - net.m // 2)
     swap = core_halves(net, k.grad_reduce, k.core_reduce)
 
     swap.wait()
@@ -1860,7 +1865,8 @@
         dict(
             grad_taps=pltpu.VMEM((2560, 384), BF16),
             grad_reduced=pltpu.VMEM((1536, 512), BF16),
-            **pair_scratch(),
+            z_other=pltpu.VMEM((2, 16, 32, 512), BF16),
+            z_last=pltpu.VMEM((16, 32, 512), BF16),
             relay=pltpu.VMEM((2, 2, 16, 32, 256), BF16),
             pyramid_sum=pltpu.VMEM((2, 16, 32, 256), BF16),
             sum_reduce=pltpu.VMEM((64, 512), BF16),
@@ -1890,7 +1896,7 @@
         ),
         96,
         hbm=dict(w_dilated=1),
-        stream=dict(half_pyramid=1, hidden_two=1, dilated=1, mask=1, hidden=1, reduced=1, x=1, shortcut=1, w_reduce=1, grad_input=1),
+        stream=dict(z_pair=1, half_pyramid=1, hidden_two=1, dilated=1, mask=1, hidden=1, reduced=1, x=1, shortcut=1, w_reduce=1, grad_input=1),
     )
 
 
@@ -2076,7 +2082,7 @@
             shortcut=back.shortcut,
             w_reduce=forward.w_reduce,
             half_pyramid=back.half_pyramid,
-            sum_pyramid=back.sum_pyramid,
+            z_pair=back.z_pair,
             sum_project=back.sum_project,
             x=x,
             hidden=forward.hidden,

time: 356 us -> 339 us (0.952)
  Pallas kernels: 355 us -> 338 us
    pallas_call x5, Pallas kernels: 355 us -> 338 us  [call_kernel(): pl.pallas_call(kernel, out_shape=[jax.ShapeDtypeStruct(s, d) for s, d in...]
where the time goes in v7:
time: 339 us
  Pallas kernels  338 us (100%)
    pallas_call x5, Pallas kernels, call_kernel(): pl.pallas_call(kernel, out_shape=[jax.ShapeDtypeStruct(s, d) for s, d in...  338 us

profile of v7, /device:TPU:0, one launch (start us, length us, event | category | flops | bytes accessed | tf_op | source)
XLA Modules:
  0.0 338.9 jit_solution(18312747050208960220)
XLA Ops:
  0.7 90.5 %bottleneck.1 = (f32[1536,128]{1,0:T(8,128)}, bf16[4,512,128]{2,1,0:T(8,128)(2,1)}, bf16[13,4,64,512]{3,2,1,0:T(8,128)(2,1)}, bf16[4,5,64,256]{3,2,1,0:T(8,128)(...) custom-call(bf16[1536,512]{1,0:T(8,128)(2,1)} %bitcast.20, ...), custom_call_target="tpu_custom_call" | custom-call | tf_op jit(solution)/shard_map/bottleneck/pallas_call | solution.py:494
  91.2 97.5 %pyramid.1 = (bf16[13,4,64,512]{3,2,1,0:T(8,128)(2,1)}, bf16[768,128]{1,0:T(8,128)(2,1)}, f32[8,128]{1,0:T(8,128)}, bf16[8,32,384]{2,1,0:T(8,128)(2,1)}, bf16[8,...) custom-call(bf16[1536,512]{1,0:T(8,128)(2,1)} %get-tuple-element.76., ...), custom_call_target="tpu_custom_call" | custom-call | tf_op jit(solution)/shard_map/pyramid/pallas_call | solution.py:494
  188.7 58.9 %pyramid_back.1 = (f32[1536,512]{1,0:T(8,128)}, bf16[1536,512]{1,0:T(8,128)(2,1)}, f32[8,512]{1,0:T(8,128)}, bf16[4,16,32,512]{3,2,1,0:T(8,128)(2,1)}, bf16[2,16...) custom-call(bf16[1536,256]{1,0:T(8,128)(2,1)} %get-tuple-element.80.refs_0_, ...), custom_call_target="tpu_custom_call" | custom-call | tf_op jit(solution)/shard_map/pyramid_back/pallas_call | solution.py:494
  247.6 84.5 %bottleneck_back.1 = (f32[1536,512]{1,0:T(8,128)}, f32[8,128]{1,0:T(8,128)}, f32[8,128]{1,0:T(8,128)}, bf16[2,16,32,256]{3,2,1,0:T(8,128)(2,1)}, bf16[2,32,384]{...) custom-call(bf16[1536,512]{1,0:T(8,128)(2,1)} %get-tuple-element.87.refs_0_, ...), custom_call_target="tpu_custom_call" | custom-call | tf_op jit(solution)/shard_map/bottleneck_back/pallas_call | solution.py:494
  332.1 6.6 %finish.1 = (bf16[12,64,128]{2,1,0:T(8,128)(2,1)}, f32[1,1]{1,0:T(1,128)}, f32[1536,512]{1,0:T(8,128)}, f32[256,128]{1,0:T(8,128)}, f32[9,64,128]{2,1,0:T(8,128)...) custom-call(f32[1536,512]{1,0:T(8,128)} %get-tuple-element.99.refs_0, ...), custom_call_target="tpu_custom_call" | custom-call | tf_op jit(solution)/shard_map/finish/pallas_call | solution.py:494

commit v8 on v7

--- a/solution.py
+++ b/solution.py
@@ -187,7 +187,7 @@
         body(pl.ds(pl.multiple_of(i * step, step), step))
         return carry
 
-    lax.fori_loop(0, total // step, run, 0)
+    lax.fori_loop(0, total // step, run, 0, unroll=2)
 
 
 def lane_block(index, width=128):
@@ -200,7 +200,7 @@
 
 
 def column_sums(fn, total, width, number):
-    step = 16384 // width
+    step = 32768 // width
 
     def run(i, sums):
         terms = fn(pl.ds(pl.multiple_of(i * step, step), step))
@@ -243,7 +243,16 @@
 
 
 def statistics(
-    net, value_ref, mask_ref, counts, outgoing, incoming, counted, folded=False, extra=None
+    net,
+    value_ref,
+    mask_ref,
+    counts,
+    outgoing,
+    incoming,
+    counted,
+    folded=False,
+    extra=None,
+    meanwhile=None,
 ):
     total, width = value_ref.shape
     same = fold if folded else (lambda row: row)
@@ -260,7 +269,7 @@
 
     second = same(column_sums(squares, total, width, 1)[0])
     pack(outgoing, first, second, extra)
-    exchange(net, outgoing, incoming)
+    exchange(net, outgoing, incoming, meanwhile)
     firsts, seconds = unpack(incoming, width)
     numbers = wide(counts, width)
     mean = jnp.sum(firsts, axis=0, keepdims=True) / counted
@@ -593,7 +602,7 @@
         k.mask[pl.ds(pl.multiple_of(i * 128, 128), 128), :] = inside
         return carry
 
-    lax.fori_loop(0, 12, mask_rows, 0)
+    lax.fori_loop(0, 12, mask_rows, 0, unroll=2)
     k.stream.done(mask=1)
     k.stream.need(x=1)
 
@@ -684,7 +693,7 @@
         k.dilated[at, :] = k.dilated[at, :] + k.left[i, 4:132, :] + k.right[i, 12:140, :]
         return carry
 
-    lax.fori_loop(0, 12, add_columns, 0)
+    lax.fori_loop(0, 12, add_columns, 0, unroll=2)
     k.stream.done(dilated=1)
     mean_2, inverse_2 = statistics(net, k.dilated, k.mask, counts, k.out_2, k.in_2, counted)
     keep_rows(k.stats_2, mean_2, inverse_2)
@@ -711,7 +720,7 @@
         u = u + k.x[at, :].astype(F32)
         k.trunk[at, :] = (u * sigmoid(u)).astype(BF16)
 
-    each_rows(1536, 32, activate_3)
+    each_rows(1536, 64, activate_3)
     for copy in late:
         copy.wait()
 
@@ -807,7 +816,7 @@
         k.cells[i, 40:168, :] = k.trunk[at, :].astype(F32)
         return carry
 
-    lax.fori_loop(0, 12, fill, 0)
+    lax.fori_loop(0, 12, fill, 0, unroll=2)
 
     def shifted(i, offset):
         cells = k.cells[pl.ds(i * 3, 3), 40 + offset : 168 + offset, :]
@@ -907,7 +916,7 @@
         u = gain_b * normed_branch(at) + bias_b
         k.spatial[at, :] = (u * sigmoid(u)).astype(BF16)
 
-    each_rows(1536, 64, activate_branches)
+    each_rows(1536, 128, activate_branches)
 
     pool_row = mm_t(pool_act, k.w_slot[...])[0:1, :]
 
@@ -1011,10 +1020,12 @@
     first_lane = lax.broadcasted_iota(jnp.int32, (32, 128), 1) == 0
     k.out_head[:, 256:384] = jnp.where(first_lane, bias_sums, loss_sums)
     quarter = pl.ds(pl.multiple_of(net.m * 8, 8), 8)
-    head_copies = [
-        net.send(k.out_head.at[quarter], k.in_head.at[net.slot], peer) for peer in net.group
-    ]
-    k.in_head[net.slot] = k.out_head[quarter, :]
+    head_copies = []
+
+    def share_head():
+        for peer in net.group:
+            head_copies.append(net.send(k.out_head.at[quarter], k.in_head.at[net.slot], peer))
+        k.in_head[net.slot] = k.out_head[quarter, :]
 
     own_head = k.head_rows[:, lane_block(net.m // 2)]
     own_head = jnp.where(odd, pltpu.roll(own_head, 64, 1), own_head)
@@ -1031,7 +1042,7 @@
 
     each_rows(768, 128, back_features)
     bias_grad, gain_grad = gradient_sums(
-        net, k.grad_p, normed_projected, k.out_3, k.in_3, folded=True
+        net, k.grad_p, normed_projected, k.out_3, k.in_3, folded=True, meanwhile=share_head
     )
     keep_rows(k.norm_p, gain_grad, bias_grad)
 
@@ -1117,7 +1128,7 @@
         net.send(k.head_sums.at[quarter], k.head_sums.at[quarter], (lax.rem(net.m + a, 4), net.r, net.z))
         for a in range(1, 4)
     ]
-    each_rows(1536, 64, back_branches)
+    each_rows(1536, 128, back_branches)
     for copy in head_copies:
         copy.wait()
 
@@ -1306,27 +1317,27 @@
             k.cells[2, i, 40:168, :] = third
             return carry
 
-        lax.fori_loop(0, 12, fill, 0)
+        lax.fori_loop(0, 12, fill, 0, unroll=2)
 
         def spread(i, carry):
             for cell, rate, base in ((0, 12, 1), (1, 24, 4), (2, 36, 7)):
                 shift_rows(pair_of, i, cell, rate, base)
             return carry
 
-        lax.fori_loop(0, 12, spread, 0)
+        lax.fori_loop(0, 12, spread, 0, unroll=2)
 
     def build_edge(pair_of):
         def fill(i, carry):
             k.cells[3, i, 40:168, :] = both(k.other, pair_of, i, 0)[1]
             return carry
 
-        lax.fori_loop(0, 12, fill, 0)
+        lax.fori_loop(0, 12, fill, 0, unroll=2)
 
         def spread(i, carry):
             shift_rows(pair_of, i, 3, 12, 10)
             return carry
 
-        lax.fori_loop(0, 12, spread, 0)
+        lax.fori_loop(0, 12, spread, 0, unroll=2)
 
     def weight_gradients(pair_of, between=None):
         owners = pl.ds(4 * pair_of, 4)
@@ -1427,7 +1438,7 @@
         grad = k.shortcut[at, :] + wide(k.mask[at, :], 512) * pooled
         k.shortcut[at, :] = grad * slope(u)
 
-    each_rows(1536, 32, back_trunk)
+    each_rows(1536, 64, back_trunk)
     k.stream.done(shortcut=1)
 
     second_swap = [to_core(far, 0, 10), to_core(far, 10, 16)]
@@ -1450,7 +1461,7 @@
         grad = gain * k.shortcut[at, :] - shared * (bias_grad + normed(at) * gain_grad)
         k.grad_expanded[at, :] = (inverse * grad).astype(BF16)
 
-    each_rows(1536, 32, back_expanded)
+    each_rows(1536, 64, back_expanded)
     k.stream.done(grad_expanded=1)
     for move_ in small_moves:
         move_.wait()

time: 339 us -> 334 us (0.985)
  Pallas kernels: 338 us -> 333 us
    pallas_call x5, Pallas kernels: 338 us -> 333 us  [call_kernel(): pl.pallas_call(kernel, out_shape=[jax.ShapeDtypeStruct(s, d) for s, d in...]
where the time goes in v8:
time: 334 us
  Pallas kernels  333 us (100%)
    pallas_call x5, Pallas kernels, call_kernel(): pl.pallas_call(kernel, out_shape=[jax.ShapeDtypeStruct(s, d) for s, d in...  333 us

profile of v8, /device:TPU:0, one launch (start us, length us, event | category | flops | bytes accessed | tf_op | source)
XLA Modules:
  0.0 333.8 jit_solution(17790348246869895182)
XLA Ops:
  0.7 89.6 %bottleneck.1 = (f32[1536,128]{1,0:T(8,128)}, bf16[4,512,128]{2,1,0:T(8,128)(2,1)}, bf16[13,4,64,512]{3,2,1,0:T(8,128)(2,1)}, bf16[4,5,64,256]{3,2,1,0:T(8,128)(...) custom-call(bf16[1536,512]{1,0:T(8,128)(2,1)} %bitcast.20, ...), custom_call_target="tpu_custom_call" | custom-call | tf_op jit(solution)/shard_map/bottleneck/pallas_call | solution.py:503
  90.3 95.3 %pyramid.1 = (bf16[13,4,64,512]{3,2,1,0:T(8,128)(2,1)}, bf16[768,128]{1,0:T(8,128)(2,1)}, f32[8,128]{1,0:T(8,128)}, bf16[8,32,384]{2,1,0:T(8,128)(2,1)}, bf16[8,...) custom-call(bf16[1536,512]{1,0:T(8,128)(2,1)} %get-tuple-element.76., ...), custom_call_target="tpu_custom_call" | custom-call | tf_op jit(solution)/shard_map/pyramid/pallas_call | solution.py:503
  185.6 57.7 %pyramid_back.1 = (f32[1536,512]{1,0:T(8,128)}, bf16[1536,512]{1,0:T(8,128)(2,1)}, f32[8,512]{1,0:T(8,128)}, bf16[4,16,32,512]{3,2,1,0:T(8,128)(2,1)}, bf16[2,16...) custom-call(bf16[1536,256]{1,0:T(8,128)(2,1)} %get-tuple-element.80.refs_0_, ...), custom_call_target="tpu_custom_call" | custom-call | tf_op jit(solution)/shard_map/pyramid_back/pallas_call | solution.py:503
  243.4 83.6 %bottleneck_back.1 = (f32[1536,512]{1,0:T(8,128)}, f32[8,128]{1,0:T(8,128)}, f32[8,128]{1,0:T(8,128)}, bf16[2,16,32,256]{3,2,1,0:T(8,128)(2,1)}, bf16[2,32,384]{...) custom-call(bf16[1536,512]{1,0:T(8,128)(2,1)} %get-tuple-element.87.refs_0_, ...), custom_call_target="tpu_custom_call" | custom-call | tf_op jit(solution)/shard_map/bottleneck_back/pallas_call | solution.py:503
  327.0 6.6 %finish.1 = (bf16[12,64,128]{2,1,0:T(8,128)(2,1)}, f32[1,1]{1,0:T(1,128)}, f32[1536,512]{1,0:T(8,128)}, f32[256,128]{1,0:T(8,128)}, f32[9,64,128]{2,1,0:T(8,128)...) custom-call(f32[1536,512]{1,0:T(8,128)} %get-tuple-element.99.refs_0, ...), custom_call_target="tpu_custom_call" | custom-call | tf_op jit(solution)/shard_map/finish/pallas_call | solution.py:503

commit v9 on v8

--- a/solution.py
+++ b/solution.py
@@ -209,7 +209,8 @@
         )
 
     sums = lax.fori_loop(
-        0, total // step, run, tuple(jnp.zeros((8, width), F32) for _ in range(number))
+        0, total // step, run, tuple(jnp.zeros((8, width), F32) for _ in range(number)),
+        unroll=2,
     )
     return [jnp.sum(s, axis=0, keepdims=True) for s in sums]
 
@@ -1260,7 +1261,7 @@
                 self.pair[h, i] = total.astype(BF16)
             return carry
 
-        lax.fori_loop(0, half.shape[1], body, 0)
+        lax.fori_loop(0, half.shape[1], body, 0, unroll=2)
 
     def finish(self, target):
         self.second.wait()
@@ -1271,7 +1272,7 @@
             target[1, i] = total[:, 256:512].astype(BF16)
             return carry
 
-        lax.fori_loop(0, target.shape[1], body, 0)
+        lax.fori_loop(0, target.shape[1], body, 0, unroll=2)
 
 
 def pyramid_backward(net, k):
@@ -1384,7 +1385,7 @@
                 k.half_pyramid[z, i] = total.astype(BF16)
             return carry
 
-        lax.fori_loop(low, high, body, 0)
+        lax.fori_loop(low, high, body, 0, unroll=2)
 
     first_swap = []
 
@@ -1739,7 +1740,7 @@
             ].astype(BF16)
         return carry
 
-    lax.fori_loop(0, 20, spread, 0)
+    lax.fori_loop(0, 20, spread, 0, unroll=2)
     for load in loads:
         load.wait()
 

time: 334 us -> 333 us (level)
  no operation moved by 1% of the time
where the time goes in v9:
time: 333 us
  Pallas kernels  332 us (100%)
    pallas_call x5, Pallas kernels, call_kernel(): pl.pallas_call(kernel, out_shape=[jax.ShapeDtypeStruct(s, d) for s, d in...  332 us

profile of v9, /device:TPU:0, one launch (start us, length us, event | category | flops | bytes accessed | tf_op | source)
XLA Modules:
  0.0 332.9 jit_solution(1123651332121255825)
XLA Ops:
  0.7 89.6 %bottleneck.1 = (f32[1536,128]{1,0:T(8,128)}, bf16[4,512,128]{2,1,0:T(8,128)(2,1)}, bf16[13,4,64,512]{3,2,1,0:T(8,128)(2,1)}, bf16[4,5,64,256]{3,2,1,0:T(8,128)(...) custom-call(bf16[1536,512]{1,0:T(8,128)(2,1)} %bitcast.20, ...), custom_call_target="tpu_custom_call" | custom-call | tf_op jit(solution)/shard_map/bottleneck/pallas_call | solution.py:504
  90.3 94.8 %pyramid.1 = (bf16[13,4,64,512]{3,2,1,0:T(8,128)(2,1)}, bf16[768,128]{1,0:T(8,128)(2,1)}, f32[8,128]{1,0:T(8,128)}, bf16[8,32,384]{2,1,0:T(8,128)(2,1)}, bf16[8,...) custom-call(bf16[1536,512]{1,0:T(8,128)(2,1)} %get-tuple-element.76., ...), custom_call_target="tpu_custom_call" | custom-call | tf_op jit(solution)/shard_map/pyramid/pallas_call | solution.py:504
  185.1 57.5 %pyramid_back.1 = (f32[1536,512]{1,0:T(8,128)}, bf16[1536,512]{1,0:T(8,128)(2,1)}, f32[8,512]{1,0:T(8,128)}, bf16[4,16,32,512]{3,2,1,0:T(8,128)(2,1)}, bf16[2,16...) custom-call(bf16[1536,256]{1,0:T(8,128)(2,1)} %get-tuple-element.80.refs_0_, ...), custom_call_target="tpu_custom_call" | custom-call | tf_op jit(solution)/shard_map/pyramid_back/pallas_call | solution.py:504
  242.6 83.5 %bottleneck_back.1 = (f32[1536,512]{1,0:T(8,128)}, f32[8,128]{1,0:T(8,128)}, f32[8,128]{1,0:T(8,128)}, bf16[2,16,32,256]{3,2,1,0:T(8,128)(2,1)}, bf16[2,32,384]{...) custom-call(bf16[1536,512]{1,0:T(8,128)(2,1)} %get-tuple-element.87.refs_0_, ...), custom_call_target="tpu_custom_call" | custom-call | tf_op jit(solution)/shard_map/bottleneck_back/pallas_call | solution.py:504
  326.1 6.6 %finish.1 = (bf16[12,64,128]{2,1,0:T(8,128)(2,1)}, f32[1,1]{1,0:T(1,128)}, f32[1536,512]{1,0:T(8,128)}, f32[256,128]{1,0:T(8,128)}, f32[9,64,128]{2,1,0:T(8,128)...) custom-call(f32[1536,512]{1,0:T(8,128)} %get-tuple-element.99.refs_0, ...), custom_call_target="tpu_custom_call" | custom-call | tf_op jit(solution)/shard_map/finish/pallas_call | solution.py:504
